TPU v7x, 32 devices: a whole 2x2x4 slice. The times are simulated.
32 devices in a mesh: lat: 4 (over z), lyr: 4 (over x, core), dp: 2 (over y).
Axes of the slice: x: 2, y: 2, z: 4, core: 2. Of those that a mesh axis runs over, the one named last changes fastest.
Arguments:
- act_codes: bfloat16 [1024, 4, 4096], P('dp', 'lyr'), may hold values from -6 to 6
- act_scales: bfloat16 [1024, 4, 32], P('dp', 'lyr'), may hold values from 0.25 to 2.5
- latents: bfloat16 [1024, 16384], P('dp', 'lat'), may hold values from 0 to 36, as said below
- dec_weight: bfloat16 [16384, 4, 4096], P('lat', 'lyr', 'dp'), may hold values from -0.296875 to 0.296875
- dec_bias: float32 [4, 4096], P('lyr'), may hold values from -3 to 3
Outputs:
- grad_enc: float32 [4096, 4, 16384], P('dp', 'lyr', 'lat')
- grad_dec: float32 [16384, 4, 4096], P('lat', 'lyr', 'dp')
- grad_bias: float32 [16384], P('lat')
Inputs may be any that keep to these rules, and one draw needn't show every extreme that they name: `latents`: nonnegative, with many exact zeros.
All inputs are finite; a program needn't handle non-finite values.
Results may differ from a plain program's by a relative error of at most 0.00065.
The roundings to bfloat16 on the way count: a program that leaves them out, or rounds other values in their place, can miss the bound.
Values may be sent and summed in bfloat16 or wider, within the bound.
No kernel may reach another device: no remote copies, remote signals or barrier semaphores. Data moves between devices by JAX's collectives and lax.ppermute only.
A program may use at most 384 MiB of HBM per device.

v0:
```python
import jax
import jax.numpy as jnp
from jax import lax
from jax.sharding import PartitionSpec as P

penalty = 1.0
epsilon = 1e-06


def dequantize(code_block, scale_block):
    row_count, layer_count, width = code_block.shape
    block_count = scale_block.shape[2]
    scaled = (
        code_block.astype(jnp.float32).reshape(
            row_count, layer_count, block_count, width // block_count
        )
        * scale_block.astype(jnp.float32)[..., None]
    )
    return scaled.reshape(row_count, layer_count, width)


def reconstruct(act_rows, weight, inputs, bias_part):
    partial_value = jnp.einsum("rf,fld->rld", act_rows, weight, preferred_element_type=jnp.float32)
    recon = lax.psum(partial_value, "lat")
    return (recon + bias_part[None] - inputs).astype(jnp.bfloat16)


def shards(act_codes, act_scales, latents, dec_weight, dec_bias):
    local_squares = jnp.sum(jnp.square(dec_weight.astype(jnp.float32)), axis=2)
    inputs = dequantize(act_codes, act_scales)
    squares, act_sum = lax.psum((local_squares, jnp.sum(latents.astype(jnp.float32), axis=0)), "dp")
    weight = lax.all_gather(dec_weight, "dp", axis=2, tiled=True)
    inputs_bf = inputs.astype(jnp.bfloat16)
    row_norms = jnp.sqrt(squares + epsilon)
    norm_total = lax.psum(jnp.sum(row_norms, axis=1), "lyr")
    resid = reconstruct(latents, weight, inputs, dec_bias)
    grad_part = jnp.einsum("rld,fld->rf", resid, weight, preferred_element_type=jnp.float32)
    grad_sum = lax.psum(grad_part, "lyr")
    grad_pre = jnp.where(latents > 0, grad_sum + penalty * norm_total[None, :], 0.0).astype(
        jnp.bfloat16
    )
    scaled_rows = (penalty * act_sum[:, None] / row_norms)[:, :, None] * dec_weight.astype(
        jnp.float32
    )
    grad_bias = lax.psum(jnp.sum(grad_pre.astype(jnp.float32), axis=0), "dp")
    grad_enc = lax.psum_scatter(
        jnp.einsum("rld,rf->dlf", inputs_bf, grad_pre, preferred_element_type=jnp.float32),
        "dp",
        scatter_dimension=0,
        tiled=True,
    )
    dec_term = jnp.einsum("rf,rld->fld", latents, resid, preferred_element_type=jnp.float32)
    grad_dec = lax.psum_scatter(dec_term, "dp", scatter_dimension=2, tiled=True) + scaled_rows
    return (grad_enc, grad_dec, grad_bias)


def solution(mesh):
    in_specs = (
        P("dp", "lyr", None),
        P("dp", "lyr", None),
        P("dp", "lat"),
        P("lat", "lyr", "dp"),
        P("lyr", None),
    )
    out_specs = (P("dp", "lyr", "lat"), P("lat", "lyr", "dp"), P("lat"))
    return jax.shard_map(shards, mesh=mesh, in_specs=in_specs, out_specs=out_specs, check_vma=False)
```

profile of v0, /device:TPU:0, one launch (start us, length us, event | category | flops | bytes accessed | tf_op | source)
XLA Modules:
  0.0 2444.9 jit_solution(5763546541803388114)
XLA Ops:
  7.2 0.0 all-gather.2.cloned.1.call-start
  7.2 0.7 all-gather.2.cloned.1.call-update
  7.9 0.0 all-reduce.4.cloned.1.call-start
  7.9 392.9 %all-gather.2.cloned.1.call-done = bf16[4096,1,4096]{2,0,1:T(8,128)(2,1)} async-done(((bf16[4096,1,2048]{2,0,1:T(8,128)(2,1)}), bf16[4096,1,4096]{2,0,1:T(8,128)(2,1)}) %all-gather.2.cloned.1.call-update) | async-done | bytes 33554448 | tf_op jit(solution)/shard_map/all_gather | solution.py:32
  400.9 23.9 fusion.6
  424.7 0.0 copy-start.1
  424.7 0.0 all-reduce.4.cloned.1.call-update
  424.7 0.0 all-reduce.6.cloned.1.call-start
  424.8 0.7 copy-done.1
  425.5 0.1 copy.12
  425.6 5.5 mul.31
  431.1 0.0 copy-start.2
  431.1 9.4 mul.32
  440.5 275.3 %all-reduce.4.cloned.1.call-done = f32[512,1,4096]{2,0,1:T(8,128)} async-done(((f32[512,1,4096]{2,0,1:T(8,128)}), f32[512,1,4096]{2,0,1:T(8,128)}) %all-reduce.4.cloned.1.call-update) | async-done | bytes 8388624 | tf_op jit(solution)/shard_map/psum | solution.py:24
  715.7 0.0 copy-done.2
  715.7 11.7 fusion.12
  727.4 24.0 fusion.2
  751.4 0.0 all-reduce.6.cloned.1.call-update
  751.4 0.2 reduce-scatter.5.cloned.1.call-start
  751.7 31.4 %convolution_bitcast_fusion = f32[4096,1,4096]{0,2,1:T(8,128)} fusion(bf16[512,4096]{1,0:T(8,128)(2,1)} %fusion.12, bf16[512,4096]{1,0:T(8,128)(2,1)} %param.7), kind=kOutput, calls=%fused_computation.2 | convolution fusion | flops 17179869184 | bytes 75497472 | tf_op jit(solution)/shard_map/rf,rld->fld/dot_general | solution.py:52
  783.0 0.0 reduce-scatter.5.cloned.1.call-update
  783.1 0.0 reduce-scatter.3.cloned.1.call-start
  783.1 21.4 copy.13
  804.5 7.4 fusion
  811.9 8.1 psum.44
  820.1 10.9 psum.45
  830.9 72.7 %all-reduce.6.cloned.1.call-done = f32[512,4096]{1,0:T(8,128)} async-done(((f32[512,4096]{1,0:T(8,128)}), f32[512,4096]{1,0:T(8,128)}) %all-reduce.6.cloned.1.call-update) | async-done | bytes 8388624 | tf_op jit(solution)/shard_map/psum | solution.py:38
  903.6 0.0 copy-start
  903.6 7.2 convert_reduce_fusion
  910.8 0.0 copy-done
  910.8 30.6 %convolution_bitcast_fusion.1 = f32[4096,1,4096]{0,2,1:T(8,128)} fusion(bf16[512,4096]{1,0:T(8,128)(2,1)S(1)} %get-tuple-element.12, f32[512,1,4096]{2,0,1:T(8,128)} %mul.32, bf16[512,1,4096]{2,0,1:T(8,128)(2,1)S(1)} %copy-done), kind=kOutput, calls=%fused_computation.3 | convolution fusion | flops 17186160640 | bytes 83886080 | tf_op jit(solution)/shard_map/rld,rf->dlf/dot_general | solution.py:47
  941.4 0.0 reduce-scatter.3.cloned.1.call-update
  941.5 9.4 all-reduce
  950.8 0.1 fusion.13
  950.9 684.2 %reduce-scatter.5.cloned.1.call-done = f32[4096,1,2048]{0,2,1:T(8,128)} async-done(((f32[4096,1,4096]{0,2,1:T(8,128)}), f32[4096,1,2048]{0,2,1:T(8,128)}) %reduce-scatter.5.cloned.1.call-update) | async-done | bytes 33554448 | tf_op jit(solution)/shard_map/reduce_scatter | solution.py:53
  1635.1 28.6 %fusion.1 = f32[4096,1,2048]{0,2,1:T(8,128)} fusion(f32[4096,1,2048]{0,2,1:T(8,128)} %reduce-scatter.5.cloned.1.call-done, bf16[4096,1,2048]{0,2,1:T(8,128)(2,1)} %copy.13, f32[4096]{0:T(1024)S(1)} %bitcast.38), kind=kLoop, calls=%fused_computation.5 | loop fusion | flops 25165824 | bytes 83902464 | tf_op jit(solution)/shard_map/add | solution.py:53
  1663.7 72.9 %copy.15 = f32[4096,1,2048]{2,1,0:T(1,128)} copy(f32[4096,1,2048]{0,2,1:T(8,128)} %fusion.1) | data formatting | bytes 67108864
  1736.6 629.1 %reduce-scatter.3.cloned.1.call-done = f32[2048,1,4096]{0,2,1:T(8,128)} async-done(((f32[4096,1,4096]{0,2,1:T(8,128)}), f32[2048,1,4096]{0,2,1:T(8,128)}) %reduce-scatter.3.cloned.1.call-update) | async-done | bytes 33554448 | tf_op jit(solution)/shard_map/reduce_scatter | solution.py:46
  2365.7 72.6 %copy.14 = f32[2048,1,4096]{2,1,0:T(1,128)} copy(f32[2048,1,4096]{0,2,1:T(8,128)} %reduce-scatter.3.cloned.1.call-done) | data formatting | bytes 67108864
  (2 shorter events, 0.0 us)
Async XLA Ops:
  7.2 393.7 %all-gather.2.cloned.1.call-start = ((), (), s32[]{:S(2)}) async-start(), calls=%async_computation.2 | async-start | bytes 50331648 | tf_op jit(solution)/shard_map/all_gather | solution.py:32
  7.9 707.8 %all-reduce.4.cloned.1.call-start = ((), (), s32[]{:S(2)}) async-start(), calls=%async_computation.3 | async-start | bytes 16777216 | tf_op jit(solution)/shard_map/psum | solution.py:24
  424.7 0.8 copy-start.1
  424.7 478.9 %all-reduce.6.cloned.1.call-start = ((), (), s32[]{:S(2)}) async-start(), calls=%async_computation.4 | async-start | bytes 16777216 | tf_op jit(solution)/shard_map/psum | solution.py:38
  431.1 284.6 %copy-start.2 = (f32[1,4096]{1,0:T(1,128)S(1)}, f32[1,4096]{1,0:T(1,128)}, u32[]{:S(2)}) copy-start(f32[1,4096]{1,0:T(1,128)} %param.9) | copy-start | bytes 49156
  751.4 883.7 %reduce-scatter.5.cloned.1.call-start = ((), (), s32[]{:S(2)}) async-start(), calls=%async_computation.6 | async-start | bytes 100663296 | tf_op jit(solution)/shard_map/reduce_scatter | solution.py:53
  783.1 1582.6 %reduce-scatter.3.cloned.1.call-start = ((), (), s32[]{:S(2)}) async-start(), calls=%async_computation.5 | async-start | bytes 100663296 | tf_op jit(solution)/shard_map/reduce_scatter | solution.py:46
  903.6 7.2 copy-start
Sparse Core Ops, SparseCore 0:
  9.6 391.2 all-gather.1
  424.9 290.8 all-reduce.3
  751.6 152.0 all-reduce.5
  905.8 729.2 reduce-scatter.4
  1637.2 728.4 reduce-scatter.2
where the time goes:
time: 2450 us; the launch traced here: 2440 us
  waiting for transfers between devices  2050 us (84%)
  local copies, waits for them, and re-layouts  183 us (7%)
  matrix products  110 us (4%)
  other arithmetic  55 us (2%)
  blocking collectives  28.4 us (1%)
    reduce_scatter x1, waiting for transfers between devices, shards(): lax.psum_scatter(dec_term, 'dp', scatter_dimension=2, tiled=True)  684 us
    reduce_scatter x1, waiting for transfers between devices, shards(): lax.psum_scatter(jnp.einsum('rld,rf->dlf', inputs_bf, grad_pre, preferred...  629 us
    all_gather x1, waiting for transfers between devices, shards(): weight = lax.all_gather(dec_weight, 'dp', axis=2, tiled=True)  393 us
    psum x1, waiting for transfers between devices, reconstruct(): recon = lax.psum(partial_value, 'lat')  275 us
    unnamed x9, local copies, waits for them, and re-layouts  168 us
    psum x1, waiting for transfers between devices, shards(): grad_sum = lax.psum(grad_part, 'lyr')  72.7 us
  transfers between devices with their start and end apart: 5, of which 5 were waited for; matrix products, arithmetic and copies ran while one was open for 9% of the time, Pallas kernels for 0%

commit v1 on v0

v1 whole, which is shorter than its diff:
```python
import functools

import jax
import jax.numpy as jnp
from jax import lax
from jax.experimental import pallas as pl
from jax.experimental.pallas import tpu as pltpu
from jax.sharding import PartitionSpec as P

penalty = 1.0
epsilon = 1e-06

CHUNKS = 4
LANES = 128
TILE = 256
VMEM_BYTES = 44 * 1024 * 1024


def swap(value, axis, bit=1):
    size = lax.axis_size(axis)
    return lax.ppermute(value, axis, [(i, i ^ bit) for i in range(size)])


def swap_split(value, first_is_dp):
    n_lyr, n_dp = lax.axis_size("lyr"), lax.axis_size("dp")
    pairs = []
    for l in range(n_lyr):
        for p in range(n_dp):
            along_dp = (l % 2 == 0) == first_is_dp
            target = (l, p ^ 1) if along_dp else (l ^ 2, p)
            pairs.append((l * n_dp + p, target[0] * n_dp + target[1]))
    return lax.ppermute(value, ("lyr", "dp"), pairs)


def line_reduce(parts, me):
    n = parts.shape[0]

    def take(i):
        return lax.dynamic_index_in_dim(parts, jnp.clip(i, 0, n - 1), 0, keepdims=False)

    right = left = None
    for t in range(n - 1):
        to_right, to_left = take(n - 1 - t + me), take(t - (n - 1) + me)
        if t:
            to_right, to_left = to_right + right, to_left + left
        right = lax.ppermute(to_right, "lat", [(i, i + 1) for i in range(t + 1)])
        left = lax.ppermute(to_left, "lat", [(i, i - 1) for i in range(n - 1 - t, n)])
    return take(me) + right + left


def line_gather(block, me, n):
    rights, lefts = [], []
    to_right = to_left = block
    for t in range(n - 1):
        to_right = lax.ppermute(to_right, "lat", [(i, i + 1) for i in range(t, n - 1)])
        to_left = lax.ppermute(to_left, "lat", [(i, i - 1) for i in range(1, n - t)])
        rights.append(to_right)
        lefts.append(to_left)
    out = jnp.zeros((n,) + block.shape, block.dtype)
    out = lax.dynamic_update_index_in_dim(out, block, me, 0)
    for t in range(n - 1):
        got = jnp.where(me > t, rights[t], lefts[n - 2 - t])
        out = lax.dynamic_update_index_in_dim(out, got, lax.rem(me - 1 - t + n, n), 0)
    return out


def reduce_rows(partial, me):
    n = lax.axis_size("lat")
    rows, width = partial.shape
    if n <= 4:
        return line_reduce(partial.reshape(n, rows // n, width), me)
    return lax.psum_scatter(partial, "lat", scatter_dimension=0, tiled=True)


def gather_rows(block, me):
    n = lax.axis_size("lat")
    rows, width = block.shape
    if n <= 4:
        return line_gather(block, me, n).reshape(n * rows, width)
    return lax.all_gather(block, "lat", axis=0, tiled=True)


def store_rows(out_ref, value, first, count):
    rows = value.shape[0]
    for j in range(value.shape[1] // LANES):
        out_ref[pl.ds(first + j, rows, stride=count), :] = value[:, j * LANES : (j + 1) * LANES]


def dec_kernel(lat_ref, resid_ref, factor_ref, weight_ref, out_ref):
    width = resid_ref.shape[1]
    step = min(512, width)
    left = lat_ref[...].T
    for c in range(0, width, step):
        value = jnp.dot(left, resid_ref[:, c : c + step], preferred_element_type=jnp.float32)
        value = value + factor_ref[...] * weight_ref[:, c : c + step].astype(jnp.float32)
        store_rows(out_ref, value, c // LANES, width // LANES)


def enc_kernel(inputs_ref, grad_ref, out_ref):
    width = grad_ref.shape[1]
    step = min(512, width)
    left = inputs_ref[...].T
    for c in range(0, width, step):
        value = jnp.dot(left, grad_ref[:, c : c + step], preferred_element_type=jnp.float32)
        store_rows(out_ref, value, c // LANES, width // LANES)


def decoder_grad(lat, resid, factor, weight):
    rows, feats = lat.shape
    width = resid.shape[1]
    tile = min(TILE, feats)
    out = pl.pallas_call(
        dec_kernel,
        grid=(feats // tile,),
        in_specs=[
            pl.BlockSpec((rows, tile), lambda i: (0, i)),
            pl.BlockSpec((rows, width), lambda i: (0, 0)),
            pl.BlockSpec((tile, 1), lambda i: (i, 0)),
            pl.BlockSpec((tile, width), lambda i: (i, 0)),
        ],
        out_specs=pl.BlockSpec((tile * width // LANES, LANES), lambda i: (i, 0)),
        out_shape=jax.ShapeDtypeStruct((feats * width // LANES, LANES), jnp.float32),
        compiler_params=pltpu.CompilerParams(vmem_limit_bytes=VMEM_BYTES),
        cost_estimate=pl.CostEstimate(
            flops=2 * rows * feats * width,
            bytes_accessed=feats * width * 6 + rows * (feats + width) * 2,
            transcendentals=0,
        ),
    )(lat, resid, factor, weight)
    return out.reshape(feats, 1, width)


def encoder_grad(inputs, grad):
    rows, width = inputs.shape
    feats = grad.shape[1]
    tile = min(TILE, width)
    out = pl.pallas_call(
        enc_kernel,
        grid=(width // tile,),
        in_specs=[
            pl.BlockSpec((rows, tile), lambda i: (0, i)),
            pl.BlockSpec((rows, feats), lambda i: (0, 0)),
        ],
        out_specs=pl.BlockSpec((tile * feats // LANES, LANES), lambda i: (i, 0)),
        out_shape=jax.ShapeDtypeStruct((width * feats // LANES, LANES), jnp.float32),
        compiler_params=pltpu.CompilerParams(vmem_limit_bytes=VMEM_BYTES),
        cost_estimate=pl.CostEstimate(
            flops=2 * rows * feats * width,
            bytes_accessed=feats * width * 4 + rows * (feats + width) * 2,
            transcendentals=0,
        ),
    )(inputs, grad)
    return out.reshape(width, 1, feats)


def after(value, *events):
    return lax.optimization_barrier((value,) + events)[0]


def reduce_plane(partial, core, column):
    rows, feats = partial.shape
    sub = rows // 8
    blocks = partial.reshape(2, 2, 2, sub, feats)
    sent = lax.dynamic_index_in_dim(blocks, 1 - core, 2, keepdims=False)
    kept = lax.dynamic_index_in_dim(blocks, core, 2, keepdims=False)
    total = (kept + swap(sent, "lyr")).reshape(4, sub, feats)

    def pick(dp_other, column_other):
        index = 2 * dp_other + jnp.where(column_other == 1, 1 - column, column)
        return lax.dynamic_index_in_dim(total, index, 0, keepdims=False)

    first_dp, first_column = jnp.where(core == 0, 0, 1), jnp.where(core == 0, 1, 0)
    second_dp, second_column = first_column, first_dp
    got = swap_split(jnp.stack([pick(first_dp, first_column), pick(1, 1)]), False)
    mine = pick(0, 0) + got[0]
    later = pick(second_dp, second_column) + got[1]
    return mine + swap_split(later, True)


def gather_plane(mine, core, column):
    sub, feats = mine.shape
    second = swap_split(mine, True)
    pair = jnp.stack([mine, second])
    got = swap_split(pair, False)
    own_other = jnp.where(core == 0, got[0], second)
    other_own = jnp.where(core == 0, second, got[0])
    four = jnp.stack([jnp.stack([mine, own_other]), jnp.stack([other_own, got[1]])])
    four = jnp.where(column == 0, four, four[:, ::-1])
    twin = swap(four, "lyr")
    both = jnp.where(core == 0, jnp.stack([four, twin], 2), jnp.stack([twin, four], 2))
    return both.reshape(8 * sub, feats)


def shards(act_codes, act_scales, latents, dec_weight, dec_bias):
    me = lax.axis_index("lat")
    layer, half = lax.axis_index("lyr"), lax.axis_index("dp")
    core, column = layer % 2, layer // 2
    n_lat = lax.axis_size("lat")
    weight = dec_weight[:, 0, :]
    codes, scales = act_codes[:, 0, :], act_scales[:, 0, :]
    feats, width = weight.shape
    own_rows = latents.shape[0]
    piece = own_rows // CHUNKS
    block_count = scales.shape[1] // 2
    block_width = width // block_count
    spread = jnp.repeat(jnp.eye(block_count, dtype=jnp.bfloat16), block_width, axis=1)

    squares = jnp.sum(jnp.square(weight.astype(jnp.float32)), axis=1)
    squares = squares + swap(squares, "dp")
    row_norms = jnp.sqrt(squares + epsilon)
    bias = lax.dynamic_slice_in_dim(dec_bias, half * width, width, 1)

    def columns(value, which, count):
        return lax.dynamic_slice_in_dim(value, which * count, count, 1)

    scales_own = columns(scales, half, block_count)
    scales_other = swap(columns(scales, 1 - half, block_count), "dp")

    lat_chunks, inputs_chunks = [], []
    done = None
    for k in range(CHUNKS):
        span = slice(k * piece, (k + 1) * piece)
        own = latents[span]
        sent = lax.dynamic_slice_in_dim(own, core * (piece // 2), piece // 2, 0)
        sent_codes = columns(codes[span], 1 - half, width)
        if done is not None:
            sent, sent_codes = lax.optimization_barrier((sent, sent_codes, done))[:2]
        got = swap(sent, "dp")
        sent_codes = after(sent_codes, got)
        codes_other = swap(sent_codes, "dp")
        done = codes_other
        twin = swap(got, "lyr")
        other = jnp.where(core == 0, jnp.concatenate([got, twin]), jnp.concatenate([twin, got]))
        lat_chunks.append(jnp.concatenate([own, other]))
        code_rows = jnp.concatenate([columns(codes[span], half, width), codes_other])
        scale_rows = jnp.concatenate([scales_own[span], scales_other[span]])
        wide = jnp.dot(scale_rows, spread, preferred_element_type=jnp.float32)
        inputs_chunks.append(code_rows.astype(jnp.float32) * wide)

    resid_chunks, grad_chunks = [], []
    block = 2 * piece // n_lat
    last = None
    for k in range(CHUNKS):
        partial = jnp.dot(lat_chunks[k], weight, preferred_element_type=jnp.float32)
        recon = reduce_rows(partial, me)
        inputs = lax.dynamic_slice_in_dim(inputs_chunks[k], me * block, block, 0)
        resid = (recon + bias - inputs).astype(jnp.bfloat16)
        resid = gather_rows(resid, me)
        resid_chunks.append(resid)
        grad_part = lax.dot_general(
            resid, weight, (((1,), (1,)), ((), ())), preferred_element_type=jnp.float32
        )
        grad_part = grad_part + (0.5 * penalty) * row_norms[None, :]
        mine = reduce_plane(grad_part, core, column)
        sub = piece // 4
        lat_mine = lax.dynamic_slice_in_dim(latents, k * piece + layer * sub, sub, 0)
        grad_pre = jnp.where(lat_mine > 0, mine, 0.0).astype(jnp.bfloat16)
        grad_chunks.append(gather_plane(grad_pre, core, column))
        last = mine

    lat_all = jnp.concatenate(lat_chunks)
    inputs_bf = jnp.concatenate([x.astype(jnp.bfloat16) for x in inputs_chunks])
    act_sum = jnp.sum(lat_all.astype(jnp.float32), axis=0)
    factor = (penalty * act_sum / row_norms)[:, None]
    grad_dec = decoder_grad(lat_all, jnp.concatenate(resid_chunks), factor, weight)
    grad_all = jnp.concatenate(grad_chunks)
    grad_bias = jnp.sum(grad_all.astype(jnp.float32), axis=0)
    grad_enc = encoder_grad(inputs_bf, grad_all)
    return (grad_enc, grad_dec, grad_bias)


def solution(mesh):
    in_specs = (
        P("dp", "lyr", None),
        P("dp", "lyr", None),
        P("dp", "lat"),
        P("lat", "lyr", "dp"),
        P("lyr", None),
    )
    out_specs = (P("dp", "lyr", "lat"), P("lat", "lyr", "dp"), P("lat"))
    return jax.shard_map(shards, mesh=mesh, in_specs=in_specs, out_specs=out_specs, check_vma=False)
```

time: 2450 us -> 617 us (0.25)
  the two profiles are of different devices: /device:TPU:0 before, /device:TPU:25 now
where the time goes in v1:
time: 617 us; the launch traced here: 606 us
  waiting for transfers between devices  172 us (28%)
  starting transfers between devices  162 us (26%)
  matrix products  89.1 us (14%)
  Pallas kernels  75.4 us (12%)
  other arithmetic  68.4 us (11%)
  local copies, waits for them, and re-layouts  36.2 us (6%)
    ppermute x16, waiting for transfers between devices, swap_split(): return lax.ppermute(value, ('lyr', 'dp'), pairs)  72.1 us
    ppermute x12, waiting for transfers between devices, line_gather(): lax.ppermute(to_right, 'lat', [(i, i + 1) for i in range(t, n - 1)])  70.1 us
    ppermute x12, starting transfers between devices, line_reduce(): lax.ppermute(to_left, 'lat', [(i, i - 1) for i in range(n - 1 - t, n)])  58.5 us
    dot_general x4, matrix products, shards(): lax.dot_general(resid, weight, (((1,), (1,)), ((), ())), preferred_elemen...  44.4 us
    pallas_call x1, Pallas kernels, encoder_grad(): pl.pallas_call(enc_kernel, grid=(width // tile,), in_specs=[pl.BlockSpec(...  41.6 us
    ppermute x22, starting transfers between devices, swap(): return lax.ppermute(value, axis, [(i, i ^ bit) for i in range(size)])  41.1 us
    pallas_call x1, Pallas kernels, decoder_grad(): pl.pallas_call(dec_kernel, grid=(feats // tile,), in_specs=[pl.BlockSpec(...  33.7 us
    dot_general x4, matrix products, shards(): partial = jnp.dot(lat_chunks[k], weight, preferred_element_type=jnp.float32)  31.6 us
  transfers between devices with their start and end apart: 86, of which 26 were waited for; matrix products, arithmetic and copies ran while one was open for 28% of the time, Pallas kernels for 6%

profile of v1, /device:TPU:25, one launch (start us, length us, event | category | flops | bytes accessed | tf_op | source)
XLA Modules:
  0.0 606.4 jit_solution(4390886571977647963)
XLA Ops:
  0.7 7.2 %multiply_reduce_fusion = f32[4096]{0:T(1024)S(1)} fusion(bf16[4096,1,2048]{2,0,1:T(8,128)(2,1)} %param.8), kind=kLoop, calls=%fused_computation | loop fusion | flops 25161728 | bytes 16793600 | tf_op jit(solution)/shard_map/reduce_sum | solution.py:208
  9.4 2.4 constant_dynamic-update-slice_fusion.7
  13.9 3.9 fusion.99
  17.8 2.4 dynamic-slice_bitcast_fusion.19
  21.3 3.9 collective-permute-done
  30.7 2.8 constant_dynamic-update-slice_fusion.6
  33.7 8.3 %fusion.6 = f32[4,64,2048]{2,1,0:T(8,128)S(1)} fusion(bf16[4,64,4096]{2,1,0:T(8,128)(2,1)S(1)} %bitcast.405, bf16[4096,1,2048]{2,0,1:T(8,128)(2,1)} %param.8), kind=kOutput, calls=%fused_computation.7 | convolution fusion | flops 4294967296 | bytes 20971520 | tf_op jit(solution)/shard_map/dot_general | solution.py:244
  43.0 2.5 collective-permute-start.13
  47.4 11.2 %collective-permute-done.3 = bf16[64,4096]{1,0:T(8,128)(2,1)S(1)} collective-permute-done((bf16[64,4096]{1,0:T(8,128)(2,1)S(1)}, bf16[64,4096]{1,0:T(8,128)(2,1)S(1)}, u32[]{:S(2)}, u32[]{:S(2)}) %collective-permute-start.3) | collective-permute-done | bytes 524320 | tf_op jit(solution)/shard_map/ppermute | solution.py:21
  60.4 3.3 fusion.104
  65.1 8.9 %collective-permute-start.14 = (f32[64,2048]{1,0:T(8,128)}, f32[64,2048]{1,0:T(8,128)S(1)}, u32[]{:S(2)}, u32[]{:S(2)}) collective-permute-start(f32[64,2048]{1,0:T(8,128)} %get-tuple-element.66), channel_id=1, source_target_pairs={{16,8},{24,16},{17,9},{25,17},{18,10},{26,18},{19,11},{27,19},{20,... | collective-permute-start | bytes 1572872 | tf_op jit(solution)/shard_map/ppermute | solution.py:47
  75.8 7.7 %fusion.4 = f32[4,64,2048]{2,1,0:T(8,128)} fusion(bf16[4,64,4096]{2,1,0:T(8,128)(2,1)} %bitcast.406, bf16[4096,1,2048]{2,0,1:T(8,128)(2,1)S(1)} %bitcast.361), kind=kOutput, calls=%fused_computation.5 | convolution fusion | flops 4294967296 | bytes 20971520 | tf_op jit(solution)/shard_map/dot_general | solution.py:244
  85.5 3.1 collective-permute-start.33
  90.9 3.2 fusion.103
  95.4 4.3 collective-permute-done.5
  99.7 3.6 collective-permute-start.48
  107.9 9.0 %collective-permute-start.34 = (f32[64,2048]{1,0:T(8,128)}, f32[64,2048]{1,0:T(8,128)}, u32[]{:S(2)}, u32[]{:S(2)}) collective-permute-start(f32[64,2048]{1,0:T(8,128)} %get-tuple-element.72), channel_id=1, source_target_pairs={{16,8},{24,16},{17,9},{25,17},{18,10},{26,18},{19,11},{27,19},{20,... | collective-permute-start | bytes 1572872 | tf_op jit(solution)/shard_map/ppermute | solution.py:47
  118.7 7.7 %fusion.2 = f32[4,64,2048]{2,1,0:T(8,128)} fusion(bf16[4,64,4096]{2,1,0:T(8,128)(2,1)} %bitcast.407, bf16[4096,1,2048]{2,0,1:T(8,128)(2,1)S(1)} %bitcast.361), kind=kOutput, calls=%fused_computation.3 | convolution fusion | flops 4294967296 | bytes 20971520 | tf_op jit(solution)/shard_map/dot_general | solution.py:244
  132.9 3.6 collective-permute-start.17
  136.6 3.3 fusion.102
  144.3 2.7 collective-permute-done.16
  147.0 4.7 collective-permute-start.52
  153.8 8.4 %collective-permute-done.20 = bf16[64,2048]{1,0:T(8,128)(2,1)S(1)} collective-permute-done((bf16[64,2048]{1,0:T(8,128)(2,1)S(1)}, bf16[64,2048]{1,0:T(8,128)(2,1)S(1)}, u32[]{:S(2)}, u32[]{:S(2)}) %collective-permute-start.20) | collective-permute-done | bytes 262176 | tf_op jit(solution)/shard_map/ppermute | solution.py:55
  165.8 5.7 collective-permute-done.21
  173.5 7.3 %collective-permute-start.67 = (bf16[64,4096]{1,0:T(8,128)(2,1)S(1)}, bf16[64,4096]{1,0:T(8,128)(2,1)S(1)}, u32[]{:S(2)}, u32[]{:S(2)}) collective-permute-start(bf16[64,4096]{1,0:T(8,128)(2,1)S(1)} %collective-permute-done.7), channel_id=1, source_target_pairs={{0,2},{2,0},{4,6},{6,4},{1,3},{3,1},{5,7},{7,5},{8,10},{10,8},{12,... | collective-permute-start | bytes 1572872 | tf_op jit(solution)/shard_map/ppermute | solution.py:21
  184.2 4.0 collective-permute-start.37
  192.6 7.9 %fusion = f32[4,64,2048]{2,1,0:T(8,128)S(1)} fusion(bf16[4,64,4096]{2,1,0:T(8,128)(2,1)} %bitcast.408, bf16[4096,1,2048]{2,0,1:T(8,128)(2,1)S(1)} %bitcast.361), kind=kOutput, calls=%fused_computation.1 | convolution fusion | flops 4294967296 | bytes 20971520 | tf_op jit(solution)/shard_map/dot_general | solution.py:244
  201.7 14.6 %collective-permute-start.53 = (f32[64,2048]{1,0:T(8,128)}, f32[64,2048]{1,0:T(8,128)}, u32[]{:S(2)}, u32[]{:S(2)}) collective-permute-start(f32[64,2048]{1,0:T(8,128)} %get-tuple-element.78), channel_id=1, source_target_pairs={{16,8},{24,16},{17,9},{25,17},{18,10},{26,18},{19,11},{27,19},{20,... | collective-permute-start | bytes 1572872 | tf_op jit(solution)/shard_map/ppermute | solution.py:47
  216.4 10.6 %convolution_add_fusion.3 = f32[256,4096]{1,0:T(8,128)} fusion(bf16[256,2048]{1,0:T(8,128)(2,1)S(1)} %bitcast.391, f32[4096]{0:T(1024)S(1)} %get-tuple-element.104, bf16[4096,1,2048]{2,0,1:T(8,128)(2,1)} %param.8), kind=kOutput, calls=%fused_computation.15 | convolution fusion | flops 4296015872 | bytes 22036480 | tf_op jit(solution)/shard_map/dot_general | solution.py:250
  227.0 3.2 dynamic-slice_bitcast_fusion.3
  231.2 3.3 fusion.101
  234.5 3.0 collective-permute-start.71
  243.3 7.9 %collective-permute-done.40 = bf16[64,2048]{1,0:T(8,128)(2,1)S(1)} collective-permute-done((bf16[64,2048]{1,0:T(8,128)(2,1)}, bf16[64,2048]{1,0:T(8,128)(2,1)S(1)}, u32[]{:S(2)}, u32[]{:S(2)}) %collective-permute-start.40) | collective-permute-done | bytes 262176 | tf_op jit(solution)/shard_map/ppermute | solution.py:55
  254.4 6.5 %collective-permute-done.41 = bf16[64,2048]{1,0:T(8,128)(2,1)S(1)} collective-permute-done((bf16[64,2048]{1,0:T(8,128)(2,1)S(1)}, bf16[64,2048]{1,0:T(8,128)(2,1)S(1)}, u32[]{:S(2)}, u32[]{:S(2)}) %collective-permute-start.41) | collective-permute-done | bytes 262176 | tf_op jit(solution)/shard_map/ppermute | solution.py:55
  263.6 3.4 collective-permute-start.72
  267.0 4.8 collective-permute-done.54
  274.9 4.1 collective-permute-start.56
  279.0 10.6 %convolution_add_fusion.2 = f32[256,4096]{1,0:T(8,128)} fusion(bf16[256,2048]{1,0:T(8,128)(2,1)S(1)} %bitcast.393, f32[4096]{0:T(1024)S(1)} %get-tuple-element.104, bf16[4096,1,2048]{2,0,1:T(8,128)(2,1)} %param.8), kind=kOutput, calls=%fused_computation.14 | convolution fusion | flops 4296015872 | bytes 22036480 | tf_op jit(solution)/shard_map/dot_general | solution.py:250
  291.6 3.3 dynamic-slice_bitcast_fusion.2
  294.9 4.9 collective-permute-start.42
  304.2 17.6 %collective-permute-done.59 = bf16[64,2048]{1,0:T(8,128)(2,1)S(1)} collective-permute-done((bf16[64,2048]{1,0:T(8,128)(2,1)S(1)}, bf16[64,2048]{1,0:T(8,128)(2,1)S(1)}, u32[]{:S(2)}, u32[]{:S(2)}) %collective-permute-start.59) | collective-permute-done | bytes 262176 | tf_op jit(solution)/shard_map/ppermute | solution.py:55
  321.8 4.6 collective-permute-start.73
  327.8 7.2 %collective-permute-done.60 = bf16[64,2048]{1,0:T(8,128)(2,1)S(1)} collective-permute-done((bf16[64,2048]{1,0:T(8,128)(2,1)S(1)}, bf16[64,2048]{1,0:T(8,128)(2,1)S(1)}, u32[]{:S(2)}, u32[]{:S(2)}) %collective-permute-start.60) | collective-permute-done | bytes 262176 | tf_op jit(solution)/shard_map/ppermute | solution.py:55
  338.8 4.1 collective-permute-start.75
  342.9 12.7 %convolution_add_fusion.1 = f32[256,4096]{1,0:T(8,128)} fusion(bf16[256,2048]{1,0:T(8,128)(2,1)} %bitcast.395, f32[4096]{0:T(1024)S(1)} %get-tuple-element.104, bf16[4096,1,2048]{2,0,1:T(8,128)(2,1)} %param.8), kind=kOutput, calls=%fused_computation.13 | convolution fusion | flops 4296015872 | bytes 22036480 | tf_op jit(solution)/shard_map/dot_general | solution.py:250
  357.6 3.3 dynamic-slice_bitcast_fusion.1
  367.5 6.3 %collective-permute-done.78 = bf16[64,2048]{1,0:T(8,128)(2,1)S(1)} collective-permute-done((bf16[64,2048]{1,0:T(8,128)(2,1)S(1)}, bf16[64,2048]{1,0:T(8,128)(2,1)S(1)}, u32[]{:S(2)}, u32[]{:S(2)}) %collective-permute-start.78) | collective-permute-done | bytes 262176 | tf_op jit(solution)/shard_map/ppermute | solution.py:55
  375.5 7.3 %collective-permute-done.79 = bf16[64,2048]{1,0:T(8,128)(2,1)S(1)} collective-permute-done((bf16[64,2048]{1,0:T(8,128)(2,1)S(1)}, bf16[64,2048]{1,0:T(8,128)(2,1)S(1)}, u32[]{:S(2)}, u32[]{:S(2)}) %collective-permute-start.79) | collective-permute-done | bytes 262176 | tf_op jit(solution)/shard_map/ppermute | solution.py:55
  389.5 10.6 %convolution_add_fusion = f32[256,4096]{1,0:T(8,128)} fusion(bf16[256,2048]{1,0:T(8,128)(2,1)S(1)} %bitcast.389, f32[4096]{0:T(1024)S(1)} %get-tuple-element.104, bf16[4096,1,2048]{2,0,1:T(8,128)(2,1)} %param.8), kind=kOutput, calls=%fused_computation.12 | convolution fusion | flops 4296015872 | bytes 22036480 | tf_op jit(solution)/shard_map/dot_general | solution.py:250
  414.2 11.1 %collective-permute-done.43 = f32[2,32,4096]{2,1,0:T(8,128)S(1)} collective-permute-done((f32[2,32,4096]{2,1,0:T(8,128)S(1)}, f32[2,32,4096]{2,1,0:T(8,128)S(1)}, u32[]{:S(2)}, u32[]{:S(2)}) %collective-permute-start.43) | collective-permute-done | bytes 1048608 | tf_op jit(solution)/shard_map/ppermute | solution.py:32
  425.3 2.3 fusion.22
  427.9 13.7 %collective-permute-done.62 = f32[2,32,4096]{2,1,0:T(8,128)S(1)} collective-permute-done((f32[2,32,4096]{2,1,0:T(8,128)S(1)}, f32[2,32,4096]{2,1,0:T(8,128)S(1)}, u32[]{:S(2)}, u32[]{:S(2)}) %collective-permute-start.62) | collective-permute-done | bytes 1048608 | tf_op jit(solution)/shard_map/ppermute | solution.py:32
  442.8 16.1 %collective-permute-done.81 = f32[2,32,4096]{2,1,0:T(8,128)S(1)} collective-permute-done((f32[2,32,4096]{2,1,0:T(8,128)S(1)}, f32[2,32,4096]{2,1,0:T(8,128)S(1)}, u32[]{:S(2)}, u32[]{:S(2)}) %collective-permute-start.81) | collective-permute-done | bytes 1048608 | tf_op jit(solution)/shard_map/ppermute | solution.py:32
  460.1 2.3 pad_maximum_fusion.1.inputs_ref
  463.2 2.2 pad_maximum_fusion.2.resid_ref
  465.4 3.0 collective-permute-done.82
  468.5 3.2 fusion.31
  472.0 33.7 %shard_map.77 = f32[65536,128]{1,0:T(8,128)} custom-call(bf16[1024,4096]{1,0:T(8,128)(2,1)} %copy-done.3, bf16[1024,2048]{1,0:T(8,128)(2,1)S(1)} %pad_maximum_fusion.2.resid_ref, f32[4096,1]{1,0:T(8,128)S(1)} %copy.18.factor_ref, bf16[4096,2048]{1,0:T(8,128)(2,1)} %bitcast.359), custom_call_target="tpu_custom_call" | custom-call | flops 17179869184 | bytes 62914560 | tf_op jit(solution)/shard_map/pallas_call | solution.py:112
  510.2 9.0 %collective-permute-done.45 = bf16[32,4096]{1,0:T(8,128)(2,1)S(1)} collective-permute-done((bf16[32,4096]{1,0:T(8,128)(2,1)S(1)}, bf16[32,4096]{1,0:T(8,128)(2,1)S(1)}, u32[]{:S(2)}, u32[]{:S(2)}) %collective-permute-start.45) | collective-permute-done | bytes 262176 | tf_op jit(solution)/shard_map/ppermute | solution.py:32
  522.6 8.2 %collective-permute-done.46 = bf16[2,32,4096]{2,1,0:T(8,128)(2,1)S(1)} collective-permute-done((bf16[2,32,4096]{2,1,0:T(8,128)(2,1)S(1)}, bf16[2,32,4096]{2,1,0:T(8,128)(2,1)S(1)}, u32[]{:S(2)}, u32[]{:S(2)}) %collective-permute-start.46) | collective-permute-done | bytes 524320 | tf_op jit(solution)/shard_map/ppermute | solution.py:32
  531.5 10.8 %collective-permute-done.65 = bf16[2,32,4096]{2,1,0:T(8,128)(2,1)S(1)} collective-permute-done((bf16[2,32,4096]{2,1,0:T(8,128)(2,1)S(1)}, bf16[2,32,4096]{2,1,0:T(8,128)(2,1)S(1)}, u32[]{:S(2)}, u32[]{:S(2)}) %collective-permute-start.65) | collective-permute-done | bytes 524320 | tf_op jit(solution)/shard_map/ppermute | solution.py:32
  544.1 7.4 %collective-permute-start.28 = (bf16[2,2,32,4096]{3,2,1,0:T(8,128)(2,1)S(1)}, bf16[2,2,32,4096]{3,2,1,0:T(8,128)(2,1)S(1)}, u32[]{:S(2)}, u32[]{:S(2)}) collective-permute-start(bf16[2,2,32,4096]{3,2,1,0:T(8,128)(2,1)S(1)} %reverse_select_fusion.3), channel_id=1, source_target_pairs={{0,2},{2,0},{4,6},{6,4},{1,3},{3,1},{5,7},{7,5},{8,10},{10,8},{12,... | collective-permute-start | bytes 3145736 | tf_op jit(solution)/shard_map/ppermute | solution.py:21
  558.8 5.4 convert_reduce_fusion
  564.3 41.6 %shard_map.76 = f32[65536,128]{1,0:T(8,128)} custom-call(bf16[1024,2048]{1,0:T(8,128)(2,1)S(1)} %copy-done.2, bf16[1024,4096]{1,0:T(8,128)(2,1)} %get-tuple-element.30.grad_ref), custom_call_target="tpu_custom_call" | custom-call | flops 17179869184 | bytes 46137344 | tf_op jit(solution)/shard_map/pallas_call | solution.py:137
  (357 shorter events, 136.7 us)
Async XLA Ops:
  7.8 193.9 %collective-permute-start.22 = (f32[4096]{0:T(1024)S(1)}, f32[4096]{0:T(1024)S(1)}, u32[]{:S(2)}, u32[]{:S(2)}) collective-permute-start(f32[4096]{0:T(1024)S(1)} %multiply_reduce_fusion), channel_id=1, source_target_pairs={{0,1},{1,0},{2,3},{3,2},{4,5},{5,4},{6,7},{7,6},{8,9},{9,8},{10,11... | collective-permute-start | bytes 49160 | tf_op jit(solution)/shard_map/ppermute | solution.py:21
  9.2 38.3 %collective-permute-start.2 = (bf16[512,16]{0,1:T(8,128)(2,1)S(1)}, bf16[512,16]{0,1:T(8,128)(2,1)S(1)}, u32[]{:S(2)}, u32[]{:S(2)}) collective-permute-start(bf16[512,16]{0,1:T(8,128)(2,1)S(1)} %fusion.68), channel_id=1, source_target_pairs={{0,1},{1,0},{2,3},{3,2},{4,5},{5,4},{6,7},{7,6},{8,9},{9,8},{10,11... | collective-permute-start | bytes 49160 | tf_op jit(solution)/shard_map/ppermute | solution.py:21
  12.7 12.5 %collective-permute-start = (bf16[64,4096]{1,0:T(8,128)(2,1)}, bf16[64,4096]{1,0:T(8,128)(2,1)}, u32[]{:S(2)}, u32[]{:S(2)}) collective-permute-start(bf16[64,4096]{1,0:T(8,128)(2,1)} %constant_dynamic-slice_fusion.17), channel_id=1, source_target_pairs={{0,1},{1,0},{2,3},{3,2},{4,5},{5,4},{6,7},{7,6},{8,9},{9,8},{10,11... | collective-permute-start | bytes 1572872 | tf_op jit(solution)/shard_map/ppermute | solution.py:21
  29.4 16.4 %collective-permute-start.1 = (bf16[128,2048]{1,0:T(8,128)(2,1)}, bf16[128,2048]{1,0:T(8,128)(2,1)S(1)}, u32[]{:S(2)}, u32[]{:S(2)}) collective-permute-start(bf16[128,2048]{1,0:T(8,128)(2,1)} %get-tuple-element.13), channel_id=1, source_target_pairs={{0,1},{1,0},{2,3},{3,2},{4,5},{5,4},{6,7},{7,6},{8,9},{9,8},{10,11... | collective-permute-start | bytes 1572872 | tf_op jit(solution)/shard_map/ppermute | solution.py:21
  43.0 20.9 %collective-permute-start.13 = (f32[64,2048]{1,0:T(8,128)S(1)}, f32[64,2048]{1,0:T(8,128)S(1)}, u32[]{:S(2)}, u32[]{:S(2)}) collective-permute-start(f32[64,2048]{1,0:T(8,128)S(1)} %get-tuple-element.68), channel_id=1, source_target_pairs={{24,16},{25,17},{26,18},{27,19},{28,20},{29,21},{30,22},{31,23}} | collective-permute-start | bytes 1572872 | tf_op jit(solution)/shard_map/ppermute | solution.py:47
  45.9 12.8 %collective-permute-start.3 = (bf16[64,4096]{1,0:T(8,128)(2,1)S(1)}, bf16[64,4096]{1,0:T(8,128)(2,1)S(1)}, u32[]{:S(2)}, u32[]{:S(2)}) collective-permute-start(bf16[64,4096]{1,0:T(8,128)(2,1)S(1)} %constant_dynamic-slice_fusion.14), channel_id=1, source_target_pairs={{0,1},{1,0},{2,3},{3,2},{4,5},{5,4},{6,7},{7,6},{8,9},{9,8},{10,11... | collective-permute-start | bytes 1572872 | tf_op jit(solution)/shard_map/ppermute | solution.py:21
  46.7 17.2 %collective-permute-start.11 = (f32[64,2048]{1,0:T(8,128)S(1)}, f32[64,2048]{1,0:T(8,128)S(1)}, u32[]{:S(2)}, u32[]{:S(2)}) collective-permute-start(f32[64,2048]{1,0:T(8,128)S(1)} %bitcast_add_fusion.21), channel_id=1, source_target_pairs={{0,8},{8,16},{1,9},{9,17},{2,10},{10,18},{3,11},{11,19},{4,12},{12... | collective-permute-start | bytes 1572872 | tf_op jit(solution)/shard_map/ppermute | solution.py:46
  58.7 15.3 %collective-permute-start.29 = (bf16[64,4096]{1,0:T(8,128)(2,1)S(1)}, bf16[64,4096]{1,0:T(8,128)(2,1)S(1)}, u32[]{:S(2)}, u32[]{:S(2)}) collective-permute-start(bf16[64,4096]{1,0:T(8,128)(2,1)S(1)} %collective-permute-done.3), channel_id=1, source_target_pairs={{0,2},{2,0},{4,6},{6,4},{1,3},{3,1},{5,7},{7,5},{8,10},{10,8},{12,... | collective-permute-start | bytes 1572872 | tf_op jit(solution)/shard_map/ppermute | solution.py:21
  63.7 25.1 %collective-permute-start.4 = (bf16[128,2048]{1,0:T(8,128)(2,1)}, bf16[128,2048]{1,0:T(8,128)(2,1)}, u32[]{:S(2)}, u32[]{:S(2)}) collective-permute-start(bf16[128,2048]{1,0:T(8,128)(2,1)} %get-tuple-element.16), channel_id=1, source_target_pairs={{0,1},{1,0},{2,3},{3,2},{4,5},{5,4},{6,7},{7,6},{8,9},{9,8},{10,11... | collective-permute-start | bytes 1572872 | tf_op jit(solution)/shard_map/ppermute | solution.py:21
  65.1 29.1 %collective-permute-start.14 = (f32[64,2048]{1,0:T(8,128)}, f32[64,2048]{1,0:T(8,128)S(1)}, u32[]{:S(2)}, u32[]{:S(2)}) collective-permute-start(f32[64,2048]{1,0:T(8,128)} %get-tuple-element.66), channel_id=1, source_target_pairs={{16,8},{24,16},{17,9},{25,17},{18,10},{26,18},{19,11},{27,19},{20,... | collective-permute-start | bytes 1572872 | tf_op jit(solution)/shard_map/ppermute | solution.py:47
  85.5 19.8 %collective-permute-start.33 = (f32[64,2048]{1,0:T(8,128)S(1)}, f32[64,2048]{1,0:T(8,128)S(1)}, u32[]{:S(2)}, u32[]{:S(2)}) collective-permute-start(f32[64,2048]{1,0:T(8,128)S(1)} %get-tuple-element.74), channel_id=1, source_target_pairs={{24,16},{25,17},{26,18},{27,19},{28,20},{29,21},{30,22},{31,23}} | collective-permute-start | bytes 1572872 | tf_op jit(solution)/shard_map/ppermute | solution.py:47
  88.9 10.8 %collective-permute-start.5 = (bf16[64,4096]{1,0:T(8,128)(2,1)S(1)}, bf16[64,4096]{1,0:T(8,128)(2,1)S(1)}, u32[]{:S(2)}, u32[]{:S(2)}) collective-permute-start(bf16[64,4096]{1,0:T(8,128)(2,1)S(1)} %constant_dynamic-slice_fusion.13), channel_id=1, source_target_pairs={{0,1},{1,0},{2,3},{3,2},{4,5},{5,4},{6,7},{7,6},{8,9},{9,8},{10,11... | collective-permute-start | bytes 1572872 | tf_op jit(solution)/shard_map/ppermute | solution.py:21
  90.2 16.3 %collective-permute-start.31 = (f32[64,2048]{1,0:T(8,128)S(1)}, f32[64,2048]{1,0:T(8,128)S(1)}, u32[]{:S(2)}, u32[]{:S(2)}) collective-permute-start(f32[64,2048]{1,0:T(8,128)S(1)} %bitcast_add_fusion.16), channel_id=1, source_target_pairs={{0,8},{8,16},{1,9},{9,17},{2,10},{10,18},{3,11},{11,19},{4,12},{12... | collective-permute-start | bytes 1572872 | tf_op jit(solution)/shard_map/ppermute | solution.py:46
  94.1 34.9 %collective-permute-start.12 = (f32[64,2048]{1,0:T(8,128)}, f32[64,2048]{1,0:T(8,128)}, u32[]{:S(2)}, u32[]{:S(2)}) collective-permute-start(f32[64,2048]{1,0:T(8,128)} %get-tuple-element.65), channel_id=1, source_target_pairs={{0,8},{8,16},{16,24},{1,9},{9,17},{17,25},{2,10},{10,18},{18,26},{... | collective-permute-start | bytes 1572872 | tf_op jit(solution)/shard_map/ppermute | solution.py:46
  105.2 25.2 %collective-permute-start.15 = (f32[64,2048]{1,0:T(8,128)}, f32[64,2048]{1,0:T(8,128)S(1)}, u32[]{:S(2)}, u32[]{:S(2)}) collective-permute-start(f32[64,2048]{1,0:T(8,128)} %bitcast_add_fusion.20), channel_id=1, source_target_pairs={{8,0},{16,8},{24,16},{9,1},{17,9},{25,17},{10,2},{18,10},{26,18},{... | collective-permute-start | bytes 1572872 | tf_op jit(solution)/shard_map/ppermute | solution.py:47
  106.5 21.7 %collective-permute-start.6 = (bf16[128,2048]{1,0:T(8,128)(2,1)}, bf16[128,2048]{1,0:T(8,128)(2,1)}, u32[]{:S(2)}, u32[]{:S(2)}) collective-permute-start(bf16[128,2048]{1,0:T(8,128)(2,1)} %get-tuple-element.19), channel_id=1, source_target_pairs={{0,1},{1,0},{2,3},{3,2},{4,5},{5,4},{6,7},{7,6},{8,9},{9,8},{10,11... | collective-permute-start | bytes 1572872 | tf_op jit(solution)/shard_map/ppermute | solution.py:21
  107.9 34.6 %collective-permute-start.34 = (f32[64,2048]{1,0:T(8,128)}, f32[64,2048]{1,0:T(8,128)}, u32[]{:S(2)}, u32[]{:S(2)}) collective-permute-start(f32[64,2048]{1,0:T(8,128)} %get-tuple-element.72), channel_id=1, source_target_pairs={{16,8},{24,16},{17,9},{25,17},{18,10},{26,18},{19,11},{27,19},{20,... | collective-permute-start | bytes 1572872 | tf_op jit(solution)/shard_map/ppermute | solution.py:47
  128.2 23.5 %collective-permute-start.49 = (f32[64,2048]{1,0:T(8,128)S(1)}, f32[64,2048]{1,0:T(8,128)S(1)}, u32[]{:S(2)}, u32[]{:S(2)}) collective-permute-start(f32[64,2048]{1,0:T(8,128)S(1)} %get-tuple-element.79), channel_id=1, source_target_pairs={{0,8},{1,9},{2,10},{3,11},{4,12},{5,13},{6,14},{7,15}} | collective-permute-start | bytes 1572872 | tf_op jit(solution)/shard_map/ppermute | solution.py:46
  129.1 10.9 %collective-permute-start.7 = (bf16[64,4096]{1,0:T(8,128)(2,1)S(1)}, bf16[64,4096]{1,0:T(8,128)(2,1)S(1)}, u32[]{:S(2)}, u32[]{:S(2)}) collective-permute-start(bf16[64,4096]{1,0:T(8,128)(2,1)S(1)} %constant_dynamic-slice_fusion.12), channel_id=1, source_target_pairs={{0,1},{1,0},{2,3},{3,2},{4,5},{5,4},{6,7},{7,6},{8,9},{9,8},{10,11... | collective-permute-start | bytes 1572872 | tf_op jit(solution)/shard_map/ppermute | solution.py:21
  141.2 31.1 %collective-permute-start.32 = (f32[64,2048]{1,0:T(8,128)S(1)}, f32[64,2048]{1,0:T(8,128)S(1)}, u32[]{:S(2)}, u32[]{:S(2)}) collective-permute-start(f32[64,2048]{1,0:T(8,128)S(1)} %copy-done.41), channel_id=1, source_target_pairs={{0,8},{8,16},{16,24},{1,9},{9,17},{17,25},{2,10},{10,18},{18,26},{... | collective-permute-start | bytes 1572872 | tf_op jit(solution)/shard_map/ppermute | solution.py:46
  142.5 10.5 %collective-permute-start.18 = (bf16[64,2048]{1,0:T(8,128)(2,1)S(1)}, bf16[64,2048]{1,0:T(8,128)(2,1)S(1)}, u32[]{:S(2)}, u32[]{:S(2)}) collective-permute-start(bf16[64,2048]{1,0:T(8,128)(2,1)S(1)} %collective-permute-done.17), channel_id=1, source_target_pairs={{8,0},{16,8},{9,1},{17,9},{10,2},{18,10},{11,3},{19,11},{12,4},{20... | collective-permute-start | bytes 786440 | tf_op jit(solution)/shard_map/ppermute | solution.py:56
  147.0 35.8 %collective-permute-start.52 = (f32[64,2048]{1,0:T(8,128)S(1)}, f32[64,2048]{1,0:T(8,128)S(1)}, u32[]{:S(2)}, u32[]{:S(2)}) collective-permute-start(f32[64,2048]{1,0:T(8,128)S(1)} %get-tuple-element.80), channel_id=1, source_target_pairs={{24,16},{25,17},{26,18},{27,19},{28,20},{29,21},{30,22},{31,23}} | collective-permute-start | bytes 1572872 | tf_op jit(solution)/shard_map/ppermute | solution.py:47
  151.7 10.4 %collective-permute-start.20 = (bf16[64,2048]{1,0:T(8,128)(2,1)S(1)}, bf16[64,2048]{1,0:T(8,128)(2,1)S(1)}, u32[]{:S(2)}, u32[]{:S(2)}) collective-permute-start(bf16[64,2048]{1,0:T(8,128)(2,1)S(1)} %collective-permute-done.16), channel_id=1, source_target_pairs={{8,16},{16,24},{9,17},{17,25},{10,18},{18,26},{11,19},{19,27},{12,... | collective-permute-start | bytes 786440 | tf_op jit(solution)/shard_map/ppermute | solution.py:55
  153.0 11.4 %collective-permute-start.19 = (bf16[64,2048]{1,0:T(8,128)(2,1)S(1)}, bf16[64,2048]{1,0:T(8,128)(2,1)S(1)}, u32[]{:S(2)}, u32[]{:S(2)}) collective-permute-start(bf16[64,2048]{1,0:T(8,128)(2,1)S(1)} %collective-permute-done.18), channel_id=1, source_target_pairs={{8,0},{9,1},{10,2},{11,3},{12,4},{13,5},{14,6},{15,7}} | collective-permute-start | bytes 786440 | tf_op jit(solution)/shard_map/ppermute | solution.py:56
  162.1 11.4 %collective-permute-start.35 = (f32[64,2048]{1,0:T(8,128)S(1)}, f32[64,2048]{1,0:T(8,128)S(1)}, u32[]{:S(2)}, u32[]{:S(2)}) collective-permute-start(f32[64,2048]{1,0:T(8,128)S(1)} %bitcast_add_fusion.15), channel_id=1, source_target_pairs={{8,0},{16,8},{24,16},{9,1},{17,9},{25,17},{10,2},{18,10},{26,18},{... | collective-permute-start | bytes 1572872 | tf_op jit(solution)/shard_map/ppermute | solution.py:47
  171.5 12.7 %collective-permute-start.50 = (f32[64,2048]{1,0:T(8,128)S(1)}, f32[64,2048]{1,0:T(8,128)S(1)}, u32[]{:S(2)}, u32[]{:S(2)}) collective-permute-start(f32[64,2048]{1,0:T(8,128)S(1)} %bitcast_add_fusion.11), channel_id=1, source_target_pairs={{0,8},{8,16},{1,9},{9,17},{2,10},{10,18},{3,11},{11,19},{4,12},{12... | collective-permute-start | bytes 1572872 | tf_op jit(solution)/shard_map/ppermute | solution.py:46
  172.3 58.0 %collective-permute-start.8 = (bf16[128,2048]{1,0:T(8,128)(2,1)}, bf16[128,2048]{1,0:T(8,128)(2,1)}, u32[]{:S(2)}, u32[]{:S(2)}) collective-permute-start(bf16[128,2048]{1,0:T(8,128)(2,1)} %get-tuple-element.22), channel_id=1, source_target_pairs={{0,1},{1,0},{2,3},{3,2},{4,5},{5,4},{6,7},{7,6},{8,9},{9,8},{10,11... | collective-permute-start | bytes 1572872 | tf_op jit(solution)/shard_map/ppermute | solution.py:21
  173.5 15.8 %collective-permute-start.67 = (bf16[64,4096]{1,0:T(8,128)(2,1)S(1)}, bf16[64,4096]{1,0:T(8,128)(2,1)S(1)}, u32[]{:S(2)}, u32[]{:S(2)}) collective-permute-start(bf16[64,4096]{1,0:T(8,128)(2,1)S(1)} %collective-permute-done.7), channel_id=1, source_target_pairs={{0,2},{2,0},{4,6},{6,4},{1,3},{3,1},{5,7},{7,5},{8,10},{10,8},{12,... | collective-permute-start | bytes 1572872 | tf_op jit(solution)/shard_map/ppermute | solution.py:21
  182.9 56.4 %collective-permute-start.36 = (bf16[64,2048]{1,0:T(8,128)(2,1)}, bf16[64,2048]{1,0:T(8,128)(2,1)}, u32[]{:S(2)}, u32[]{:S(2)}) collective-permute-start(bf16[64,2048]{1,0:T(8,128)(2,1)} %get-tuple-element.42), channel_id=1, source_target_pairs={{0,8},{8,16},{16,24},{1,9},{9,17},{17,25},{2,10},{10,18},{18,26},{... | collective-permute-start | bytes 786440 | tf_op jit(solution)/shard_map/ppermute | solution.py:55
  184.2 50.3 %collective-permute-start.37 = (bf16[64,2048]{1,0:T(8,128)(2,1)}, bf16[64,2048]{1,0:T(8,128)(2,1)S(1)}, u32[]{:S(2)}, u32[]{:S(2)}) collective-permute-start(bf16[64,2048]{1,0:T(8,128)(2,1)} %get-tuple-element.42), channel_id=1, source_target_pairs={{8,0},{16,8},{24,16},{9,1},{17,9},{25,17},{10,2},{18,10},{26,18},{... | collective-permute-start | bytes 786440 | tf_op jit(solution)/shard_map/ppermute | solution.py:56
  189.3 77.7 %collective-permute-start.51 = (f32[64,2048]{1,0:T(8,128)}, f32[64,2048]{1,0:T(8,128)}, u32[]{:S(2)}, u32[]{:S(2)}) collective-permute-start(f32[64,2048]{1,0:T(8,128)} %get-tuple-element.77), channel_id=1, source_target_pairs={{0,8},{8,16},{16,24},{1,9},{9,17},{17,25},{2,10},{10,18},{18,26},{... | collective-permute-start | bytes 1572872 | tf_op jit(solution)/shard_map/ppermute | solution.py:46
  201.7 35.7 %collective-permute-start.53 = (f32[64,2048]{1,0:T(8,128)}, f32[64,2048]{1,0:T(8,128)}, u32[]{:S(2)}, u32[]{:S(2)}) collective-permute-start(f32[64,2048]{1,0:T(8,128)} %get-tuple-element.78), channel_id=1, source_target_pairs={{16,8},{24,16},{17,9},{25,17},{18,10},{26,18},{19,11},{27,19},{20,... | collective-permute-start | bytes 1572872 | tf_op jit(solution)/shard_map/ppermute | solution.py:47
  230.3 11.0 %collective-permute-start.68 = (f32[64,2048]{1,0:T(8,128)S(1)}, f32[64,2048]{1,0:T(8,128)S(1)}, u32[]{:S(2)}, u32[]{:S(2)}) collective-permute-start(f32[64,2048]{1,0:T(8,128)S(1)} %get-tuple-element.85), channel_id=1, source_target_pairs={{0,8},{1,9},{2,10},{3,11},{4,12},{5,13},{6,14},{7,15}} | collective-permute-start | bytes 1572872 | tf_op jit(solution)/shard_map/ppermute | solution.py:46
  234.5 27.8 %collective-permute-start.71 = (f32[64,2048]{1,0:T(8,128)S(1)}, f32[64,2048]{1,0:T(8,128)S(1)}, u32[]{:S(2)}, u32[]{:S(2)}) collective-permute-start(f32[64,2048]{1,0:T(8,128)S(1)} %get-tuple-element.86), channel_id=1, source_target_pairs={{24,16},{25,17},{26,18},{27,19},{28,20},{29,21},{30,22},{31,23}} | collective-permute-start | bytes 1572872 | tf_op jit(solution)/shard_map/ppermute | solution.py:47
  239.3 126.2 %collective-permute-start.23 = (f32[2,2,32,4096]{3,2,1,0:T(8,128)}, f32[2,2,32,4096]{3,2,1,0:T(8,128)}, u32[]{:S(2)}, u32[]{:S(2)}) collective-permute-start(f32[2,2,32,4096]{3,2,1,0:T(8,128)} %dynamic-slice_bitcast_fusion.3), channel_id=1, source_target_pairs={{0,2},{2,0},{4,6},{6,4},{1,3},{3,1},{5,7},{7,5},{8,10},{10,8},{12,... | collective-permute-start | bytes 6291464 | tf_op jit(solution)/shard_map/ppermute | solution.py:21
  251.3 11.0 %collective-permute-start.69 = (f32[64,2048]{1,0:T(8,128)S(1)}, f32[64,2048]{1,0:T(8,128)S(1)}, u32[]{:S(2)}, u32[]{:S(2)}) collective-permute-start(f32[64,2048]{1,0:T(8,128)S(1)} %bitcast_add_fusion.6), channel_id=1, source_target_pairs={{0,8},{8,16},{1,9},{9,17},{2,10},{10,18},{3,11},{11,19},{4,12},{12... | collective-permute-start | bytes 1572872 | tf_op jit(solution)/shard_map/ppermute | solution.py:46
  260.9 10.9 %collective-permute-start.54 = (f32[64,2048]{1,0:T(8,128)S(1)}, f32[64,2048]{1,0:T(8,128)S(1)}, u32[]{:S(2)}, u32[]{:S(2)}) collective-permute-start(f32[64,2048]{1,0:T(8,128)S(1)} %bitcast_add_fusion.10), channel_id=1, source_target_pairs={{8,0},{16,8},{24,16},{9,1},{17,9},{25,17},{10,2},{18,10},{26,18},{... | collective-permute-start | bytes 1572872 | tf_op jit(solution)/shard_map/ppermute | solution.py:47
  263.6 37.5 %collective-permute-start.72 = (f32[64,2048]{1,0:T(8,128)}, f32[64,2048]{1,0:T(8,128)}, u32[]{:S(2)}, u32[]{:S(2)}) collective-permute-start(f32[64,2048]{1,0:T(8,128)} %get-tuple-element.84), channel_id=1, source_target_pairs={{16,8},{24,16},{17,9},{25,17},{18,10},{26,18},{19,11},{27,19},{20,... | collective-permute-start | bytes 1572872 | tf_op jit(solution)/shard_map/ppermute | solution.py:47
  274.9 16.0 %collective-permute-start.56 = (bf16[64,2048]{1,0:T(8,128)(2,1)}, bf16[64,2048]{1,0:T(8,128)(2,1)S(1)}, u32[]{:S(2)}, u32[]{:S(2)}) collective-permute-start(bf16[64,2048]{1,0:T(8,128)(2,1)} %get-tuple-element.44), channel_id=1, source_target_pairs={{8,0},{16,8},{24,16},{9,1},{17,9},{25,17},{10,2},{18,10},{26,18},{... | collective-permute-start | bytes 786440 | tf_op jit(solution)/shard_map/ppermute | solution.py:56
  290.9 11.5 %collective-permute-start.57 = (bf16[64,2048]{1,0:T(8,128)(2,1)S(1)}, bf16[64,2048]{1,0:T(8,128)(2,1)S(1)}, u32[]{:S(2)}, u32[]{:S(2)}) collective-permute-start(bf16[64,2048]{1,0:T(8,128)(2,1)S(1)} %collective-permute-done.56), channel_id=1, source_target_pairs={{8,0},{16,8},{9,1},{17,9},{10,2},{18,10},{11,3},{19,11},{12,4},{20... | collective-permute-start | bytes 786440 | tf_op jit(solution)/shard_map/ppermute | solution.py:56
  294.9 87.9 %collective-permute-start.42 = (f32[2,2,32,4096]{3,2,1,0:T(8,128)}, f32[2,2,32,4096]{3,2,1,0:T(8,128)}, u32[]{:S(2)}, u32[]{:S(2)}) collective-permute-start(f32[2,2,32,4096]{3,2,1,0:T(8,128)} %dynamic-slice_bitcast_fusion.2), channel_id=1, source_target_pairs={{0,2},{2,0},{4,6},{6,4},{1,3},{3,1},{5,7},{7,5},{8,10},{10,8},{12,... | collective-permute-start | bytes 6291464 | tf_op jit(solution)/shard_map/ppermute | solution.py:21
  299.8 35.3 %collective-permute-start.70 = (f32[64,2048]{1,0:T(8,128)S(1)}, f32[64,2048]{1,0:T(8,128)S(1)}, u32[]{:S(2)}, u32[]{:S(2)}) collective-permute-start(f32[64,2048]{1,0:T(8,128)S(1)} %copy-done.42), channel_id=1, source_target_pairs={{0,8},{8,16},{16,24},{1,9},{9,17},{17,25},{2,10},{10,18},{18,26},{... | collective-permute-start | bytes 1572872 | tf_op jit(solution)/shard_map/ppermute | solution.py:46
  301.1 20.7 %collective-permute-start.59 = (bf16[64,2048]{1,0:T(8,128)(2,1)S(1)}, bf16[64,2048]{1,0:T(8,128)(2,1)S(1)}, u32[]{:S(2)}, u32[]{:S(2)}) collective-permute-start(bf16[64,2048]{1,0:T(8,128)(2,1)S(1)} %collective-permute-done.55), channel_id=1, source_target_pairs={{8,16},{16,24},{9,17},{17,25},{10,18},{18,26},{11,19},{19,27},{12,... | collective-permute-start | bytes 786440 | tf_op jit(solution)/shard_map/ppermute | solution.py:55
  302.4 24.0 %collective-permute-start.58 = (bf16[64,2048]{1,0:T(8,128)(2,1)S(1)}, bf16[64,2048]{1,0:T(8,128)(2,1)S(1)}, u32[]{:S(2)}, u32[]{:S(2)}) collective-permute-start(bf16[64,2048]{1,0:T(8,128)(2,1)S(1)} %collective-permute-done.57), channel_id=1, source_target_pairs={{8,0},{9,1},{10,2},{11,3},{12,4},{13,5},{14,6},{15,7}} | collective-permute-start | bytes 786440 | tf_op jit(solution)/shard_map/ppermute | solution.py:56
  321.8 15.0 %collective-permute-start.73 = (f32[64,2048]{1,0:T(8,128)S(1)}, f32[64,2048]{1,0:T(8,128)S(1)}, u32[]{:S(2)}, u32[]{:S(2)}) collective-permute-start(f32[64,2048]{1,0:T(8,128)S(1)} %bitcast_add_fusion.5), channel_id=1, source_target_pairs={{8,0},{16,8},{24,16},{9,1},{17,9},{25,17},{10,2},{18,10},{26,18},{... | collective-permute-start | bytes 1572872 | tf_op jit(solution)/shard_map/ppermute | solution.py:47
  338.8 18.1 %collective-permute-start.75 = (bf16[64,2048]{1,0:T(8,128)(2,1)}, bf16[64,2048]{1,0:T(8,128)(2,1)S(1)}, u32[]{:S(2)}, u32[]{:S(2)}) collective-permute-start(bf16[64,2048]{1,0:T(8,128)(2,1)} %get-tuple-element.46), channel_id=1, source_target_pairs={{8,0},{16,8},{24,16},{9,1},{17,9},{25,17},{10,2},{18,10},{26,18},{... | collective-permute-start | bytes 786440 | tf_op jit(solution)/shard_map/ppermute | solution.py:56
  360.9 48.5 %collective-permute-start.61 = (f32[2,2,32,4096]{3,2,1,0:T(8,128)}, f32[2,2,32,4096]{3,2,1,0:T(8,128)}, u32[]{:S(2)}, u32[]{:S(2)}) collective-permute-start(f32[2,2,32,4096]{3,2,1,0:T(8,128)} %dynamic-slice_bitcast_fusion.1), channel_id=1, source_target_pairs={{0,2},{2,0},{4,6},{6,4},{1,3},{3,1},{5,7},{7,5},{8,10},{10,8},{12,... | collective-permute-start | bytes 6291464 | tf_op jit(solution)/shard_map/ppermute | solution.py:21
  363.5 10.3 %collective-permute-start.78 = (bf16[64,2048]{1,0:T(8,128)(2,1)S(1)}, bf16[64,2048]{1,0:T(8,128)(2,1)S(1)}, u32[]{:S(2)}, u32[]{:S(2)}) collective-permute-start(bf16[64,2048]{1,0:T(8,128)(2,1)S(1)} %collective-permute-done.74), channel_id=1, source_target_pairs={{8,16},{16,24},{9,17},{17,25},{10,18},{18,26},{11,19},{19,27},{12,... | collective-permute-start | bytes 786440 | tf_op jit(solution)/shard_map/ppermute | solution.py:55
  364.8 10.5 %collective-permute-start.77 = (bf16[64,2048]{1,0:T(8,128)(2,1)S(1)}, bf16[64,2048]{1,0:T(8,128)(2,1)S(1)}, u32[]{:S(2)}, u32[]{:S(2)}) collective-permute-start(bf16[64,2048]{1,0:T(8,128)(2,1)S(1)} %collective-permute-done.76), channel_id=1, source_target_pairs={{8,0},{9,1},{10,2},{11,3},{12,4},{13,5},{14,6},{15,7}} | collective-permute-start | bytes 786440 | tf_op jit(solution)/shard_map/ppermute | solution.py:56
  387.5 19.8 %collective-permute-start.24 = (f32[2,32,4096]{2,1,0:T(8,128)}, f32[2,32,4096]{2,1,0:T(8,128)}, u32[]{:S(2)}, u32[]{:S(2)}) collective-permute-start(f32[2,32,4096]{2,1,0:T(8,128)} %pad_maximum_fusion.7), channel_id=1, source_target_pairs={{0,4},{1,5},{2,3},{3,2},{4,0},{5,1},{6,7},{7,6},{8,12},{9,13},{10,... | collective-permute-start | bytes 3145736 | tf_op jit(solution)/shard_map/ppermute | solution.py:32
  405.1 20.3 %collective-permute-start.43 = (f32[2,32,4096]{2,1,0:T(8,128)S(1)}, f32[2,32,4096]{2,1,0:T(8,128)S(1)}, u32[]{:S(2)}, u32[]{:S(2)}) collective-permute-start(f32[2,32,4096]{2,1,0:T(8,128)S(1)} %pad_maximum_fusion.9), channel_id=1, source_target_pairs={{0,4},{1,5},{2,3},{3,2},{4,0},{5,1},{6,7},{7,6},{8,12},{9,13},{10,... | collective-permute-start | bytes 3145736 | tf_op jit(solution)/shard_map/ppermute | solution.py:32
  409.2 56.3 %collective-permute-start.25 = (f32[32,4096]{1,0:T(8,128)}, f32[32,4096]{1,0:T(8,128)}, u32[]{:S(2)}, u32[]{:S(2)}) collective-permute-start(f32[32,4096]{1,0:T(8,128)} %fusion.27), channel_id=1, source_target_pairs={{0,1},{1,0},{2,6},{3,7},{4,5},{5,4},{6,2},{7,3},{8,9},{9,8},{10,14... | collective-permute-start | bytes 1572872 | tf_op jit(solution)/shard_map/ppermute | solution.py:32
  412.5 29.1 %collective-permute-start.62 = (f32[2,32,4096]{2,1,0:T(8,128)S(1)}, f32[2,32,4096]{2,1,0:T(8,128)S(1)}, u32[]{:S(2)}, u32[]{:S(2)}) collective-permute-start(f32[2,32,4096]{2,1,0:T(8,128)S(1)} %pad_maximum_fusion.11), channel_id=1, source_target_pairs={{0,4},{1,5},{2,3},{3,2},{4,0},{5,1},{6,7},{7,6},{8,12},{9,13},{10,... | collective-permute-start | bytes 3145736 | tf_op jit(solution)/shard_map/ppermute | solution.py:32
  412.7 46.2 %collective-permute-start.81 = (f32[2,32,4096]{2,1,0:T(8,128)S(1)}, f32[2,32,4096]{2,1,0:T(8,128)S(1)}, u32[]{:S(2)}, u32[]{:S(2)}) collective-permute-start(f32[2,32,4096]{2,1,0:T(8,128)S(1)} %pad_maximum_fusion.13), channel_id=1, source_target_pairs={{0,4},{1,5},{2,3},{3,2},{4,0},{5,1},{6,7},{7,6},{8,12},{9,13},{10,... | collective-permute-start | bytes 3145736 | tf_op jit(solution)/shard_map/ppermute | solution.py:32
  427.6 37.8 %collective-permute-start.44 = (f32[32,4096]{1,0:T(8,128)}, f32[32,4096]{1,0:T(8,128)}, u32[]{:S(2)}, u32[]{:S(2)}) collective-permute-start(f32[32,4096]{1,0:T(8,128)} %fusion.22), channel_id=1, source_target_pairs={{0,1},{1,0},{2,6},{3,7},{4,5},{5,4},{6,2},{7,3},{8,9},{9,8},{10,14... | collective-permute-start | bytes 1572872 | tf_op jit(solution)/shard_map/ppermute | solution.py:32
  442.6 22.9 %collective-permute-start.63 = (f32[32,4096]{1,0:T(8,128)}, f32[32,4096]{1,0:T(8,128)}, u32[]{:S(2)}, u32[]{:S(2)}) collective-permute-start(f32[32,4096]{1,0:T(8,128)} %fusion.17), channel_id=1, source_target_pairs={{0,1},{1,0},{2,6},{3,7},{4,5},{5,4},{6,2},{7,3},{8,9},{9,8},{10,14... | collective-permute-start | bytes 1572872 | tf_op jit(solution)/shard_map/ppermute | solution.py:32
  471.7 36.8 %collective-permute-start.26 = (bf16[32,4096]{1,0:T(8,128)(2,1)S(1)}, bf16[32,4096]{1,0:T(8,128)(2,1)S(1)}, u32[]{:S(2)}, u32[]{:S(2)}) collective-permute-start(bf16[32,4096]{1,0:T(8,128)(2,1)S(1)} %get-tuple-element.47), channel_id=1, source_target_pairs={{0,1},{1,0},{2,6},{3,7},{4,5},{5,4},{6,2},{7,3},{8,9},{9,8},{10,14... | collective-permute-start | bytes 786440 | tf_op jit(solution)/shard_map/ppermute | solution.py:32
  505.7 15.2 %collective-permute-start.83 = (bf16[32,4096]{1,0:T(8,128)(2,1)S(1)}, bf16[32,4096]{1,0:T(8,128)(2,1)S(1)}, u32[]{:S(2)}, u32[]{:S(2)}) collective-permute-start(bf16[32,4096]{1,0:T(8,128)(2,1)S(1)} %get-tuple-element.48), channel_id=1, source_target_pairs={{0,1},{1,0},{2,6},{3,7},{4,5},{5,4},{6,2},{7,3},{8,9},{9,8},{10,14... | collective-permute-start | bytes 786440 | tf_op jit(solution)/shard_map/ppermute | solution.py:32
  507.0 14.0 %collective-permute-start.64 = (bf16[32,4096]{1,0:T(8,128)(2,1)S(1)}, bf16[32,4096]{1,0:T(8,128)(2,1)S(1)}, u32[]{:S(2)}, u32[]{:S(2)}) collective-permute-start(bf16[32,4096]{1,0:T(8,128)(2,1)S(1)} %get-tuple-element.49), channel_id=1, source_target_pairs={{0,1},{1,0},{2,6},{3,7},{4,5},{5,4},{6,2},{7,3},{8,9},{9,8},{10,14... | collective-permute-start | bytes 786440 | tf_op jit(solution)/shard_map/ppermute | solution.py:32
  507.3 12.0 %collective-permute-start.45 = (bf16[32,4096]{1,0:T(8,128)(2,1)S(1)}, bf16[32,4096]{1,0:T(8,128)(2,1)S(1)}, u32[]{:S(2)}, u32[]{:S(2)}) collective-permute-start(bf16[32,4096]{1,0:T(8,128)(2,1)S(1)} %get-tuple-element.50), channel_id=1, source_target_pairs={{0,1},{1,0},{2,6},{3,7},{4,5},{5,4},{6,2},{7,3},{8,9},{9,8},{10,14... | collective-permute-start | bytes 786440 | tf_op jit(solution)/shard_map/ppermute | solution.py:32
  508.5 34.5 %collective-permute-start.27 = (bf16[2,32,4096]{2,1,0:T(8,128)(2,1)S(1)}, bf16[2,32,4096]{2,1,0:T(8,128)(2,1)S(1)}, u32[]{:S(2)}, u32[]{:S(2)}) collective-permute-start(bf16[2,32,4096]{2,1,0:T(8,128)(2,1)S(1)} %pad_maximum_fusion.15), channel_id=1, source_target_pairs={{0,4},{1,5},{2,3},{3,2},{4,0},{5,1},{6,7},{7,6},{8,12},{9,13},{10,... | collective-permute-start | bytes 1572872 | tf_op jit(solution)/shard_map/ppermute | solution.py:32
  519.3 11.5 %collective-permute-start.46 = (bf16[2,32,4096]{2,1,0:T(8,128)(2,1)S(1)}, bf16[2,32,4096]{2,1,0:T(8,128)(2,1)S(1)}, u32[]{:S(2)}, u32[]{:S(2)}) collective-permute-start(bf16[2,32,4096]{2,1,0:T(8,128)(2,1)S(1)} %pad_maximum_fusion.17), channel_id=1, source_target_pairs={{0,4},{1,5},{2,3},{3,2},{4,0},{5,1},{6,7},{7,6},{8,12},{9,13},{10,... | collective-permute-start | bytes 1572872 | tf_op jit(solution)/shard_map/ppermute | solution.py:32
  520.9 22.2 %collective-permute-start.84 = (bf16[2,32,4096]{2,1,0:T(8,128)(2,1)S(1)}, bf16[2,32,4096]{2,1,0:T(8,128)(2,1)S(1)}, u32[]{:S(2)}, u32[]{:S(2)}) collective-permute-start(bf16[2,32,4096]{2,1,0:T(8,128)(2,1)S(1)} %pad_maximum_fusion.21), channel_id=1, source_target_pairs={{0,4},{1,5},{2,3},{3,2},{4,0},{5,1},{6,7},{7,6},{8,12},{9,13},{10,... | collective-permute-start | bytes 1572872 | tf_op jit(solution)/shard_map/ppermute | solution.py:32
  521.1 21.3 %collective-permute-start.65 = (bf16[2,32,4096]{2,1,0:T(8,128)(2,1)S(1)}, bf16[2,32,4096]{2,1,0:T(8,128)(2,1)S(1)}, u32[]{:S(2)}, u32[]{:S(2)}) collective-permute-start(bf16[2,32,4096]{2,1,0:T(8,128)(2,1)S(1)} %pad_maximum_fusion.19), channel_id=1, source_target_pairs={{0,4},{1,5},{2,3},{3,2},{4,0},{5,1},{6,7},{7,6},{8,12},{9,13},{10,... | collective-permute-start | bytes 1572872 | tf_op jit(solution)/shard_map/ppermute | solution.py:32
  (74 other events, 1035.8 us)

commit v2 on v0

v2 whole, which is shorter than its diff:
```python
import functools

import jax
import jax.numpy as jnp
from jax import lax
from jax.experimental import pallas as pl
from jax.experimental.pallas import tpu as pltpu
from jax.sharding import PartitionSpec as P

penalty = 1.0
epsilon = 1e-06

CHUNKS = (2, 3, 2, 1)
LANES = 128
TILE = 1024
GROUP = 8
VMEM_BYTES = 44 * 1024 * 1024


def swap(value, axis, bit=1):
    size = lax.axis_size(axis)
    return lax.ppermute(value, axis, [(i, i ^ bit) for i in range(size)])


def swap_split(value, first_is_dp):
    n_lyr, n_dp = lax.axis_size("lyr"), lax.axis_size("dp")
    pairs = []
    for l in range(n_lyr):
        for p in range(n_dp):
            along_dp = (l % 2 == 0) == first_is_dp
            target = (l, p ^ 1) if along_dp else (l ^ 2, p)
            pairs.append((l * n_dp + p, target[0] * n_dp + target[1]))
    return lax.ppermute(value, ("lyr", "dp"), pairs)


def reduce_rows(partial):
    return lax.psum_scatter(partial, "lat", scatter_dimension=0, tiled=True)


def gather_rows(block, me):
    n = lax.axis_size("lat")
    rows, width = block.shape
    if n > 4:
        return lax.all_gather(block, "lat", axis=0, tiled=True)
    out = jnp.zeros((n, rows, width), block.dtype)
    out = lax.dynamic_update_index_in_dim(out, block, me, 0)
    for shift in range(1, n):
        got = lax.ppermute(block, "lat", [(i, (i + shift) % n) for i in range(n)])
        out = lax.dynamic_update_index_in_dim(out, got, lax.rem(me - shift + n, n), 0)
    return out.reshape(n * rows, width)


def store_rows(out_ref, value):
    groups = value.shape[1] // LANES
    value = jnp.stack([value[:, j * LANES : (j + 1) * LANES] for j in range(groups)])
    out_ref[...] = jnp.swapaxes(value, 0, 1)


def product(lefts, rights):
    left = jnp.concatenate([ref[...] for ref in lefts], axis=1)
    right = jnp.concatenate([ref[...] for ref in rights], axis=0)
    return jnp.dot(left, right, preferred_element_type=jnp.float32)


def dec_kernel(count, *refs):
    factor_ref, weight_ref = refs[:2]
    lefts, rights, out_ref = refs[2 : 2 + count], refs[2 + count : 2 + 2 * count], refs[-1]
    value = product(lefts, rights)
    store_rows(out_ref, value + factor_ref[...] * weight_ref[...].astype(jnp.float32))


def enc_kernel(count, *refs):
    rights, (out_ref, bias_ref) = refs[1 : 1 + count], refs[1 + count :]
    store_rows(out_ref, product(refs[:1], rights))

    @pl.when(pl.program_id(1) == 0)
    def _():
        total = jnp.zeros(bias_ref.shape, jnp.float32)
        for ref in rights:
            total = total + jnp.sum(ref[...].astype(jnp.float32), axis=0, keepdims=True)
        bias_ref[...] = total


def params():
    return pltpu.CompilerParams(vmem_limit_bytes=VMEM_BYTES)


def decoder_grad(lefts, pieces, factor, weight, part, parts, earlier):
    feats, width = weight.shape
    rows = sum(piece.shape[0] for piece in pieces)
    share = feats // parts
    tile, step = min(TILE, share), min(GROUP * LANES, width)
    tiles = share // tile
    operands = [factor, weight, *lefts, *pieces]
    in_specs = [
        pl.BlockSpec((tile, 1), lambda i, j: (i + part * tiles, 0)),
        pl.BlockSpec((tile, step), lambda i, j: (i + part * tiles, j)),
    ]
    for left in lefts:
        in_specs.append(pl.BlockSpec((tile, left.shape[1]), lambda i, j: (i + part * tiles, 0)))
    for piece in pieces:
        in_specs.append(pl.BlockSpec((piece.shape[0], step), lambda i, j: (0, j)))
    aliases = {}
    if earlier is not None:
        aliases = {len(operands): 0}
        operands.append(earlier)
        in_specs.append(pl.BlockSpec(memory_space=pl.ANY))
    return pl.pallas_call(
        functools.partial(dec_kernel, len(pieces)),
        grid=(tiles, width // step),
        in_specs=in_specs,
        out_specs=pl.BlockSpec(
            (tile, step // LANES, LANES), lambda i, j: (i + part * tiles, j, 0)
        ),
        out_shape=jax.ShapeDtypeStruct((feats, width // LANES, LANES), jnp.float32),
        input_output_aliases=aliases,
        compiler_params=params(),
        cost_estimate=pl.CostEstimate(
            flops=2 * rows * share * width,
            bytes_accessed=share * width * 6 + rows * (share + width) * 2,
            transcendentals=0,
        ),
    )(*operands)


def encoder_grad(inputs_t, pieces):
    width, rows = inputs_t.shape
    feats = pieces[0].shape[1]
    tile, step = min(TILE, width), min(GROUP * LANES, feats)
    out, bias = pl.pallas_call(
        functools.partial(enc_kernel, len(pieces)),
        grid=(feats // step, width // tile),
        in_specs=[pl.BlockSpec((tile, rows), lambda j, i: (i, 0))]
        + [pl.BlockSpec((piece.shape[0], step), lambda j, i: (0, j)) for piece in pieces],
        out_specs=[
            pl.BlockSpec((tile, step // LANES, LANES), lambda j, i: (i, j, 0)),
            pl.BlockSpec((1, step), lambda j, i: (0, j)),
        ],
        out_shape=[
            jax.ShapeDtypeStruct((width, feats // LANES, LANES), jnp.float32),
            jax.ShapeDtypeStruct((1, feats), jnp.float32),
        ],
        compiler_params=params(),
        cost_estimate=pl.CostEstimate(
            flops=2 * rows * feats * width,
            bytes_accessed=feats * width * 4 + rows * (feats + width) * 2,
            transcendentals=0,
        ),
    )(inputs_t, *pieces)
    return out.reshape(width, 1, feats), bias.reshape(feats)


def after(value, *events):
    return lax.optimization_barrier((value,) + events)[0]


def transposed(value, selected):
    return lax.dot_general(
        value, selected, (((0,), (0,)), ((), ())), preferred_element_type=jnp.float32
    ).astype(jnp.bfloat16)


def reduce_plane(resid, weight, offset, core, column):
    sub, feats = resid.shape[0] // 8, weight.shape[0]
    terms = lax.dot_general(
        resid, weight, (((1,), (1,)), ((), ())), preferred_element_type=jnp.float32
    )
    blocks = (terms + offset[None, :]).reshape(2, 2, 2, sub, feats)
    to_send = lax.dynamic_index_in_dim(blocks, 1 - core, 2, keepdims=False)
    to_keep = lax.dynamic_index_in_dim(blocks, core, 2, keepdims=False)
    total = (to_keep + swap(to_send, "lyr")).reshape(4, sub, feats)

    def pick(dp_other, column_other):
        index = 2 * dp_other + jnp.where(column_other == 1, 1 - column, column)
        return lax.dynamic_index_in_dim(total, index, 0, keepdims=False)

    first_dp, first_column = jnp.where(core == 0, 0, 1), jnp.where(core == 0, 1, 0)
    second_dp, second_column = first_column, first_dp
    got = swap_split(jnp.stack([pick(first_dp, first_column), pick(1, 1)]), False)
    mine = pick(0, 0) + got[0]
    later = pick(second_dp, second_column) + got[1]
    return total, mine + swap_split(later, True)


def gather_plane(mine):
    pair = jnp.stack([mine, swap_split(mine, True)])
    twin_pair = swap(pair, "lyr")
    got = swap_split(pair, False)
    twin_got = swap(got, "lyr")
    rows = jnp.concatenate([pair, got, twin_pair, twin_got])
    return rows.reshape(-1, mine.shape[1]), pair


def plane_rows(core, column):
    order = []
    for c in (core, 1 - core):
        across, beside = 4 + 2 * column + c, 2 * (1 - column) + c
        order += [
            2 * column + c,
            jnp.where(c == 0, across, beside),
            jnp.where(c == 0, beside, across),
            4 + 2 * (1 - column) + c,
        ]
    return jnp.stack(order)


def shards(act_codes, act_scales, latents, dec_weight, dec_bias):
    me = lax.axis_index("lat")
    layer, half = lax.axis_index("lyr"), lax.axis_index("dp")
    core, column = layer % 2, layer // 2
    n_lat = lax.axis_size("lat")
    weight = dec_weight[:, 0, :]
    codes, scales = act_codes[:, 0, :], act_scales[:, 0, :]
    feats, width = weight.shape
    own_rows = latents.shape[0]
    unit = own_rows // sum(CHUNKS)
    starts = [unit * sum(CHUNKS[:k]) for k in range(len(CHUNKS) + 1)]
    block_count = scales.shape[1] // 2
    spread = jnp.repeat(jnp.eye(block_count, dtype=jnp.bfloat16), width // block_count, axis=1)

    def columns(value, which, count):
        return lax.dynamic_slice_in_dim(value, which * count, count, 1)

    groups = [(0, 1), (1, 2), (2, len(CHUNKS))]
    lat_chunks, codes_other = [], []
    partials, recons, resid_own, resid_chunks, grad_chunks, mines = [], [], [], [], [], []

    def local_recon(k):
        lat = lat_chunks[k] if k < 2 else after(lat_chunks[k], resid_own[k - 2])
        partials.append(jnp.dot(lat, weight, preferred_element_type=jnp.float32))
        recons.append(reduce_rows(after(partials[k], *recons[2:k])))

    done = None
    for first, last in groups:
        rows = starts[last] - starts[first]
        source = latents if done is None else after(latents, done)
        sent = lax.dynamic_slice_in_dim(source, starts[first] + core * (rows // 2), rows // 2, 0)
        got = swap(sent, "dp")
        done = got
        if partials:
            got = after(got, partials[-1])
        twin = swap(got, "lyr")
        both = jnp.where(core == 0, jnp.stack([got, twin]), jnp.stack([twin, got]))
        both = both.reshape(rows, feats)
        for k in range(first, last):
            inner = slice(starts[k] - starts[first], starts[k + 1] - starts[first])
            lat_chunks.append(jnp.concatenate([latents[starts[k] : starts[k + 1]], both[inner]]))
        if len(partials) < 2:
            local_recon(first)
        codes_here = after(codes, *partials[first : first + 1], done)
        span = slice(starts[first], starts[last])
        codes_got = swap(columns(codes_here[span], 1 - half, width), "dp")
        for k in range(first, last):
            inner = slice(starts[k] - starts[first], starts[k + 1] - starts[first])
            codes_other.append(codes_got[inner])

    scales_here = after(scales, partials[0])
    weight_here = after(weight, partials[0])
    scales_own = columns(scales_here, half, block_count)
    scales_other = swap(columns(scales_here, 1 - half, block_count), "dp")
    squares = jnp.sum(jnp.square(weight_here.astype(jnp.float32)), axis=1)
    squares = squares + swap(squares, "dp")
    row_norms = jnp.sqrt(squares + epsilon)
    offset = (0.5 * penalty) * row_norms
    bias = lax.dynamic_slice_in_dim(dec_bias, half * width, width, 1)

    inputs_chunks = []
    for k in range(len(CHUNKS)):
        span = slice(starts[k], starts[k + 1])
        code_rows = jnp.concatenate([columns(codes[span], half, width), codes_other[k]])
        scale_rows = jnp.concatenate([scales_own[span], scales_other[span]])
        wide = jnp.dot(scale_rows, spread, preferred_element_type=jnp.float32)
        inputs_chunks.append(code_rows.astype(jnp.float32) * wide)
    count = len(CHUNKS)
    for k in range(count):
        if len(partials) < min(k + 2, count):
            local_recon(k + 1)
        events = partials[k + 1 : k + 2]
        if 2 <= k < count - 1:
            events = events + [mines[k - 2]]
        recon = after(recons[k], *events) if events else recons[k]
        block = 2 * (starts[k + 1] - starts[k]) // n_lat
        inputs = lax.dynamic_slice_in_dim(inputs_chunks[k], me * block, block, 0)
        resid_own.append((recon + bias - inputs).astype(jnp.bfloat16))
        resid = gather_rows(resid_own[k], me)
        resid_chunks.append(resid)
        if k >= 1:
            resid = after(resid, mines[k - 1])
        total, mine = reduce_plane(resid, weight, offset, core, column)
        if k >= 1:
            mine = after(mine, grad_chunks[k - 1])
        mines.append(mine)
        sub = (starts[k + 1] - starts[k]) // 4
        lat_mine = lax.dynamic_slice_in_dim(latents, starts[k] + layer * sub, sub, 0)
        grad_pre = jnp.where(lat_mine > 0, mine, 0.0).astype(jnp.bfloat16)
        grad_rows, pair = gather_plane(grad_pre)
        grad_chunks.append(grad_rows)

    inputs_bf = jnp.concatenate([x.astype(jnp.bfloat16) for x in inputs_chunks])
    order = after(plane_rows(core, column), resid_own[0])
    sources = []
    for k in range(count):
        sub = (starts[k + 1] - starts[k]) // 4
        source = (order * sub)[:, None] + jnp.arange(sub)[None, :]
        sources.append(2 * starts[k] + source.reshape(-1))
    rows = jnp.arange(2 * own_rows)
    selected = (rows[:, None] == jnp.concatenate(sources)[None, :]).astype(jnp.bfloat16)
    inputs_t = transposed(inputs_bf, selected)

    lat_t, act_sum = [], 0.0
    for k in range(count):
        lat = after(lat_chunks[k], resid_own[min(max(k, 1), 2)])
        lat_t.append(transposed(lat, jnp.eye(lat.shape[0], dtype=jnp.bfloat16)))
        act_sum = act_sum + jnp.sum(lat.astype(jnp.float32), axis=0)
    factor = (penalty * act_sum / row_norms)[:, None]

    grad_dec = None
    for part, event in enumerate((total, mine)):
        pieces = [after(lat_t[0], event)] + lat_t[1:]
        grad_dec = decoder_grad(pieces, resid_chunks, factor, weight, part, 2, grad_dec)
    grad_enc, grad_bias = encoder_grad(inputs_t, grad_chunks)
    return (grad_enc, grad_dec.reshape(feats, 1, width), grad_bias)


def solution(mesh):
    in_specs = (
        P("dp", "lyr", None),
        P("dp", "lyr", None),
        P("dp", "lat"),
        P("lat", "lyr", "dp"),
        P("lyr", None),
    )
    out_specs = (P("dp", "lyr", "lat"), P("lat", "lyr", "dp"), P("lat"))
    return jax.shard_map(shards, mesh=mesh, in_specs=in_specs, out_specs=out_specs, check_vma=False)
```

time: 2450 us -> 549 us (0.22)
  the two profiles are of different devices: /device:TPU:0 before, /device:TPU:31 now
where the time goes in v2:
time: 549 us; the launch traced here: 540 us
  waiting for transfers between devices  179 us (33%)
  matrix products  115 us (21%)
  local copies, waits for them, and re-layouts  69.1 us (13%)
  Pallas kernels  61.7 us (11%)
  starting transfers between devices  52 us (9%)
  other arithmetic  47.6 us (9%)
  between operations  15.2 us (3%)
    ppermute x12, waiting for transfers between devices, gather_rows(): got = lax.ppermute(block, 'lat', [(i, (i + shift) % n) for i in range(n)])  78.1 us
    ppermute x16, waiting for transfers between devices, swap_split(): return lax.ppermute(value, ('lyr', 'dp'), pairs)  59 us
    dot_general x4, matrix products, reduce_plane(): lax.dot_general(resid, weight, (((1,), (1,)), ((), ())), preferred_elemen...  47.2 us
    ppermute x23, waiting for transfers between devices, swap(): return lax.ppermute(value, axis, [(i, i ^ bit) for i in range(size)])  42.1 us
    dot_general x4, matrix products, local_recon(): partials.append(jnp.dot(lat, weight, preferred_element_type=jnp.float32))  40.1 us
    ppermute x23, starting transfers between devices, swap(): return lax.ppermute(value, axis, [(i, i ^ bit) for i in range(size)])  35.5 us
    pallas_call x2, Pallas kernels, decoder_grad(): pl.pallas_call(functools.partial(dec_kernel, len(pieces)), grid=(tiles, w...  34.3 us
    pallas_call x1, Pallas kernels, encoder_grad(): pl.pallas_call(functools.partial(enc_kernel, len(pieces)), grid=(feats //...  27.5 us
  transfers between devices with their start and end apart: 55, of which 19 were waited for; matrix products, arithmetic and copies ran while one was open for 38% of the time, Pallas kernels for 6%

profile of v2, /device:TPU:31, one launch (start us, length us, event | category | flops | bytes accessed | tf_op | source)
XLA Modules:
  0.0 540.0 jit_solution(5438064077529961672)
XLA Ops:
  7.2 2.3 fusion.78
  9.8 2.7 fusion.79
  12.5 3.1 fusion.80
  19.6 3.0 collective-permute-done
  26.4 2.1 constant_dynamic-slice_fusion.13
  31.4 9.5 %fusion.73 = f32[256,2048]{1,0:T(8,128)} fusion(bf16[4096,1,2048]{2,0,1:T(8,128)(2,1)} %param.8, bf16[128,4096]{1,0:T(8,128)(2,1)S(1)} %bitcast.229, bf16[128,4096]{1,0:T(8,128)(2,1)S(1)} %get-tuple-element.89), kind=kOutput, calls=%fused_computation.192 | convolution fusion | flops 4299161600 | bytes 20971520 | tf_op jit(solution)/shard_map/dot_general | solution.py:230
  43.9 7.3 %multiply_reduce_fusion = f32[4096]{0:T(1024)S(1)} fusion(bf16[4096,2048]{1,0:T(8,128)(2,1)} %bitcast.198), kind=kLoop, calls=%fused_computation | loop fusion | flops 25161728 | bytes 16793600 | tf_op jit(solution)/shard_map/reduce_sum | solution.py:261
  52.9 7.0 %collective-permute-done.12 = f32[4096]{0:T(1024)S(1)} collective-permute-done((f32[4096]{0:T(1024)S(1)}, f32[4096]{0:T(1024)S(1)}, u32[]{:S(2)}, u32[]{:S(2)}) %collective-permute-start.12) | collective-permute-done | bytes 16416 | tf_op jit(solution)/shard_map/ppermute | solution.py:22
  61.4 2.1 constant_dynamic-slice_fusion.11
  63.9 2.1 fusion.85
  67.6 12.0 %fusion.71 = f32[384,2048]{1,0:T(8,128)} fusion(bf16[4096,1,2048]{2,0,1:T(8,128)(2,1)} %param.8, bf16[192,4096]{1,0:T(8,128)(2,1)S(1)} %bitcast.218, bf16[192,4096]{1,0:T(8,128)(2,1)S(1)} %slice.103), kind=kOutput, calls=%fused_computation.190 | convolution fusion | flops 6448742400 | bytes 23068672 | tf_op jit(solution)/shard_map/dot_general | solution.py:230
  79.6 3.4 collective-permute-done.7
  88.9 1.8 pad_maximum_fusion
  90.8 2.2 maximum_select_fusion.1
  95.1 27.5 %collective-permute-done.8 = bf16[192,2048]{1,0:T(8,128)(2,1)} collective-permute-done((bf16[192,2048]{1,0:T(8,128)(2,1)}, bf16[192,2048]{1,0:T(8,128)(2,1)}, u32[]{:S(2)}, u32[]{:S(2)}) %collective-permute-start.8) | collective-permute-done | bytes 786464 | tf_op jit(solution)/shard_map/ppermute | solution.py:22
  127.9 4.7 fusion.84
  132.6 2.1 fusion.83
  134.8 2.0 bitcast_dynamic-update-slice_fusion.11
  138.8 9.5 %fusion.68 = f32[256,2048]{1,0:T(8,128)} fusion(bf16[256,4096]{1,0:T(8,128)(2,1)S(1)} %get-tuple-element.58, bf16[4096,1,2048]{2,0,1:T(8,128)(2,1)} %param.8), kind=kOutput, calls=%fused_computation.187 | convolution fusion | flops 4294967296 | bytes 20971520 | tf_op jit(solution)/shard_map/dot_general | solution.py:230
  148.3 2.7 collective-permute-done.9
  152.0 18.0 %collective-permute-done.10 = bf16[64,2048]{1,0:T(8,128)(2,1)} collective-permute-done((bf16[64,2048]{1,0:T(8,128)(2,1)}, bf16[64,2048]{1,0:T(8,128)(2,1)}, u32[]{:S(2)}, u32[]{:S(2)}) %collective-permute-start.10) | collective-permute-done | bytes 262176 | tf_op jit(solution)/shard_map/ppermute | solution.py:48
  171.0 10.9 %convolution_add_fusion.2 = f32[256,4096]{1,0:T(8,128)} fusion(bf16[256,2048]{1,0:T(8,128)(2,1)S(1)} %bitcast.192, f32[4096]{0:T(1024)S(1)} %broadcast_multiply_fusion, bf16[4096,1,2048]{2,0,1:T(8,128)(2,1)} %param.8), kind=kOutput, calls=%fused_computation.5 | convolution fusion | flops 4296015872 | bytes 22036480 | tf_op jit(solution)/shard_map/dot_general | solution.py:165
  181.9 3.1 dynamic-slice_bitcast_fusion.2
  186.4 8.7 %fusion.8.refs_0_ = bf16[2048,1024]{1,0:T(8,128)(2,1)} fusion(bf16[128,2048]{1,0:T(8,128)(2,1)} %get-tuple-element.107, bf16[256,2048]{1,0:T(8,128)(2,1)} %get-tuple-element.109, bf16[384,2048]{1,0:T(8,128)(2,1)} %get-tuple-element.111, bf16[256,2048]{1,0:T(8,128)(2,1)S(1)} %copy-done.28, s32[1024]{0:T(1024)S(1)} %pad_add_fusion), kind=kOutput, calls=%fused_computation.20 | convolution fusion | flops 4314890240 | bytes 8392704 | tf_op jit(solution)/shard_map/dot_general | solution.py:158
  198.7 2.4 bitcast_dynamic-update-slice_fusion.3
  204.1 3.6 convolution_convert_fusion.refs_3_
  209.6 9.2 %fusion.65 = f32[128,2048]{1,0:T(8,128)} fusion(bf16[128,4096]{1,0:T(8,128)(2,1)S(1)} %copy-done.9, bf16[4096,1,2048]{2,0,1:T(8,128)(2,1)} %param.8), kind=kOutput, calls=%fused_computation.184 | convolution fusion | flops 2147483648 | bytes 18874368 | tf_op jit(solution)/shard_map/dot_general | solution.py:230
  220.4 4.5 collective-permute-done.21
  224.9 1.8 bitcast_dynamic-update-slice_fusion.2
  226.7 34.6 %collective-permute-done.22 = bf16[96,2048]{1,0:T(8,128)(2,1)} collective-permute-done((bf16[96,2048]{1,0:T(8,128)(2,1)}, bf16[96,2048]{1,0:T(8,128)(2,1)}, u32[]{:S(2)}, u32[]{:S(2)}) %collective-permute-start.22) | collective-permute-done | bytes 393248 | tf_op jit(solution)/shard_map/ppermute | solution.py:48
  263.9 2.1 constant_dynamic-update-slice_fusion.4
  266.0 10.7 %convolution_add_fusion = f32[384,4096]{1,0:T(8,128)S(1)} fusion(bf16[384,2048]{1,0:T(8,128)(2,1)} %bitcast.43.refs_7_, f32[4096]{0:T(1024)S(1)} %copy-done.38, bf16[4096,1,2048]{2,0,1:T(8,128)(2,1)} %param.8), kind=kOutput, calls=%fused_computation.2 | convolution fusion | flops 6444023808 | bytes 24657920 | tf_op jit(solution)/shard_map/dot_general | solution.py:165
  276.7 2.0 dynamic-slice_bitcast_fusion
  282.5 2.1 bitcast_dynamic-update-slice_fusion.7
  286.2 1.9 convert_reduce_fusion.1
  288.3 2.0 copy.12.refs_0_
  290.3 3.8 convolution_convert_fusion.1.refs_4_
  300.4 18.3 %collective-permute-done.32 = bf16[64,2048]{1,0:T(8,128)(2,1)} collective-permute-done((bf16[64,2048]{1,0:T(8,128)(2,1)}, bf16[64,2048]{1,0:T(8,128)(2,1)}, u32[]{:S(2)}, u32[]{:S(2)}) %collective-permute-start.32) | collective-permute-done | bytes 262176 | tf_op jit(solution)/shard_map/ppermute | solution.py:48
  320.4 3.3 bitcast_add_fusion
  327.6 2.8 collective-permute-start.19
  330.4 1.9 constant_dynamic-update-slice_fusion.2
  335.7 10.1 %collective-permute-done.25 = f32[2,48,4096]{2,1,0:T(8,128)} collective-permute-done((f32[2,48,4096]{2,1,0:T(8,128)}, f32[2,48,4096]{2,1,0:T(8,128)}, u32[]{:S(2)}, u32[]{:S(2)}) %collective-permute-start.25) | collective-permute-done | bytes 1572896 | tf_op jit(solution)/shard_map/ppermute | solution.py:33
  347.3 2.1 collective-permute-start.26
  349.4 1.9 constant_dynamic-update-slice_fusion
  352.1 7.0 %collective-permute-done.26 = f32[48,4096]{1,0:T(8,128)S(1)} collective-permute-done((f32[48,4096]{1,0:T(8,128)S(1)}, f32[48,4096]{1,0:T(8,128)S(1)}, u32[]{:S(2)}, u32[]{:S(2)}) %collective-permute-start.26) | collective-permute-done | bytes 786464 | tf_op jit(solution)/shard_map/ppermute | solution.py:33
  360.6 12.6 %convolution_add_fusion.1 = f32[256,4096]{1,0:T(8,128)} fusion(bf16[256,2048]{1,0:T(8,128)(2,1)} %bitcast.57.refs_8_, f32[4096]{0:T(1024)S(1)} %copy-done.39, bf16[4096,1,2048]{2,0,1:T(8,128)(2,1)} %param.8), kind=kOutput, calls=%fused_computation.4 | convolution fusion | flops 4296015872 | bytes 22036480 | tf_op jit(solution)/shard_map/dot_general | solution.py:165
  373.3 1.9 dynamic-slice_bitcast_fusion.1
  375.2 3.9 collective-permute-start.34
  383.4 5.3 collective-permute-done.27
  392.0 8.0 %collective-permute-done.28 = bf16[2,48,4096]{2,1,0:T(8,128)(2,1)S(1)} collective-permute-done((bf16[2,48,4096]{2,1,0:T(8,128)(2,1)S(1)}, bf16[2,48,4096]{2,1,0:T(8,128)(2,1)S(1)}, u32[]{:S(2)}, u32[]{:S(2)}) %collective-permute-start.28) | collective-permute-done | bytes 786464 | tf_op jit(solution)/shard_map/ppermute | solution.py:33
  401.8 9.4 %collective-permute-done.35 = f32[2,32,4096]{2,1,0:T(8,128)S(1)} collective-permute-done((f32[2,32,4096]{2,1,0:T(8,128)S(1)}, f32[2,32,4096]{2,1,0:T(8,128)S(1)}, u32[]{:S(2)}, u32[]{:S(2)}) %collective-permute-start.35) | collective-permute-done | bytes 1048608 | tf_op jit(solution)/shard_map/ppermute | solution.py:33
  413.2 6.5 %collective-permute-done.36 = f32[32,4096]{1,0:T(8,128)S(1)} collective-permute-done((f32[32,4096]{1,0:T(8,128)S(1)}, f32[32,4096]{1,0:T(8,128)S(1)}, u32[]{:S(2)}, u32[]{:S(2)}) %collective-permute-start.36) | collective-permute-done | bytes 524320 | tf_op jit(solution)/shard_map/ppermute | solution.py:33
  419.8 12.9 %broadcast_add_fusion = f32[128,4096]{1,0:T(8,128)} fusion(f32[4096]{0:T(1024)S(1)} %copy-done.39, bf16[128,2048]{1,0:T(8,128)(2,1)} %bitcast.71.refs_9_, bf16[4096,1,2048]{2,0,1:T(8,128)(2,1)} %param.8), kind=kOutput, calls=%fused_computation.44 | convolution fusion | flops 2148007936 | bytes 19415040 | tf_op jit(solution)/shard_map/dot_general | solution.py:165
  435.1 4.3 collective-permute-start.44
  440.5 2.5 collective-permute-start.39
  443.0 5.0 collective-permute-done.38
  448.0 4.1 collective-permute-start.40
  452.5 1.8 collective-permute-start.45
  454.3 17.2 %shard_map.77.refs_10_ = f32[4096,16,128]{2,1,0:T(8,128)} custom-call(f32[4096,1]{1,0:T(8,128)S(1)} %copy-done.2, bf16[4096,2048]{1,0:T(8,128)(2,1)} %bitcast.199, bf16[4096,256]{1,0:T(8,128)(2,1)S(1)} %convolution_convert_fusion.2.refs_2_, bf16[4096,384]{1,0:T(8,128)(2,1)} %convolution_convert_fusion.refs_3_, ...), custom_call_target="tpu_custom_call" | custom-call | flops 8589934592 | bytes 33554432 | tf_op jit(solution)/shard_map/pallas_call | solution.py:108
  471.7 5.4 %collective-permute-done.46 = f32[16,4096]{1,0:T(8,128)S(1)} collective-permute-done((f32[16,4096]{1,0:T(8,128)S(1)}, f32[16,4096]{1,0:T(8,128)S(1)}, u32[]{:S(2)}, u32[]{:S(2)}) %collective-permute-start.46) | collective-permute-done | bytes 262176 | tf_op jit(solution)/shard_map/ppermute | solution.py:33
  478.2 17.1 %shard_map.78 = f32[4096,16,128]{2,1,0:T(8,128)} custom-call(f32[4096,1]{1,0:T(8,128)S(1)} %copy-done.2, bf16[4096,2048]{1,0:T(8,128)(2,1)} %bitcast.200, bf16[4096,256]{1,0:T(8,128)(2,1)S(1)} %convolution_convert_fusion.2.refs_2_, bf16[4096,384]{1,0:T(8,128)(2,1)} %convolution_convert_fusion.refs_3_, ...), custom_call_target="tpu_custom_call", output_to_operand_aliasing={{}: (10, {})} | custom-call | flops 8589934592 | bytes 33554432 | tf_op jit(solution)/shard_map/pallas_call | solution.py:108
  498.5 2.1 collective-permute-done.48
  500.6 3.7 collective-permute-start.50
  505.5 27.5 %shard_map.76 = (f32[2048,32,128]{2,1,0:T(8,128)}, f32[1,4096]{1,0:T(1,128)}) custom-call(bf16[2048,1024]{1,0:T(8,128)(2,1)} %fusion.8.refs_0_, bf16[256,4096]{1,0:T(8,128)(2,1)} %bitcast.35.refs_1_, bf16[384,4096]{1,0:T(8,128)(2,1)S(1)} %bitcast.195, bf16[256,4096]{1,0:T(8,128)(2,1)S(1)} %bitcast.196, bf16[128,4096]{1,0:T(8,128)(2,1)S(1)} %bitcast.197), custom_call_target="tpu_custom_call" | custom-call | flops 17179869184 | bytes 46137344 | tf_op jit(solution)/shard_map/pallas_call | solution.py:130
  (284 shorter events, 95.6 us)
Async XLA Ops:
  7.2 127.5 %reduce-scatter.5.cloned.1.call-start = ((), (), s32[]{:S(2)}) async-start(), calls=%async_computation.4 | async-start | bytes 2621440 | tf_op jit(solution)/shard_map/reduce_scatter | solution.py:37
  9.5 13.1 %collective-permute-start = (bf16[64,4096]{1,0:T(8,128)(2,1)}, bf16[64,4096]{1,0:T(8,128)(2,1)}, u32[]{:S(2)}, u32[]{:S(2)}) collective-permute-start(bf16[64,4096]{1,0:T(8,128)(2,1)} %get-tuple-element.87), channel_id=1, source_target_pairs={{0,1},{1,0},{2,3},{3,2},{4,5},{5,4},{6,7},{7,6},{8,9},{9,8},{10,11... | collective-permute-start | bytes 1572872 | tf_op jit(solution)/shard_map/ppermute | solution.py:22
  12.5 18.0 %copy-start.22 = (bf16[128,4096]{1,0:T(8,128)(2,1)}, bf16[128,4096]{1,0:T(8,128)(2,1)S(1)}, u32[]{:S(2)}) copy-start(bf16[128,4096]{1,0:T(8,128)(2,1)S(1)} %get-tuple-element.89) | copy-start | bytes 3145732
  16.6 182.1 %copy-start.29 = (f32[1,2048]{1,0:T(1,128)}, f32[1,2048]{1,0:T(1,128)S(1)}, u32[]{:S(2)}) copy-start(f32[1,2048]{1,0:T(1,128)S(1)} %constant_dynamic-slice_fusion.9) | copy-start | bytes 24580
  22.6 6.1 %collective-permute-start.1 = (bf16[64,4096]{1,0:T(8,128)(2,1)}, bf16[64,4096]{1,0:T(8,128)(2,1)}, u32[]{:S(2)}, u32[]{:S(2)}) collective-permute-start(bf16[64,4096]{1,0:T(8,128)(2,1)} %collective-permute-done), channel_id=1, source_target_pairs={{0,2},{2,0},{4,6},{6,4},{1,3},{3,1},{5,7},{7,5},{8,10},{10,8},{12,... | collective-permute-start | bytes 1572872 | tf_op jit(solution)/shard_map/ppermute | solution.py:22
  28.5 31.4 %collective-permute-start.4 = (bf16[96,4096]{1,0:T(8,128)(2,1)}, bf16[96,4096]{1,0:T(8,128)(2,1)}, u32[]{:S(2)}, u32[]{:S(2)}) collective-permute-start(bf16[96,4096]{1,0:T(8,128)(2,1)} %constant_dynamic-slice_fusion.13), channel_id=1, source_target_pairs={{0,1},{1,0},{2,3},{3,2},{4,5},{5,4},{6,7},{7,6},{8,9},{9,8},{10,11... | collective-permute-start | bytes 2359304 | tf_op jit(solution)/shard_map/ppermute | solution.py:22
  40.9 156.4 %reduce-scatter.7.cloned.1.call-start = ((), (), s32[]{:S(2)}) async-start(), calls=%async_computation.5 | async-start | bytes 3932160 | tf_op jit(solution)/shard_map/reduce_scatter | solution.py:37
  42.3 21.4 %collective-permute-start.2 = (bf16[128,2048]{1,0:T(8,128)(2,1)S(1)}, bf16[128,2048]{1,0:T(8,128)(2,1)S(1)}, u32[]{:S(2)}, u32[]{:S(2)}) collective-permute-start(bf16[128,2048]{1,0:T(8,128)(2,1)S(1)} %constant_dynamic-slice_fusion.15), channel_id=1, source_target_pairs={{0,1},{1,0},{2,3},{3,2},{4,5},{5,4},{6,7},{7,6},{8,9},{9,8},{10,11... | collective-permute-start | bytes 1572872 | tf_op jit(solution)/shard_map/ppermute | solution.py:22
  43.6 17.1 %collective-permute-start.3 = (bf16[512,16]{0,1:T(8,128)(2,1)S(1)}, bf16[512,16]{0,1:T(8,128)(2,1)S(1)}, u32[]{:S(2)}, u32[]{:S(2)}) collective-permute-start(bf16[512,16]{0,1:T(8,128)(2,1)S(1)} %constant_dynamic-slice_fusion.14), channel_id=1, source_target_pairs={{0,1},{1,0},{2,3},{3,2},{4,5},{5,4},{6,7},{7,6},{8,9},{9,8},{10,11... | collective-permute-start | bytes 49160 | tf_op jit(solution)/shard_map/ppermute | solution.py:22
  51.2 8.7 %collective-permute-start.12 = (f32[4096]{0:T(1024)S(1)}, f32[4096]{0:T(1024)S(1)}, u32[]{:S(2)}, u32[]{:S(2)}) collective-permute-start(f32[4096]{0:T(1024)S(1)} %multiply_reduce_fusion), channel_id=1, source_target_pairs={{0,1},{1,0},{2,3},{3,2},{4,5},{5,4},{6,7},{7,6},{8,9},{9,8},{10,11... | collective-permute-start | bytes 49160 | tf_op jit(solution)/shard_map/ppermute | solution.py:22
  59.9 111.1 %copy-start.37 = (f32[4096]{0:T(1024)}, f32[4096]{0:T(1024)S(1)}, u32[]{:S(2)}) copy-start(f32[4096]{0:T(1024)S(1)} %broadcast_multiply_fusion) | copy-start | bytes 49156
  59.9 6.0 %collective-permute-start.5 = (bf16[96,4096]{1,0:T(8,128)(2,1)}, bf16[96,4096]{1,0:T(8,128)(2,1)S(1)}, u32[]{:S(2)}, u32[]{:S(2)}) collective-permute-start(bf16[96,4096]{1,0:T(8,128)(2,1)} %collective-permute-done.4), channel_id=1, source_target_pairs={{0,2},{2,0},{4,6},{6,4},{1,3},{3,1},{5,7},{7,5},{8,10},{10,8},{12,... | collective-permute-start | bytes 2359304 | tf_op jit(solution)/shard_map/ppermute | solution.py:22
  63.5 19.5 %collective-permute-start.7 = (bf16[96,4096]{1,0:T(8,128)(2,1)}, bf16[96,4096]{1,0:T(8,128)(2,1)}, u32[]{:S(2)}, u32[]{:S(2)}) collective-permute-start(bf16[96,4096]{1,0:T(8,128)(2,1)} %constant_dynamic-slice_fusion.11), channel_id=1, source_target_pairs={{0,1},{1,0},{2,3},{3,2},{4,5},{5,4},{6,7},{7,6},{8,9},{9,8},{10,11... | collective-permute-start | bytes 2359304 | tf_op jit(solution)/shard_map/ppermute | solution.py:22
  83.0 7.8 %collective-permute-start.20 = (bf16[96,4096]{1,0:T(8,128)(2,1)}, bf16[96,4096]{1,0:T(8,128)(2,1)}, u32[]{:S(2)}, u32[]{:S(2)}) collective-permute-start(bf16[96,4096]{1,0:T(8,128)(2,1)} %collective-permute-done.7), channel_id=1, source_target_pairs={{0,2},{2,0},{4,6},{6,4},{1,3},{3,1},{5,7},{7,5},{8,10},{10,8},{12,... | collective-permute-start | bytes 2359304 | tf_op jit(solution)/shard_map/ppermute | solution.py:22
  86.3 41.6 %collective-permute-start.6 = (bf16[192,2048]{1,0:T(8,128)(2,1)}, bf16[192,2048]{1,0:T(8,128)(2,1)}, u32[]{:S(2)}, u32[]{:S(2)}) collective-permute-start(bf16[192,2048]{1,0:T(8,128)(2,1)} %constant_dynamic-slice_fusion.12), channel_id=1, source_target_pairs={{0,1},{1,0},{2,3},{3,2},{4,5},{5,4},{6,7},{7,6},{8,9},{9,8},{10,11... | collective-permute-start | bytes 2359304 | tf_op jit(solution)/shard_map/ppermute | solution.py:22
  87.6 34.9 %collective-permute-start.8 = (bf16[192,2048]{1,0:T(8,128)(2,1)}, bf16[192,2048]{1,0:T(8,128)(2,1)}, u32[]{:S(2)}, u32[]{:S(2)}) collective-permute-start(bf16[192,2048]{1,0:T(8,128)(2,1)} %constant_dynamic-slice_fusion.10), channel_id=1, source_target_pairs={{0,1},{1,0},{2,3},{3,2},{4,5},{5,4},{6,7},{7,6},{8,9},{9,8},{10,11... | collective-permute-start | bytes 2359304 | tf_op jit(solution)/shard_map/ppermute | solution.py:22
  88.9 192.5 %reduce-scatter.9.cloned.1.call-start = ((), (), s32[]{:S(2)}) async-start(), calls=%async_computation.6 | async-start | bytes 2621440 | tf_op jit(solution)/shard_map/reduce_scatter | solution.py:37
  95.0 31.2 %copy-start.20 = (bf16[2,64,4096]{2,1,0:T(8,128)(2,1)S(1)}, bf16[2,64,4096]{2,1,0:T(8,128)(2,1)}, u32[]{:S(2)}) copy-start(bf16[2,64,4096]{2,1,0:T(8,128)(2,1)} %copy-done.19) | copy-start | bytes 3145732
  95.0 31.2 %copy-start.21 = (bf16[128,4096]{1,0:T(8,128)(2,1)S(1)}, bf16[128,4096]{1,0:T(8,128)(2,1)}, u32[]{:S(2)}) copy-start(bf16[128,4096]{1,0:T(8,128)(2,1)} %get-tuple-element.88) | copy-start | bytes 3145732
  95.0 31.2 %copy-start.23 = (bf16[128,4096]{1,0:T(8,128)(2,1)S(1)}, bf16[128,4096]{1,0:T(8,128)(2,1)}, u32[]{:S(2)}) copy-start(bf16[128,4096]{1,0:T(8,128)(2,1)} %copy-done.22) | copy-start | bytes 3145732
  136.8 14.2 %collective-permute-start.9 = (bf16[64,2048]{1,0:T(8,128)(2,1)}, bf16[64,2048]{1,0:T(8,128)(2,1)}, u32[]{:S(2)}, u32[]{:S(2)}) collective-permute-start(bf16[64,2048]{1,0:T(8,128)(2,1)} %get-tuple-element.85), channel_id=1, source_target_pairs={{0,8},{8,16},{16,24},{24,0},{1,9},{9,17},{17,25},{25,1},{2,10},{10... | collective-permute-start | bytes 786440 | tf_op jit(solution)/shard_map/ppermute | solution.py:48
  136.8 33.1 %collective-permute-start.10 = (bf16[64,2048]{1,0:T(8,128)(2,1)}, bf16[64,2048]{1,0:T(8,128)(2,1)}, u32[]{:S(2)}, u32[]{:S(2)}) collective-permute-start(bf16[64,2048]{1,0:T(8,128)(2,1)} %get-tuple-element.85), channel_id=1, source_target_pairs={{0,16},{8,24},{16,0},{24,8},{1,17},{9,25},{17,1},{25,9},{2,18},{10... | collective-permute-start | bytes 786440 | tf_op jit(solution)/shard_map/ppermute | solution.py:48
  138.2 32.7 %collective-permute-start.11 = (bf16[64,2048]{1,0:T(8,128)(2,1)}, bf16[64,2048]{1,0:T(8,128)(2,1)S(1)}, u32[]{:S(2)}, u32[]{:S(2)}) collective-permute-start(bf16[64,2048]{1,0:T(8,128)(2,1)} %get-tuple-element.85), channel_id=1, source_target_pairs={{0,24},{8,0},{16,8},{24,16},{1,25},{9,1},{17,9},{25,17},{2,26},{10... | collective-permute-start | bytes 786440 | tf_op jit(solution)/shard_map/ppermute | solution.py:48
  185.1 10.0 %collective-permute-start.13 = (f32[2,2,32,4096]{3,2,1,0:T(8,128)}, f32[2,2,32,4096]{3,2,1,0:T(8,128)S(1)}, u32[]{:S(2)}, u32[]{:S(2)}) collective-permute-start(f32[2,2,32,4096]{3,2,1,0:T(8,128)} %dynamic-slice_bitcast_fusion.2), channel_id=1, source_target_pairs={{0,2},{2,0},{4,6},{6,4},{1,3},{3,1},{5,7},{7,5},{8,10},{10,8},{12,... | collective-permute-start | bytes 6291464 | tf_op jit(solution)/shard_map/ppermute | solution.py:22
  186.3 146.8 %reduce-scatter.11.cloned.1.call-start = ((), (), s32[]{:S(2)}) async-start(), calls=%async_computation.7 | async-start | bytes 1310720 | tf_op jit(solution)/shard_map/reduce_scatter | solution.py:37
  197.1 21.7 %collective-permute-start.14 = (f32[2,32,4096]{2,1,0:T(8,128)}, f32[2,32,4096]{2,1,0:T(8,128)}, u32[]{:S(2)}, u32[]{:S(2)}) collective-permute-start(f32[2,32,4096]{2,1,0:T(8,128)} %pad_maximum_fusion.4), channel_id=1, source_target_pairs={{0,4},{1,5},{2,3},{3,2},{4,0},{5,1},{6,7},{7,6},{8,12},{9,13},{10,... | collective-permute-start | bytes 3145736 | tf_op jit(solution)/shard_map/ppermute | solution.py:33
  201.1 23.8 %collective-permute-start.21 = (bf16[96,2048]{1,0:T(8,128)(2,1)}, bf16[96,2048]{1,0:T(8,128)(2,1)}, u32[]{:S(2)}, u32[]{:S(2)}) collective-permute-start(bf16[96,2048]{1,0:T(8,128)(2,1)} %get-tuple-element.80), channel_id=1, source_target_pairs={{0,8},{8,16},{16,24},{24,0},{1,9},{9,17},{17,25},{25,1},{2,10},{10... | collective-permute-start | bytes 1179656 | tf_op jit(solution)/shard_map/ppermute | solution.py:48
  201.1 60.2 %collective-permute-start.22 = (bf16[96,2048]{1,0:T(8,128)(2,1)}, bf16[96,2048]{1,0:T(8,128)(2,1)}, u32[]{:S(2)}, u32[]{:S(2)}) collective-permute-start(bf16[96,2048]{1,0:T(8,128)(2,1)} %get-tuple-element.80), channel_id=1, source_target_pairs={{0,16},{8,24},{16,0},{24,8},{1,17},{9,25},{17,1},{25,9},{2,18},{10... | collective-permute-start | bytes 1179656 | tf_op jit(solution)/shard_map/ppermute | solution.py:48
  201.3 61.8 %collective-permute-start.23 = (bf16[96,2048]{1,0:T(8,128)(2,1)}, bf16[96,2048]{1,0:T(8,128)(2,1)S(1)}, u32[]{:S(2)}, u32[]{:S(2)}) collective-permute-start(bf16[96,2048]{1,0:T(8,128)(2,1)} %get-tuple-element.80), channel_id=1, source_target_pairs={{0,24},{8,0},{16,8},{24,16},{1,25},{9,1},{17,9},{25,17},{2,26},{10... | collective-permute-start | bytes 1179656 | tf_op jit(solution)/shard_map/ppermute | solution.py:48
  220.1 43.8 %collective-permute-start.15 = (f32[32,4096]{1,0:T(8,128)S(1)}, f32[32,4096]{1,0:T(8,128)S(1)}, u32[]{:S(2)}, u32[]{:S(2)}) collective-permute-start(f32[32,4096]{1,0:T(8,128)S(1)} %fusion.18), channel_id=1, source_target_pairs={{0,1},{1,0},{2,6},{3,7},{4,5},{5,4},{6,2},{7,3},{8,9},{9,8},{10,14... | collective-permute-start | bytes 1572872 | tf_op jit(solution)/shard_map/ppermute | solution.py:33
  226.7 39.2 %copy-start.38 = (f32[4096]{0:T(1024)S(1)}, f32[4096]{0:T(1024)}, u32[]{:S(2)}) copy-start(f32[4096]{0:T(1024)} %copy-done.37) | copy-start | bytes 49156
  280.4 40.1 %collective-permute-start.24 = (f32[2,2,48,4096]{3,2,1,0:T(8,128)}, f32[2,2,48,4096]{3,2,1,0:T(8,128)}, u32[]{:S(2)}, u32[]{:S(2)}) collective-permute-start(f32[2,2,48,4096]{3,2,1,0:T(8,128)} %dynamic-slice_bitcast_fusion), channel_id=1, source_target_pairs={{0,2},{2,0},{4,6},{6,4},{1,3},{3,1},{5,7},{7,5},{8,10},{10,8},{12,... | collective-permute-start | bytes 9437192 | tf_op jit(solution)/shard_map/ppermute | solution.py:22
  281.1 13.5 %collective-permute-start.16 = (bf16[32,4096]{1,0:T(8,128)(2,1)S(1)}, bf16[32,4096]{1,0:T(8,128)(2,1)}, u32[]{:S(2)}, u32[]{:S(2)}) collective-permute-start(bf16[32,4096]{1,0:T(8,128)(2,1)S(1)} %get-tuple-element.82), channel_id=1, source_target_pairs={{0,1},{1,0},{2,6},{3,7},{4,5},{5,4},{6,2},{7,3},{8,9},{9,8},{10,14... | collective-permute-start | bytes 786440 | tf_op jit(solution)/shard_map/ppermute | solution.py:33
  284.6 13.0 %collective-permute-start.31 = (bf16[64,2048]{1,0:T(8,128)(2,1)}, bf16[64,2048]{1,0:T(8,128)(2,1)}, u32[]{:S(2)}, u32[]{:S(2)}) collective-permute-start(bf16[64,2048]{1,0:T(8,128)(2,1)} %get-tuple-element.76), channel_id=1, source_target_pairs={{0,8},{8,16},{16,24},{24,0},{1,9},{9,17},{17,25},{25,1},{2,10},{10... | collective-permute-start | bytes 786440 | tf_op jit(solution)/shard_map/ppermute | solution.py:48
  284.7 34.1 %collective-permute-start.32 = (bf16[64,2048]{1,0:T(8,128)(2,1)}, bf16[64,2048]{1,0:T(8,128)(2,1)}, u32[]{:S(2)}, u32[]{:S(2)}) collective-permute-start(bf16[64,2048]{1,0:T(8,128)(2,1)} %get-tuple-element.76), channel_id=1, source_target_pairs={{0,16},{8,24},{16,0},{24,8},{1,17},{9,25},{17,1},{25,9},{2,18},{10... | collective-permute-start | bytes 786440 | tf_op jit(solution)/shard_map/ppermute | solution.py:48
  284.8 41.2 %collective-permute-start.33 = (bf16[64,2048]{1,0:T(8,128)(2,1)}, bf16[64,2048]{1,0:T(8,128)(2,1)}, u32[]{:S(2)}, u32[]{:S(2)}) collective-permute-start(bf16[64,2048]{1,0:T(8,128)(2,1)} %get-tuple-element.76), channel_id=1, source_target_pairs={{0,24},{8,0},{16,8},{24,16},{1,25},{9,1},{17,9},{25,17},{2,26},{10... | collective-permute-start | bytes 786440 | tf_op jit(solution)/shard_map/ppermute | solution.py:48
  295.6 32.0 %collective-permute-start.17 = (bf16[2,32,4096]{2,1,0:T(8,128)(2,1)S(1)}, bf16[2,32,4096]{2,1,0:T(8,128)(2,1)}, u32[]{:S(2)}, u32[]{:S(2)}) collective-permute-start(bf16[2,32,4096]{2,1,0:T(8,128)(2,1)S(1)} %pad_maximum_fusion.8), channel_id=1, source_target_pairs={{0,4},{1,5},{2,3},{3,2},{4,0},{5,1},{6,7},{7,6},{8,12},{9,13},{10,... | collective-permute-start | bytes 1572872 | tf_op jit(solution)/shard_map/ppermute | solution.py:33
  297.6 34.7 %collective-permute-start.18 = (bf16[2,32,4096]{2,1,0:T(8,128)(2,1)S(1)}, bf16[2,32,4096]{2,1,0:T(8,128)(2,1)S(1)}, u32[]{:S(2)}, u32[]{:S(2)}) collective-permute-start(bf16[2,32,4096]{2,1,0:T(8,128)(2,1)S(1)} %pad_maximum_fusion.8), channel_id=1, source_target_pairs={{0,2},{2,0},{4,6},{6,4},{1,3},{3,1},{5,7},{7,5},{8,10},{10,8},{12,... | collective-permute-start | bytes 1572872 | tf_op jit(solution)/shard_map/ppermute | solution.py:22
  325.9 19.9 %collective-permute-start.25 = (f32[2,48,4096]{2,1,0:T(8,128)}, f32[2,48,4096]{2,1,0:T(8,128)}, u32[]{:S(2)}, u32[]{:S(2)}) collective-permute-start(f32[2,48,4096]{2,1,0:T(8,128)} %pad_maximum_fusion.3), channel_id=1, source_target_pairs={{0,4},{1,5},{2,3},{3,2},{4,0},{5,1},{6,7},{7,6},{8,12},{9,13},{10,... | collective-permute-start | bytes 4718600 | tf_op jit(solution)/shard_map/ppermute | solution.py:33
  327.6 21.8 %collective-permute-start.19 = (bf16[2,32,4096]{2,1,0:T(8,128)(2,1)}, bf16[2,32,4096]{2,1,0:T(8,128)(2,1)}, u32[]{:S(2)}, u32[]{:S(2)}) collective-permute-start(bf16[2,32,4096]{2,1,0:T(8,128)(2,1)} %collective-permute-done.17), channel_id=1, source_target_pairs={{0,2},{2,0},{4,6},{6,4},{1,3},{3,1},{5,7},{7,5},{8,10},{10,8},{12,... | collective-permute-start | bytes 1572872 | tf_op jit(solution)/shard_map/ppermute | solution.py:22
  335.7 15.7 %collective-permute-start.41 = (bf16[32,2048]{1,0:T(8,128)(2,1)}, bf16[32,2048]{1,0:T(8,128)(2,1)S(1)}, u32[]{:S(2)}, u32[]{:S(2)}) collective-permute-start(bf16[32,2048]{1,0:T(8,128)(2,1)} %get-tuple-element.72), channel_id=1, source_target_pairs={{0,8},{8,16},{16,24},{24,0},{1,9},{9,17},{17,25},{25,1},{2,10},{10... | collective-permute-start | bytes 393224 | tf_op jit(solution)/shard_map/ppermute | solution.py:48
  347.3 11.9 %collective-permute-start.26 = (f32[48,4096]{1,0:T(8,128)S(1)}, f32[48,4096]{1,0:T(8,128)S(1)}, u32[]{:S(2)}, u32[]{:S(2)}) collective-permute-start(f32[48,4096]{1,0:T(8,128)S(1)} %fusion.12), channel_id=1, source_target_pairs={{0,1},{1,0},{2,6},{3,7},{4,5},{5,4},{6,2},{7,3},{8,9},{9,8},{10,14... | collective-permute-start | bytes 2359304 | tf_op jit(solution)/shard_map/ppermute | solution.py:33
  351.2 27.8 %collective-permute-start.42 = (bf16[32,2048]{1,0:T(8,128)(2,1)}, bf16[32,2048]{1,0:T(8,128)(2,1)}, u32[]{:S(2)}, u32[]{:S(2)}) collective-permute-start(bf16[32,2048]{1,0:T(8,128)(2,1)} %get-tuple-element.72), channel_id=1, source_target_pairs={{0,16},{8,24},{16,0},{24,8},{1,17},{9,25},{17,1},{25,9},{2,18},{10... | collective-permute-start | bytes 393224 | tf_op jit(solution)/shard_map/ppermute | solution.py:48
  351.2 30.6 %collective-permute-start.43 = (bf16[32,2048]{1,0:T(8,128)(2,1)}, bf16[32,2048]{1,0:T(8,128)(2,1)}, u32[]{:S(2)}, u32[]{:S(2)}) collective-permute-start(bf16[32,2048]{1,0:T(8,128)(2,1)} %get-tuple-element.72), channel_id=1, source_target_pairs={{0,24},{8,0},{16,8},{24,16},{1,25},{9,1},{17,9},{25,17},{2,26},{10... | collective-permute-start | bytes 393224 | tf_op jit(solution)/shard_map/ppermute | solution.py:48
  375.2 15.1 %collective-permute-start.34 = (f32[2,2,32,4096]{3,2,1,0:T(8,128)S(1)}, f32[2,2,32,4096]{3,2,1,0:T(8,128)S(1)}, u32[]{:S(2)}, u32[]{:S(2)}) collective-permute-start(f32[2,2,32,4096]{3,2,1,0:T(8,128)S(1)} %dynamic-slice_bitcast_fusion.1), channel_id=1, source_target_pairs={{0,2},{2,0},{4,6},{6,4},{1,3},{3,1},{5,7},{7,5},{8,10},{10,8},{12,... | collective-permute-start | bytes 6291464 | tf_op jit(solution)/shard_map/ppermute | solution.py:22
  381.7 7.0 %collective-permute-start.27 = (bf16[48,4096]{1,0:T(8,128)(2,1)S(1)}, bf16[48,4096]{1,0:T(8,128)(2,1)S(1)}, u32[]{:S(2)}, u32[]{:S(2)}) collective-permute-start(bf16[48,4096]{1,0:T(8,128)(2,1)S(1)} %get-tuple-element.78), channel_id=1, source_target_pairs={{0,1},{1,0},{2,6},{3,7},{4,5},{5,4},{6,2},{7,3},{8,9},{9,8},{10,14... | collective-permute-start | bytes 1179656 | tf_op jit(solution)/shard_map/ppermute | solution.py:33
  388.8 11.2 %collective-permute-start.28 = (bf16[2,48,4096]{2,1,0:T(8,128)(2,1)S(1)}, bf16[2,48,4096]{2,1,0:T(8,128)(2,1)S(1)}, u32[]{:S(2)}, u32[]{:S(2)}) collective-permute-start(bf16[2,48,4096]{2,1,0:T(8,128)(2,1)S(1)} %pad_maximum_fusion.7), channel_id=1, source_target_pairs={{0,4},{1,5},{2,3},{3,2},{4,0},{5,1},{6,7},{7,6},{8,12},{9,13},{10,... | collective-permute-start | bytes 2359304 | tf_op jit(solution)/shard_map/ppermute | solution.py:33
  390.3 21.1 %collective-permute-start.29 = (bf16[2,48,4096]{2,1,0:T(8,128)(2,1)S(1)}, bf16[2,48,4096]{2,1,0:T(8,128)(2,1)S(1)}, u32[]{:S(2)}, u32[]{:S(2)}) collective-permute-start(bf16[2,48,4096]{2,1,0:T(8,128)(2,1)S(1)} %pad_maximum_fusion.7), channel_id=1, source_target_pairs={{0,2},{2,0},{4,6},{6,4},{1,3},{3,1},{5,7},{7,5},{8,10},{10,8},{12,... | collective-permute-start | bytes 2359304 | tf_op jit(solution)/shard_map/ppermute | solution.py:22
  390.7 20.6 %collective-permute-start.35 = (f32[2,32,4096]{2,1,0:T(8,128)S(1)}, f32[2,32,4096]{2,1,0:T(8,128)S(1)}, u32[]{:S(2)}, u32[]{:S(2)}) collective-permute-start(f32[2,32,4096]{2,1,0:T(8,128)S(1)} %pad_maximum_fusion.6), channel_id=1, source_target_pairs={{0,4},{1,5},{2,3},{3,2},{4,0},{5,1},{6,7},{7,6},{8,12},{9,13},{10,... | collective-permute-start | bytes 3145736 | tf_op jit(solution)/shard_map/ppermute | solution.py:33
  400.0 11.4 %collective-permute-start.30 = (bf16[2,48,4096]{2,1,0:T(8,128)(2,1)S(1)}, bf16[2,48,4096]{2,1,0:T(8,128)(2,1)S(1)}, u32[]{:S(2)}, u32[]{:S(2)}) collective-permute-start(bf16[2,48,4096]{2,1,0:T(8,128)(2,1)S(1)} %collective-permute-done.28), channel_id=1, source_target_pairs={{0,2},{2,0},{4,6},{6,4},{1,3},{3,1},{5,7},{7,5},{8,10},{10,8},{12,... | collective-permute-start | bytes 2359304 | tf_op jit(solution)/shard_map/ppermute | solution.py:22
  411.3 8.4 %collective-permute-start.36 = (f32[32,4096]{1,0:T(8,128)S(1)}, f32[32,4096]{1,0:T(8,128)S(1)}, u32[]{:S(2)}, u32[]{:S(2)}) collective-permute-start(f32[32,4096]{1,0:T(8,128)S(1)} %fusion.15), channel_id=1, source_target_pairs={{0,1},{1,0},{2,6},{3,7},{4,5},{5,4},{6,2},{7,3},{8,9},{9,8},{10,14... | collective-permute-start | bytes 1572872 | tf_op jit(solution)/shard_map/ppermute | solution.py:33
  433.7 5.7 %collective-permute-start.37 = (bf16[32,4096]{1,0:T(8,128)(2,1)S(1)}, bf16[32,4096]{1,0:T(8,128)(2,1)S(1)}, u32[]{:S(2)}, u32[]{:S(2)}) collective-permute-start(bf16[32,4096]{1,0:T(8,128)(2,1)S(1)} %get-tuple-element.74), channel_id=1, source_target_pairs={{0,1},{1,0},{2,6},{3,7},{4,5},{5,4},{6,2},{7,3},{8,9},{9,8},{10,14... | collective-permute-start | bytes 786440 | tf_op jit(solution)/shard_map/ppermute | solution.py:33
  435.1 17.1 %collective-permute-start.44 = (f32[2,2,16,4096]{3,2,1,0:T(8,128)S(1)}, f32[2,2,16,4096]{3,2,1,0:T(8,128)S(1)}, u32[]{:S(2)}, u32[]{:S(2)}) collective-permute-start(f32[2,2,16,4096]{3,2,1,0:T(8,128)S(1)} %dynamic-slice_bitcast_fusion.3), channel_id=1, source_target_pairs={{0,2},{2,0},{4,6},{6,4},{1,3},{3,1},{5,7},{7,5},{8,10},{10,8},{12,... | collective-permute-start | bytes 3145736 | tf_op jit(solution)/shard_map/ppermute | solution.py:22
  439.5 8.5 %collective-permute-start.38 = (bf16[2,32,4096]{2,1,0:T(8,128)(2,1)S(1)}, bf16[2,32,4096]{2,1,0:T(8,128)(2,1)S(1)}, u32[]{:S(2)}, u32[]{:S(2)}) collective-permute-start(bf16[2,32,4096]{2,1,0:T(8,128)(2,1)S(1)} %pad_maximum_fusion.9), channel_id=1, source_target_pairs={{0,4},{1,5},{2,3},{3,2},{4,0},{5,1},{6,7},{7,6},{8,12},{9,13},{10,... | collective-permute-start | bytes 1572872 | tf_op jit(solution)/shard_map/ppermute | solution.py:33
  440.5 11.6 %collective-permute-start.39 = (bf16[2,32,4096]{2,1,0:T(8,128)(2,1)S(1)}, bf16[2,32,4096]{2,1,0:T(8,128)(2,1)S(1)}, u32[]{:S(2)}, u32[]{:S(2)}) collective-permute-start(bf16[2,32,4096]{2,1,0:T(8,128)(2,1)S(1)} %pad_maximum_fusion.9), channel_id=1, source_target_pairs={{0,2},{2,0},{4,6},{6,4},{1,3},{3,1},{5,7},{7,5},{8,10},{10,8},{12,... | collective-permute-start | bytes 1572872 | tf_op jit(solution)/shard_map/ppermute | solution.py:22
  448.0 23.6 %collective-permute-start.40 = (bf16[2,32,4096]{2,1,0:T(8,128)(2,1)S(1)}, bf16[2,32,4096]{2,1,0:T(8,128)(2,1)S(1)}, u32[]{:S(2)}, u32[]{:S(2)}) collective-permute-start(bf16[2,32,4096]{2,1,0:T(8,128)(2,1)S(1)} %collective-permute-done.38), channel_id=1, source_target_pairs={{0,2},{2,0},{4,6},{6,4},{1,3},{3,1},{5,7},{7,5},{8,10},{10,8},{12,... | collective-permute-start | bytes 1572872 | tf_op jit(solution)/shard_map/ppermute | solution.py:22
  452.5 19.0 %collective-permute-start.45 = (f32[2,16,4096]{2,1,0:T(8,128)S(1)}, f32[2,16,4096]{2,1,0:T(8,128)S(1)}, u32[]{:S(2)}, u32[]{:S(2)}) collective-permute-start(f32[2,16,4096]{2,1,0:T(8,128)S(1)} %pad_maximum_fusion.10), channel_id=1, source_target_pairs={{0,4},{1,5},{2,3},{3,2},{4,0},{5,1},{6,7},{7,6},{8,12},{9,13},{10,... | collective-permute-start | bytes 1572872 | tf_op jit(solution)/shard_map/ppermute | solution.py:33
  471.5 5.6 %collective-permute-start.46 = (f32[16,4096]{1,0:T(8,128)S(1)}, f32[16,4096]{1,0:T(8,128)S(1)}, u32[]{:S(2)}, u32[]{:S(2)}) collective-permute-start(f32[16,4096]{1,0:T(8,128)S(1)} %fusion.21), channel_id=1, source_target_pairs={{0,1},{1,0},{2,6},{3,7},{4,5},{5,4},{6,2},{7,3},{8,9},{9,8},{10,14... | collective-permute-start | bytes 786440 | tf_op jit(solution)/shard_map/ppermute | solution.py:33
  478.1 17.2 %collective-permute-start.47 = (bf16[16,4096]{1,0:T(8,128)(2,1)S(1)}, bf16[16,4096]{1,0:T(8,128)(2,1)S(1)}, u32[]{:S(2)}, u32[]{:S(2)}) collective-permute-start(bf16[16,4096]{1,0:T(8,128)(2,1)S(1)} %get-tuple-element.70), channel_id=1, source_target_pairs={{0,1},{1,0},{2,6},{3,7},{4,5},{5,4},{6,2},{7,3},{8,9},{9,8},{10,14... | collective-permute-start | bytes 393224 | tf_op jit(solution)/shard_map/ppermute | solution.py:33
  478.2 27.3 %copy-start.6 = (bf16[8,48,4096]{2,1,0:T(8,128)(2,1)S(1)}, bf16[8,48,4096]{2,1,0:T(8,128)(2,1)}, u32[]{:S(2)}) copy-start(bf16[8,48,4096]{2,1,0:T(8,128)(2,1)} %copy-done.5) | copy-start | bytes 9437188
  495.3 5.3 collective-permute-start.48
  496.9 7.5 %collective-permute-start.49 = (bf16[2,16,4096]{2,1,0:T(8,128)(2,1)S(1)}, bf16[2,16,4096]{2,1,0:T(8,128)(2,1)S(1)}, u32[]{:S(2)}, u32[]{:S(2)}) collective-permute-start(bf16[2,16,4096]{2,1,0:T(8,128)(2,1)S(1)} %pad_maximum_fusion.11), channel_id=1, source_target_pairs={{0,2},{2,0},{4,6},{6,4},{1,3},{3,1},{5,7},{7,5},{8,10},{10,8},{12,... | collective-permute-start | bytes 786440 | tf_op jit(solution)/shard_map/ppermute | solution.py:22
  500.6 4.8 collective-permute-start.50
  505.5 27.5 %copy-start.1 = (f32[1,4096]{1,0:T(1,128)S(1)}, f32[1,4096]{1,0:T(1,128)}, u32[]{:S(2)}) copy-start(f32[1,4096]{1,0:T(1,128)} %param.9) | copy-start | bytes 49156
  (38 other events, 193.5 us)
Sparse Core Ops, SparseCore 0:
  41.0 42.8 reduce-scatter.4
  89.0 68.1 reduce-scatter.6
  186.4 69.1 reduce-scatter.8
  286.3 38.8 reduce-scatter.10

commit v3 on v2

--- a/solution.py
+++ b/solution.py
@@ -10,7 +10,7 @@
 penalty = 1.0
 epsilon = 1e-06
 
-CHUNKS = (2, 3, 2, 1)
+CHUNKS = (3, 3, 2)
 LANES = 128
 TILE = 1024
 GROUP = 8
@@ -44,7 +44,7 @@
         return lax.all_gather(block, "lat", axis=0, tiled=True)
     out = jnp.zeros((n, rows, width), block.dtype)
     out = lax.dynamic_update_index_in_dim(out, block, me, 0)
-    for shift in range(1, n):
+    for shift in sorted(range(1, n), key=lambda i: min(i, n - i)):
         got = lax.ppermute(block, "lat", [(i, (i + shift) % n) for i in range(n)])
         out = lax.dynamic_update_index_in_dim(out, got, lax.rem(me - shift + n, n), 0)
     return out.reshape(n * rows, width)
@@ -160,7 +160,7 @@
     ).astype(jnp.bfloat16)
 
 
-def reduce_plane(resid, weight, offset, core, column):
+def reduce_pair(resid, weight, offset, core):
     sub, feats = resid.shape[0] // 8, weight.shape[0]
     terms = lax.dot_general(
         resid, weight, (((1,), (1,)), ((), ())), preferred_element_type=jnp.float32
@@ -168,8 +168,10 @@
     blocks = (terms + offset[None, :]).reshape(2, 2, 2, sub, feats)
     to_send = lax.dynamic_index_in_dim(blocks, 1 - core, 2, keepdims=False)
     to_keep = lax.dynamic_index_in_dim(blocks, core, 2, keepdims=False)
-    total = (to_keep + swap(to_send, "lyr")).reshape(4, sub, feats)
-
+    return (to_keep + swap(to_send, "lyr")).reshape(4, sub, feats), to_send
+
+
+def reduce_plane(total, core, column):
     def pick(dp_other, column_other):
         index = 2 * dp_other + jnp.where(column_other == 1, 1 - column, column)
         return lax.dynamic_index_in_dim(total, index, 0, keepdims=False)
@@ -179,7 +181,7 @@
     got = swap_split(jnp.stack([pick(first_dp, first_column), pick(1, 1)]), False)
     mine = pick(0, 0) + got[0]
     later = pick(second_dp, second_column) + got[1]
-    return total, mine + swap_split(later, True)
+    return mine + swap_split(later, True)
 
 
 def gather_plane(mine):
@@ -221,38 +223,26 @@
     def columns(value, which, count):
         return lax.dynamic_slice_in_dim(value, which * count, count, 1)
 
-    groups = [(0, 1), (1, 2), (2, len(CHUNKS))]
     lat_chunks, codes_other = [], []
     partials, recons, resid_own, resid_chunks, grad_chunks, mines = [], [], [], [], [], []
 
-    def local_recon(k):
-        lat = lat_chunks[k] if k < 2 else after(lat_chunks[k], resid_own[k - 2])
-        partials.append(jnp.dot(lat, weight, preferred_element_type=jnp.float32))
-        recons.append(reduce_rows(after(partials[k], *recons[2:k])))
-
     done = None
-    for first, last in groups:
-        rows = starts[last] - starts[first]
-        source = latents if done is None else after(latents, done)
-        sent = lax.dynamic_slice_in_dim(source, starts[first] + core * (rows // 2), rows // 2, 0)
+    for k in range(len(CHUNKS)):
+        rows = starts[k + 1] - starts[k]
+        source = latents if done is None else after(latents, done, partials[0])
+        sent = lax.dynamic_slice_in_dim(source, starts[k] + core * (rows // 2), rows // 2, 0)
         got = swap(sent, "dp")
         done = got
         if partials:
             got = after(got, partials[-1])
         twin = swap(got, "lyr")
         both = jnp.where(core == 0, jnp.stack([got, twin]), jnp.stack([twin, got]))
-        both = both.reshape(rows, feats)
-        for k in range(first, last):
-            inner = slice(starts[k] - starts[first], starts[k + 1] - starts[first])
-            lat_chunks.append(jnp.concatenate([latents[starts[k] : starts[k + 1]], both[inner]]))
-        if len(partials) < 2:
-            local_recon(first)
-        codes_here = after(codes, *partials[first : first + 1], done)
-        span = slice(starts[first], starts[last])
-        codes_got = swap(columns(codes_here[span], 1 - half, width), "dp")
-        for k in range(first, last):
-            inner = slice(starts[k] - starts[first], starts[k + 1] - starts[first])
-            codes_other.append(codes_got[inner])
+        other = both.reshape(rows, feats)
+        lat_chunks.append(jnp.concatenate([latents[starts[k] : starts[k + 1]], other]))
+        partials.append(jnp.dot(lat_chunks[k], weight, preferred_element_type=jnp.float32))
+        recons.append(reduce_rows(after(partials[k], *recons[: max(k - 1, 0)])))
+        codes_here = after(codes, partials[k], done)[starts[k] : starts[k + 1]]
+        codes_other.append(swap(columns(codes_here, 1 - half, width), "dp"))
 
     scales_here = after(scales, partials[0])
     weight_here = after(weight, partials[0])
@@ -264,29 +254,35 @@
     offset = (0.5 * penalty) * row_norms
     bias = lax.dynamic_slice_in_dim(dec_bias, half * width, width, 1)
 
-    inputs_chunks = []
-    for k in range(len(CHUNKS)):
+    def inputs_of(k):
         span = slice(starts[k], starts[k + 1])
-        code_rows = jnp.concatenate([columns(codes[span], half, width), codes_other[k]])
+        codes_got = codes_other[k] if k == 0 else after(codes_other[k], resid_own[k - 1])
+        code_rows = jnp.concatenate([columns(codes[span], half, width), codes_got])
         scale_rows = jnp.concatenate([scales_own[span], scales_other[span]])
         wide = jnp.dot(scale_rows, spread, preferred_element_type=jnp.float32)
-        inputs_chunks.append(code_rows.astype(jnp.float32) * wide)
+        return code_rows.astype(jnp.float32) * wide
+
     count = len(CHUNKS)
-    for k in range(count):
-        if len(partials) < min(k + 2, count):
-            local_recon(k + 1)
-        events = partials[k + 1 : k + 2]
-        if 2 <= k < count - 1:
-            events = events + [mines[k - 2]]
-        recon = after(recons[k], *events) if events else recons[k]
+    inputs_chunks = []
+
+    def local_resid(k, *events):
+        recon = after(recons[k], *partials[k + 1 :], *events)
         block = 2 * (starts[k + 1] - starts[k]) // n_lat
+        inputs_chunks.append(inputs_of(k))
         inputs = lax.dynamic_slice_in_dim(inputs_chunks[k], me * block, block, 0)
         resid_own.append((recon + bias - inputs).astype(jnp.bfloat16))
-        resid = gather_rows(resid_own[k], me)
-        resid_chunks.append(resid)
+        resid_chunks.append(gather_rows(resid_own[k], me))
+
+    local_resid(0, squares)
+    for k in range(count):
+        resid = resid_chunks[k]
         if k >= 1:
             resid = after(resid, mines[k - 1])
-        total, mine = reduce_plane(resid, weight, offset, core, column)
+        total, terms = reduce_pair(resid, weight, offset, core)
+        if k + 1 < count:
+            local_resid(k + 1, terms)
+            total = after(total, resid_own[k + 1])
+        mine = reduce_plane(total, core, column)
         if k >= 1:
             mine = after(mine, grad_chunks[k - 1])
         mines.append(mine)

time: 549 us -> 540 us (0.984)
  the two profiles are of different devices: /device:TPU:31 before, /device:TPU:0 now
where the time goes in v3:
time: 540 us; the launch traced here: 533 us
  waiting for transfers between devices  227 us (42%)
  matrix products  101 us (19%)
  Pallas kernels  57.6 us (11%)
  local copies, waits for them, and re-layouts  48.8 us (9%)
  other arithmetic  41.4 us (8%)
  starting transfers between devices  41.3 us (8%)
  between operations  14.9 us (3%)
    ppermute x9, waiting for transfers between devices, gather_rows(): got = lax.ppermute(block, 'lat', [(i, (i + shift) % n) for i in range(n)])  124 us
    ppermute x12, waiting for transfers between devices, swap_split(): return lax.ppermute(value, ('lyr', 'dp'), pairs)  75.1 us
    dot_general x3, matrix products, reduce_pair(): lax.dot_general(resid, weight, (((1,), (1,)), ((), ())), preferred_elemen...  40.6 us
    dot_general x3, matrix products, shards(): jnp.dot(lat_chunks[k], weight, preferred_element_type=jnp.float32)  33.4 us
    pallas_call x2, Pallas kernels, decoder_grad(): pl.pallas_call(functools.partial(dec_kernel, len(pieces)), grid=(tiles, w...  30.5 us
    ppermute x20, waiting for transfers between devices, swap(): return lax.ppermute(value, axis, [(i, i ^ bit) for i in range(size)])  27.9 us
    pallas_call x1, Pallas kernels, encoder_grad(): pl.pallas_call(functools.partial(enc_kernel, len(pieces)), grid=(feats //...  27.2 us
    ppermute x12, starting transfers between devices, swap_split(): return lax.ppermute(value, ('lyr', 'dp'), pairs)  16.5 us
  transfers between devices with their start and end apart: 44, of which 23 were waited for; matrix products, arithmetic and copies ran while one was open for 26% of the time, Pallas kernels for 6%

profile of v3, /device:TPU:0, one launch (start us, length us, event | category | flops | bytes accessed | tf_op | source)
XLA Modules:
  0.0 532.5 jit_solution(6902185398712932985)
XLA Ops:
  8.4 3.0 collective-permute-start
  12.9 3.6 fusion.56
  16.5 2.3 slice.77
  18.9 2.1 dynamic-slice_bitcast_fusion.4
  21.9 7.2 %collective-permute-done = bf16[96,4096]{1,0:T(8,128)(2,1)} collective-permute-done((bf16[96,4096]{1,0:T(8,128)(2,1)S(1)}, bf16[96,4096]{1,0:T(8,128)(2,1)}, u32[]{:S(2)}, u32[]{:S(2)}) %collective-permute-start) | collective-permute-done | bytes 786464 | tf_op jit(solution)/shard_map/ppermute | solution.py:22
  29.1 2.2 fusion.57
  31.6 1.8 maximum_select_fusion
  34.6 11.9 %fusion.51 = f32[384,2048]{1,0:T(8,128)} fusion(bf16[4096,1,2048]{2,0,1:T(8,128)(2,1)} %param.8, bf16[192,4096]{1,0:T(8,128)(2,1)S(1)} %bitcast.174, bf16[192,4096]{1,0:T(8,128)(2,1)S(1)} %get-tuple-element.85), kind=kOutput, calls=%fused_computation.147 | convolution fusion | flops 6448742400 | bytes 23068672 | tf_op jit(solution)/shard_map/dot_general | solution.py:242
  46.5 2.1 constant_dynamic-slice_fusion.11
  50.4 7.3 %multiply_reduce_fusion = f32[4096]{0:T(1024)S(1)} fusion(bf16[4096,2048]{1,0:T(8,128)(2,1)} %bitcast.158), kind=kLoop, calls=%fused_computation | loop fusion | flops 25161728 | bytes 16793600 | tf_op jit(solution)/shard_map/reduce_sum | solution.py:251
  60.4 1.9 collective-permute-start.2
  62.4 6.8 %collective-permute-done.4 = bf16[96,4096]{1,0:T(8,128)(2,1)} collective-permute-done((bf16[96,4096]{1,0:T(8,128)(2,1)}, bf16[96,4096]{1,0:T(8,128)(2,1)}, u32[]{:S(2)}, u32[]{:S(2)}) %collective-permute-start.4) | collective-permute-done | bytes 786464 | tf_op jit(solution)/shard_map/ppermute | solution.py:22
  70.1 1.9 constant_dynamic-slice_fusion.9
  71.9 1.7 collective-permute-start.7
  76.5 11.9 %fusion.49 = f32[384,2048]{1,0:T(8,128)} fusion(bf16[4096,1,2048]{2,0,1:T(8,128)(2,1)} %param.8, bf16[192,4096]{1,0:T(8,128)(2,1)S(1)} %bitcast.176, bf16[192,4096]{1,0:T(8,128)(2,1)S(1)} %get-tuple-element.84), kind=kOutput, calls=%fused_computation.145 | convolution fusion | flops 6448742400 | bytes 23068672 | tf_op jit(solution)/shard_map/dot_general | solution.py:242
  88.4 9.1 %collective-permute-done.7 = bf16[64,4096]{1,0:T(8,128)(2,1)S(1)} collective-permute-done((bf16[64,4096]{1,0:T(8,128)(2,1)}, bf16[64,4096]{1,0:T(8,128)(2,1)S(1)}, u32[]{:S(2)}, u32[]{:S(2)}) %collective-permute-start.7) | collective-permute-done | bytes 524320 | tf_op jit(solution)/shard_map/ppermute | solution.py:22
  97.7 4.3 fusion.62
  103.2 9.5 %fusion.47 = f32[256,2048]{1,0:T(8,128)} fusion(bf16[4096,1,2048]{2,0,1:T(8,128)(2,1)} %param.8, bf16[128,4096]{1,0:T(8,128)(2,1)S(1)} %bitcast.184, bf16[128,4096]{1,0:T(8,128)(2,1)S(1)} %slice.74), kind=kOutput, calls=%fused_computation.143 | convolution fusion | flops 4299161600 | bytes 20971520 | tf_op jit(solution)/shard_map/dot_general | solution.py:242
  112.9 2.3 bitcast_dynamic-update-slice_fusion.7
  115.2 1.8 collective-permute-start.11
  116.9 1.9 dynamic-slice_bitcast_fusion.5
  122.1 2.5 collective-permute-start.12
  125.4 4.0 collective-permute-done.11
  130.4 21.7 %collective-permute-done.12 = bf16[96,2048]{1,0:T(8,128)(2,1)S(1)} collective-permute-done((bf16[96,2048]{1,0:T(8,128)(2,1)}, bf16[96,2048]{1,0:T(8,128)(2,1)S(1)}, u32[]{:S(2)}, u32[]{:S(2)}) %collective-permute-start.12) | collective-permute-done | bytes 393248 | tf_op jit(solution)/shard_map/ppermute | solution.py:48
  152.1 44.2 %collective-permute-done.13 = bf16[96,2048]{1,0:T(8,128)(2,1)S(1)} collective-permute-done((bf16[96,2048]{1,0:T(8,128)(2,1)}, bf16[96,2048]{1,0:T(8,128)(2,1)S(1)}, u32[]{:S(2)}, u32[]{:S(2)}) %collective-permute-start.13) | collective-permute-done | bytes 393248 | tf_op jit(solution)/shard_map/ppermute | solution.py:48
  196.4 11.0 %convolution_add_fusion.1 = f32[384,4096]{1,0:T(8,128)S(1)} fusion(bf16[384,2048]{1,0:T(8,128)(2,1)S(1)} %bitcast.149, f32[4096]{0:T(1024)S(1)} %get-tuple-element.78, bf16[4096,1,2048]{2,0,1:T(8,128)(2,1)} %param.8), kind=kOutput, calls=%fused_computation.4 | convolution fusion | flops 6444023808 | bytes 24657920 | tf_op jit(solution)/shard_map/dot_general | solution.py:165
  207.4 1.9 dynamic-slice_bitcast_fusion.1
  209.3 2.8 copy-done.19
  213.1 3.2 pad_maximum_fusion
  220.6 4.3 fusion.61
  226.7 3.8 collective-permute-start.22
  230.5 2.0 collective-permute-done.10
  232.5 3.2 bitcast_add_fusion.1
  237.6 2.9 fusion.60
  240.4 3.5 convolution_convert_fusion.refs_3_
  245.9 3.6 convolution_convert_fusion.1.refs_2_
  249.5 7.0 %collective-permute-done.15 = f32[2,48,4096]{2,1,0:T(8,128)S(1)} collective-permute-done((f32[2,48,4096]{2,1,0:T(8,128)S(1)}, f32[2,48,4096]{2,1,0:T(8,128)S(1)}, u32[]{:S(2)}, u32[]{:S(2)}) %collective-permute-start.15) | collective-permute-done | bytes 1572896 | tf_op jit(solution)/shard_map/ppermute | solution.py:33
  258.1 6.3 %collective-permute-done.22 = bf16[96,2048]{1,0:T(8,128)(2,1)S(1)} collective-permute-done((bf16[96,2048]{1,0:T(8,128)(2,1)S(1)}, bf16[96,2048]{1,0:T(8,128)(2,1)S(1)}, u32[]{:S(2)}, u32[]{:S(2)}) %collective-permute-start.22) | collective-permute-done | bytes 393248 | tf_op jit(solution)/shard_map/ppermute | solution.py:48
  264.5 29.8 %collective-permute-done.23 = bf16[96,2048]{1,0:T(8,128)(2,1)S(1)} collective-permute-done((bf16[96,2048]{1,0:T(8,128)(2,1)S(1)}, bf16[96,2048]{1,0:T(8,128)(2,1)S(1)}, u32[]{:S(2)}, u32[]{:S(2)}) %collective-permute-start.23) | collective-permute-done | bytes 393248 | tf_op jit(solution)/shard_map/ppermute | solution.py:48
  294.4 2.2 constant_dynamic-update-slice_fusion.4
  296.6 10.3 %convolution_add_fusion = f32[384,4096]{1,0:T(8,128)S(1)} fusion(bf16[384,2048]{1,0:T(8,128)(2,1)S(1)} %bitcast.146, f32[4096]{0:T(1024)S(1)} %copy-done.39, bf16[4096,1,2048]{2,0,1:T(8,128)(2,1)} %param.8), kind=kOutput, calls=%fused_computation.3 | convolution fusion | flops 6444023808 | bytes 24657920 | tf_op jit(solution)/shard_map/dot_general | solution.py:165
  307.0 1.9 dynamic-slice_bitcast_fusion
  308.8 2.3 copy-done.20
  311.1 6.2 %fusion.6.refs_0_ = bf16[2048,1024]{1,0:T(8,128)(2,1)} fusion(bf16[256,2048]{1,0:T(8,128)(2,1)S(1)} %get-tuple-element.98, bf16[384,2048]{1,0:T(8,128)(2,1)S(1)} %copy-done.29, bf16[384,2048]{1,0:T(8,128)(2,1)S(1)} %copy-done.28, s32[1024]{0:T(1024)S(1)} %pad_add_fusion), kind=kOutput, calls=%fused_computation.16 | convolution fusion | flops 4310695936 | bytes 8392704 | tf_op jit(solution)/shard_map/dot_general | solution.py:158
  318.8 3.1 convert_reduce_fusion.1
  321.9 3.8 collective-permute-start.32
  329.8 5.2 collective-permute-done.32
  335.0 11.2 %collective-permute-done.33 = bf16[64,2048]{1,0:T(8,128)(2,1)S(1)} collective-permute-done((bf16[64,2048]{1,0:T(8,128)(2,1)S(1)}, bf16[64,2048]{1,0:T(8,128)(2,1)S(1)}, u32[]{:S(2)}, u32[]{:S(2)}) %collective-permute-start.33) | collective-permute-done | bytes 262176 | tf_op jit(solution)/shard_map/ppermute | solution.py:48
  346.2 3.3 bitcast_add_fusion
  352.0 26.6 %collective-permute-done.18 = bf16[2,48,4096]{2,1,0:T(8,128)(2,1)S(1)} collective-permute-done((bf16[2,48,4096]{2,1,0:T(8,128)(2,1)S(1)}, bf16[2,48,4096]{2,1,0:T(8,128)(2,1)S(1)}, u32[]{:S(2)}, u32[]{:S(2)}) %collective-permute-start.18) | collective-permute-done | bytes 786464 | tf_op jit(solution)/shard_map/ppermute | solution.py:33
  382.7 8.2 %collective-permute-done.26 = f32[48,4096]{1,0:T(8,128)S(1)} collective-permute-done((f32[48,4096]{1,0:T(8,128)S(1)}, f32[48,4096]{1,0:T(8,128)S(1)}, u32[]{:S(2)}, u32[]{:S(2)}) %collective-permute-start.26) | collective-permute-done | bytes 786464 | tf_op jit(solution)/shard_map/ppermute | solution.py:33
  391.0 19.3 %broadcast_add_fusion = f32[256,4096]{1,0:T(8,128)} fusion(f32[4096]{0:T(1024)S(1)} %copy-done.40, bf16[256,2048]{1,0:T(8,128)(2,1)S(1)} %bitcast.152, bf16[4096,1,2048]{2,0,1:T(8,128)(2,1)} %param.8), kind=kOutput, calls=%fused_computation.29 | convolution fusion | flops 4296015872 | bytes 22036480 | tf_op jit(solution)/shard_map/dot_general | solution.py:165
  410.3 3.2 dynamic-slice_bitcast_fusion.2
  413.5 2.0 constant_dynamic-update-slice_fusion.9
  419.0 2.5 convolution_convert_fusion.2.refs_4_
  421.5 2.0 collective-permute-done.27
  426.2 10.5 %collective-permute-done.28 = bf16[2,48,4096]{2,1,0:T(8,128)(2,1)S(1)} collective-permute-done((bf16[2,48,4096]{2,1,0:T(8,128)(2,1)S(1)}, bf16[2,48,4096]{2,1,0:T(8,128)(2,1)S(1)}, u32[]{:S(2)}, u32[]{:S(2)}) %collective-permute-start.28) | collective-permute-done | bytes 786464 | tf_op jit(solution)/shard_map/ppermute | solution.py:33
  436.7 1.9 bitcast_add_fusion.2
  440.4 13.1 %collective-permute-done.35 = f32[2,32,4096]{2,1,0:T(8,128)S(1)} collective-permute-done((f32[2,32,4096]{2,1,0:T(8,128)S(1)}, f32[2,32,4096]{2,1,0:T(8,128)S(1)}, u32[]{:S(2)}, u32[]{:S(2)}) %collective-permute-start.35) | collective-permute-done | bytes 1048608 | tf_op jit(solution)/shard_map/ppermute | solution.py:33
  455.2 15.2 %shard_map.77.refs_8_ = f32[4096,16,128]{2,1,0:T(8,128)} custom-call(f32[4096,1]{1,0:T(8,128)S(1)} %copy.12.refs_0_, bf16[4096,2048]{1,0:T(8,128)(2,1)} %bitcast.159, bf16[4096,384]{1,0:T(8,128)(2,1)} %convolution_convert_fusion.1.refs_2_, bf16[4096,384]{1,0:T(8,128)(2,1)} %convolution_convert_fusion.refs_3_, ...), custom_call_target="tpu_custom_call" | custom-call | flops 8589934592 | bytes 33554432 | tf_op jit(solution)/shard_map/pallas_call | solution.py:108
  472.1 15.2 %shard_map.78 = f32[4096,16,128]{2,1,0:T(8,128)} custom-call(f32[4096,1]{1,0:T(8,128)S(1)} %copy.12.refs_0_, bf16[4096,2048]{1,0:T(8,128)(2,1)} %bitcast.160, bf16[4096,384]{1,0:T(8,128)(2,1)} %convolution_convert_fusion.1.refs_2_, bf16[4096,384]{1,0:T(8,128)(2,1)} %convolution_convert_fusion.refs_3_, ...), custom_call_target="tpu_custom_call", output_to_operand_aliasing={{}: (8, {})} | custom-call | flops 8589934592 | bytes 33554432 | tf_op jit(solution)/shard_map/pallas_call | solution.py:108
  489.0 7.7 %collective-permute-done.38 = bf16[2,32,4096]{2,1,0:T(8,128)(2,1)S(1)} collective-permute-done((bf16[2,32,4096]{2,1,0:T(8,128)(2,1)S(1)}, bf16[2,32,4096]{2,1,0:T(8,128)(2,1)S(1)}, u32[]{:S(2)}, u32[]{:S(2)}) %collective-permute-start.38) | collective-permute-done | bytes 524320 | tf_op jit(solution)/shard_map/ppermute | solution.py:33
  496.8 1.8 collective-permute-done.40
  498.6 27.2 %shard_map.76 = (f32[2048,32,128]{2,1,0:T(8,128)}, f32[1,4096]{1,0:T(1,128)}) custom-call(bf16[2048,1024]{1,0:T(8,128)(2,1)} %fusion.6.refs_0_, bf16[384,4096]{1,0:T(8,128)(2,1)S(1)} %bitcast.156, bf16[384,4096]{1,0:T(8,128)(2,1)S(1)} %bitcast.155, bf16[256,4096]{1,0:T(8,128)(2,1)S(1)} %bitcast.157), custom_call_target="tpu_custom_call" | custom-call | flops 17179869184 | bytes 46137344 | tf_op jit(solution)/shard_map/pallas_call | solution.py:130
  (220 shorter events, 57.6 us)
Async XLA Ops:
  7.2 11.7 %copy-start = (f32[1,4096]{1,0:T(1,128)S(1)}, f32[1,4096]{1,0:T(1,128)}, u32[]{:S(2)}) copy-start(f32[1,4096]{1,0:T(1,128)} %param.9) | copy-start | bytes 49156
  7.2 105.5 %reduce-scatter.4.cloned.1.call-start = ((), (), s32[]{:S(2)}) async-start(), calls=%async_computation.3 | async-start | bytes 3932160 | tf_op jit(solution)/shard_map/reduce_scatter | solution.py:37
  8.4 20.7 %collective-permute-start = (bf16[96,4096]{1,0:T(8,128)(2,1)S(1)}, bf16[96,4096]{1,0:T(8,128)(2,1)}, u32[]{:S(2)}, u32[]{:S(2)}) collective-permute-start(bf16[96,4096]{1,0:T(8,128)(2,1)S(1)} %constant_dynamic-slice_fusion.14), channel_id=1, source_target_pairs={{0,1},{1,0},{2,3},{3,2},{4,5},{5,4},{6,7},{7,6},{8,9},{9,8},{10,11... | collective-permute-start | bytes 2359304 | tf_op jit(solution)/shard_map/ppermute | solution.py:22
  12.8 89.4 %copy-start.24 = (bf16[128,4096]{1,0:T(8,128)(2,1)}, bf16[128,4096]{1,0:T(8,128)(2,1)S(1)}, u32[]{:S(2)}) copy-start(bf16[128,4096]{1,0:T(8,128)(2,1)S(1)} %slice.74) | copy-start | bytes 3145732
  18.9 206.3 %copy-start.30 = (f32[1,2048]{1,0:T(1,128)}, f32[1,2048]{1,0:T(1,128)S(1)}, u32[]{:S(2)}) copy-start(f32[1,2048]{1,0:T(1,128)S(1)} %constant_dynamic-slice_fusion.8) | copy-start | bytes 24580
  29.1 2.5 collective-permute-start.1
  48.6 20.6 %collective-permute-start.4 = (bf16[96,4096]{1,0:T(8,128)(2,1)}, bf16[96,4096]{1,0:T(8,128)(2,1)}, u32[]{:S(2)}, u32[]{:S(2)}) collective-permute-start(bf16[96,4096]{1,0:T(8,128)(2,1)} %constant_dynamic-slice_fusion.11), channel_id=1, source_target_pairs={{0,1},{1,0},{2,3},{3,2},{4,5},{5,4},{6,7},{7,6},{8,9},{9,8},{10,11... | collective-permute-start | bytes 2359304 | tf_op jit(solution)/shard_map/ppermute | solution.py:22
  50.3 174.6 %reduce-scatter.6.cloned.1.call-start = ((), (), s32[]{:S(2)}) async-start(), calls=%async_computation.4 | async-start | bytes 3932160 | tf_op jit(solution)/shard_map/reduce_scatter | solution.py:37
  57.7 11.7 %collective-permute-start.9 = (f32[4096]{0:T(1024)S(1)}, f32[4096]{0:T(1024)S(1)}, u32[]{:S(2)}, u32[]{:S(2)}) collective-permute-start(f32[4096]{0:T(1024)S(1)} %multiply_reduce_fusion), channel_id=1, source_target_pairs={{0,1},{1,0},{2,3},{3,2},{4,5},{5,4},{6,7},{7,6},{8,9},{9,8},{10,11... | collective-permute-start | bytes 49160 | tf_op jit(solution)/shard_map/ppermute | solution.py:22
  60.4 37.2 %collective-permute-start.2 = (bf16[192,2048]{1,0:T(8,128)(2,1)}, bf16[192,2048]{1,0:T(8,128)(2,1)}, u32[]{:S(2)}, u32[]{:S(2)}) collective-permute-start(bf16[192,2048]{1,0:T(8,128)(2,1)} %constant_dynamic-slice_fusion.13), channel_id=1, source_target_pairs={{0,1},{1,0},{2,3},{3,2},{4,5},{5,4},{6,7},{7,6},{8,9},{9,8},{10,11... | collective-permute-start | bytes 2359304 | tf_op jit(solution)/shard_map/ppermute | solution.py:22
  62.3 35.3 %collective-permute-start.3 = (bf16[512,16]{0,1:T(8,128)(2,1)S(1)}, bf16[512,16]{0,1:T(8,128)(2,1)S(1)}, u32[]{:S(2)}, u32[]{:S(2)}) collective-permute-start(bf16[512,16]{0,1:T(8,128)(2,1)S(1)} %constant_dynamic-slice_fusion.12), channel_id=1, source_target_pairs={{0,1},{1,0},{2,3},{3,2},{4,5},{5,4},{6,7},{7,6},{8,9},{9,8},{10,11... | collective-permute-start | bytes 49160 | tf_op jit(solution)/shard_map/ppermute | solution.py:22
  69.2 4.5 collective-permute-start.5
  70.1 126.3 %copy-start.38 = (f32[4096]{0:T(1024)}, f32[4096]{0:T(1024)S(1)}, u32[]{:S(2)}) copy-start(f32[4096]{0:T(1024)S(1)} %get-tuple-element.78) | copy-start | bytes 49156
  71.9 25.6 %collective-permute-start.7 = (bf16[64,4096]{1,0:T(8,128)(2,1)}, bf16[64,4096]{1,0:T(8,128)(2,1)S(1)}, u32[]{:S(2)}, u32[]{:S(2)}) collective-permute-start(bf16[64,4096]{1,0:T(8,128)(2,1)} %constant_dynamic-slice_fusion.9), channel_id=1, source_target_pairs={{0,1},{1,0},{2,3},{3,2},{4,5},{5,4},{6,7},{7,6},{8,9},{9,8},{10,11... | collective-permute-start | bytes 1572872 | tf_op jit(solution)/shard_map/ppermute | solution.py:22
  97.5 4.5 collective-permute-start.8
  97.6 21.3 %copy-start.37 = (bf16[512,16]{0,1:T(8,128)(2,1)}, bf16[512,16]{0,1:T(8,128)(2,1)S(1)}, u32[]{:S(2)}) copy-start(bf16[512,16]{0,1:T(8,128)(2,1)S(1)} %collective-permute-done.3) | copy-start | bytes 49156
  115.2 14.2 %collective-permute-start.11 = (bf16[96,2048]{1,0:T(8,128)(2,1)}, bf16[96,2048]{1,0:T(8,128)(2,1)}, u32[]{:S(2)}, u32[]{:S(2)}) collective-permute-start(bf16[96,2048]{1,0:T(8,128)(2,1)} %get-tuple-element.81), channel_id=1, source_target_pairs={{0,8},{8,16},{16,24},{24,0},{1,9},{9,17},{17,25},{25,1},{2,10},{10... | collective-permute-start | bytes 1179656 | tf_op jit(solution)/shard_map/ppermute | solution.py:48
  118.8 198.5 %reduce-scatter.8.cloned.1.call-start = ((), (), s32[]{:S(2)}) async-start(), calls=%async_computation.5 | async-start | bytes 2621440 | tf_op jit(solution)/shard_map/reduce_scatter | solution.py:37
  120.5 99.7 %collective-permute-start.6 = (bf16[192,2048]{1,0:T(8,128)(2,1)S(1)}, bf16[192,2048]{1,0:T(8,128)(2,1)}, u32[]{:S(2)}, u32[]{:S(2)}) collective-permute-start(bf16[192,2048]{1,0:T(8,128)(2,1)S(1)} %constant_dynamic-slice_fusion.10), channel_id=1, source_target_pairs={{0,1},{1,0},{2,3},{3,2},{4,5},{5,4},{6,7},{7,6},{8,9},{9,8},{10,11... | collective-permute-start | bytes 2359304 | tf_op jit(solution)/shard_map/ppermute | solution.py:22
  122.1 30.0 %collective-permute-start.12 = (bf16[96,2048]{1,0:T(8,128)(2,1)}, bf16[96,2048]{1,0:T(8,128)(2,1)S(1)}, u32[]{:S(2)}, u32[]{:S(2)}) collective-permute-start(bf16[96,2048]{1,0:T(8,128)(2,1)} %get-tuple-element.81), channel_id=1, source_target_pairs={{0,24},{8,0},{16,8},{24,16},{1,25},{9,1},{17,9},{25,17},{2,26},{10... | collective-permute-start | bytes 1179656 | tf_op jit(solution)/shard_map/ppermute | solution.py:48
  124.6 71.8 %collective-permute-start.13 = (bf16[96,2048]{1,0:T(8,128)(2,1)}, bf16[96,2048]{1,0:T(8,128)(2,1)S(1)}, u32[]{:S(2)}, u32[]{:S(2)}) collective-permute-start(bf16[96,2048]{1,0:T(8,128)(2,1)} %get-tuple-element.81), channel_id=1, source_target_pairs={{0,16},{8,24},{16,0},{24,8},{1,17},{9,25},{17,1},{25,9},{2,18},{10... | collective-permute-start | bytes 1179656 | tf_op jit(solution)/shard_map/ppermute | solution.py:48
  196.4 11.0 %copy-start.4 = (bf16[4,96,2048]{2,1,0:T(8,128)(2,1)}, bf16[4,96,2048]{2,1,0:T(8,128)(2,1)S(1)}, u32[]{:S(2)}) copy-start(bf16[4,96,2048]{2,1,0:T(8,128)(2,1)S(1)} %bitcast_dynamic-update-slice_fusion.4) | copy-start | bytes 4718596
  212.1 20.4 %collective-permute-start.14 = (f32[2,2,48,4096]{3,2,1,0:T(8,128)}, f32[2,2,48,4096]{3,2,1,0:T(8,128)}, u32[]{:S(2)}, u32[]{:S(2)}) collective-permute-start(f32[2,2,48,4096]{3,2,1,0:T(8,128)} %dynamic-slice_bitcast_fusion.1), channel_id=1, source_target_pairs={{0,2},{2,0},{4,6},{6,4},{1,3},{3,1},{5,7},{7,5},{8,10},{10,8},{12,... | collective-permute-start | bytes 9437192 | tf_op jit(solution)/shard_map/ppermute | solution.py:22
  218.5 14.0 %collective-permute-start.10 = (bf16[128,2048]{1,0:T(8,128)(2,1)}, bf16[128,2048]{1,0:T(8,128)(2,1)}, u32[]{:S(2)}, u32[]{:S(2)}) collective-permute-start(bf16[128,2048]{1,0:T(8,128)(2,1)} %constant_dynamic-slice_fusion.7), channel_id=1, source_target_pairs={{0,1},{1,0},{2,3},{3,2},{4,5},{5,4},{6,7},{7,6},{8,9},{9,8},{10,11... | collective-permute-start | bytes 1572872 | tf_op jit(solution)/shard_map/ppermute | solution.py:22
  220.2 107.0 %copy-start.10 = (bf16[256,4096]{1,0:T(8,128)(2,1)}, bf16[256,4096]{1,0:T(8,128)(2,1)S(1)}, u32[]{:S(2)}) copy-start(bf16[256,4096]{1,0:T(8,128)(2,1)S(1)} %pad_maximum_fusion.2) | copy-start | bytes 6291460
  226.6 22.8 %collective-permute-start.21 = (bf16[96,2048]{1,0:T(8,128)(2,1)S(1)}, bf16[96,2048]{1,0:T(8,128)(2,1)S(1)}, u32[]{:S(2)}, u32[]{:S(2)}) collective-permute-start(bf16[96,2048]{1,0:T(8,128)(2,1)S(1)} %get-tuple-element.74), channel_id=1, source_target_pairs={{0,8},{8,16},{16,24},{24,0},{1,9},{9,17},{17,25},{25,1},{2,10},{10... | collective-permute-start | bytes 1179656 | tf_op jit(solution)/shard_map/ppermute | solution.py:48
  226.7 37.7 %collective-permute-start.22 = (bf16[96,2048]{1,0:T(8,128)(2,1)S(1)}, bf16[96,2048]{1,0:T(8,128)(2,1)S(1)}, u32[]{:S(2)}, u32[]{:S(2)}) collective-permute-start(bf16[96,2048]{1,0:T(8,128)(2,1)S(1)} %get-tuple-element.74), channel_id=1, source_target_pairs={{0,24},{8,0},{16,8},{24,16},{1,25},{9,1},{17,9},{25,17},{2,26},{10... | collective-permute-start | bytes 1179656 | tf_op jit(solution)/shard_map/ppermute | solution.py:48
  230.5 63.8 %collective-permute-start.23 = (bf16[96,2048]{1,0:T(8,128)(2,1)S(1)}, bf16[96,2048]{1,0:T(8,128)(2,1)S(1)}, u32[]{:S(2)}, u32[]{:S(2)}) collective-permute-start(bf16[96,2048]{1,0:T(8,128)(2,1)S(1)} %get-tuple-element.74), channel_id=1, source_target_pairs={{0,16},{8,24},{16,0},{24,8},{1,17},{9,25},{17,1},{25,9},{2,18},{10... | collective-permute-start | bytes 1179656 | tf_op jit(solution)/shard_map/ppermute | solution.py:48
  236.0 20.5 %collective-permute-start.15 = (f32[2,48,4096]{2,1,0:T(8,128)S(1)}, f32[2,48,4096]{2,1,0:T(8,128)S(1)}, u32[]{:S(2)}, u32[]{:S(2)}) collective-permute-start(f32[2,48,4096]{2,1,0:T(8,128)S(1)} %pad_maximum_fusion.3), channel_id=1, source_target_pairs={{0,4},{1,5},{2,3},{3,2},{4,0},{5,1},{6,7},{7,6},{8,12},{9,13},{10,... | collective-permute-start | bytes 4718600 | tf_op jit(solution)/shard_map/ppermute | solution.py:33
  256.6 40.0 %copy-start.39 = (f32[4096]{0:T(1024)S(1)}, f32[4096]{0:T(1024)}, u32[]{:S(2)}) copy-start(f32[4096]{0:T(1024)} %copy-done.38) | copy-start | bytes 49156
  256.6 37.8 %collective-permute-start.16 = (f32[48,4096]{1,0:T(8,128)S(1)}, f32[48,4096]{1,0:T(8,128)S(1)}, u32[]{:S(2)}, u32[]{:S(2)}) collective-permute-start(f32[48,4096]{1,0:T(8,128)S(1)} %fusion.13), channel_id=1, source_target_pairs={{0,1},{1,0},{2,6},{3,7},{4,5},{5,4},{6,2},{7,3},{8,9},{9,8},{10,14... | collective-permute-start | bytes 2359304 | tf_op jit(solution)/shard_map/ppermute | solution.py:33
  294.3 12.6 %copy-start.2 = (bf16[4,96,2048]{2,1,0:T(8,128)(2,1)}, bf16[4,96,2048]{2,1,0:T(8,128)(2,1)S(1)}, u32[]{:S(2)}) copy-start(bf16[4,96,2048]{2,1,0:T(8,128)(2,1)S(1)} %bitcast_dynamic-update-slice_fusion) | copy-start | bytes 4718596
  311.1 35.1 %collective-permute-start.24 = (f32[2,2,48,4096]{3,2,1,0:T(8,128)}, f32[2,2,48,4096]{3,2,1,0:T(8,128)}, u32[]{:S(2)}, u32[]{:S(2)}) collective-permute-start(f32[2,2,48,4096]{3,2,1,0:T(8,128)} %dynamic-slice_bitcast_fusion), channel_id=1, source_target_pairs={{0,2},{2,0},{4,6},{6,4},{1,3},{3,1},{5,7},{7,5},{8,10},{10,8},{12,... | collective-permute-start | bytes 9437192 | tf_op jit(solution)/shard_map/ppermute | solution.py:22
  318.8 11.0 %collective-permute-start.31 = (bf16[64,2048]{1,0:T(8,128)(2,1)S(1)}, bf16[64,2048]{1,0:T(8,128)(2,1)S(1)}, u32[]{:S(2)}, u32[]{:S(2)}) collective-permute-start(bf16[64,2048]{1,0:T(8,128)(2,1)S(1)} %get-tuple-element.70), channel_id=1, source_target_pairs={{0,8},{8,16},{16,24},{24,0},{1,9},{9,17},{17,25},{25,1},{2,10},{10... | collective-permute-start | bytes 786440 | tf_op jit(solution)/shard_map/ppermute | solution.py:48
  321.9 13.1 %collective-permute-start.32 = (bf16[64,2048]{1,0:T(8,128)(2,1)S(1)}, bf16[64,2048]{1,0:T(8,128)(2,1)S(1)}, u32[]{:S(2)}, u32[]{:S(2)}) collective-permute-start(bf16[64,2048]{1,0:T(8,128)(2,1)S(1)} %get-tuple-element.70), channel_id=1, source_target_pairs={{0,24},{8,0},{16,8},{24,16},{1,25},{9,1},{17,9},{25,17},{2,26},{10... | collective-permute-start | bytes 786440 | tf_op jit(solution)/shard_map/ppermute | solution.py:48
  325.7 20.5 %collective-permute-start.33 = (bf16[64,2048]{1,0:T(8,128)(2,1)S(1)}, bf16[64,2048]{1,0:T(8,128)(2,1)S(1)}, u32[]{:S(2)}, u32[]{:S(2)}) collective-permute-start(bf16[64,2048]{1,0:T(8,128)(2,1)S(1)} %get-tuple-element.70), channel_id=1, source_target_pairs={{0,16},{8,24},{16,0},{24,8},{1,17},{9,25},{17,1},{25,9},{2,18},{10... | collective-permute-start | bytes 786440 | tf_op jit(solution)/shard_map/ppermute | solution.py:48
  325.7 25.6 %collective-permute-start.17 = (bf16[48,4096]{1,0:T(8,128)(2,1)S(1)}, bf16[48,4096]{1,0:T(8,128)(2,1)S(1)}, u32[]{:S(2)}, u32[]{:S(2)}) collective-permute-start(bf16[48,4096]{1,0:T(8,128)(2,1)S(1)} %get-tuple-element.76), channel_id=1, source_target_pairs={{0,1},{1,0},{2,6},{3,7},{4,5},{5,4},{6,2},{7,3},{8,9},{9,8},{10,14... | collective-permute-start | bytes 1179656 | tf_op jit(solution)/shard_map/ppermute | solution.py:33
  349.8 29.0 %collective-permute-start.25 = (f32[2,48,4096]{2,1,0:T(8,128)S(1)}, f32[2,48,4096]{2,1,0:T(8,128)S(1)}, u32[]{:S(2)}, u32[]{:S(2)}) collective-permute-start(f32[2,48,4096]{2,1,0:T(8,128)S(1)} %pad_maximum_fusion.4), channel_id=1, source_target_pairs={{0,4},{1,5},{2,3},{3,2},{4,0},{5,1},{6,7},{7,6},{8,12},{9,13},{10,... | collective-permute-start | bytes 4718600 | tf_op jit(solution)/shard_map/ppermute | solution.py:33
  351.4 27.3 %collective-permute-start.18 = (bf16[2,48,4096]{2,1,0:T(8,128)(2,1)S(1)}, bf16[2,48,4096]{2,1,0:T(8,128)(2,1)S(1)}, u32[]{:S(2)}, u32[]{:S(2)}) collective-permute-start(bf16[2,48,4096]{2,1,0:T(8,128)(2,1)S(1)} %pad_maximum_fusion.6), channel_id=1, source_target_pairs={{0,4},{1,5},{2,3},{3,2},{4,0},{5,1},{6,7},{7,6},{8,12},{9,13},{10,... | collective-permute-start | bytes 2359304 | tf_op jit(solution)/shard_map/ppermute | solution.py:33
  352.0 28.4 %collective-permute-start.19 = (bf16[2,48,4096]{2,1,0:T(8,128)(2,1)S(1)}, bf16[2,48,4096]{2,1,0:T(8,128)(2,1)S(1)}, u32[]{:S(2)}, u32[]{:S(2)}) collective-permute-start(bf16[2,48,4096]{2,1,0:T(8,128)(2,1)S(1)} %pad_maximum_fusion.6), channel_id=1, source_target_pairs={{0,2},{2,0},{4,6},{6,4},{1,3},{3,1},{5,7},{7,5},{8,10},{10,8},{12,... | collective-permute-start | bytes 2359304 | tf_op jit(solution)/shard_map/ppermute | solution.py:22
  378.7 2.3 collective-permute-start.20
  378.8 12.2 %copy-start.40 = (f32[4096]{0:T(1024)S(1)}, f32[4096]{0:T(1024)}, u32[]{:S(2)}) copy-start(f32[4096]{0:T(1024)} %copy-done.38) | copy-start | bytes 49156
  378.8 12.1 %collective-permute-start.26 = (f32[48,4096]{1,0:T(8,128)S(1)}, f32[48,4096]{1,0:T(8,128)S(1)}, u32[]{:S(2)}, u32[]{:S(2)}) collective-permute-start(f32[48,4096]{1,0:T(8,128)S(1)} %fusion.10), channel_id=1, source_target_pairs={{0,1},{1,0},{2,6},{3,7},{4,5},{5,4},{6,2},{7,3},{8,9},{9,8},{10,14... | collective-permute-start | bytes 2359304 | tf_op jit(solution)/shard_map/ppermute | solution.py:33
  410.3 6.7 %copy-start.32 = (f32[4096]{0:T(1024)S(1)}, f32[4096]{0:T(1024)}, u32[]{:S(2)}) copy-start(f32[4096]{0:T(1024)} %convert_reduce_fusion) | copy-start | bytes 49156
  410.3 6.7 %copy-start.33 = (f32[4096]{0:T(1024)S(1)}, f32[4096]{0:T(1024)}, u32[]{:S(2)}) copy-start(f32[4096]{0:T(1024)} %convert_reduce_fusion.1) | copy-start | bytes 49156
  410.3 6.7 %copy-start.34 = (f32[4096]{0:T(1024)S(1)}, f32[4096]{0:T(1024)}, u32[]{:S(2)}) copy-start(f32[4096]{0:T(1024)} %convert_reduce_fusion.2) | copy-start | bytes 49156
  410.3 6.7 %copy-start.35 = (f32[4096]{0:T(1024)S(1)}, f32[4096]{0:T(1024)}, u32[]{:S(2)}) copy-start(f32[4096]{0:T(1024)} %get-tuple-element.79) | copy-start | bytes 49156
  413.5 23.1 %collective-permute-start.34 = (f32[2,2,32,4096]{3,2,1,0:T(8,128)}, f32[2,2,32,4096]{3,2,1,0:T(8,128)}, u32[]{:S(2)}, u32[]{:S(2)}) collective-permute-start(f32[2,2,32,4096]{3,2,1,0:T(8,128)} %dynamic-slice_bitcast_fusion.2), channel_id=1, source_target_pairs={{0,2},{2,0},{4,6},{6,4},{1,3},{3,1},{5,7},{7,5},{8,10},{10,8},{12,... | collective-permute-start | bytes 6291464 | tf_op jit(solution)/shard_map/ppermute | solution.py:22
  415.5 8.0 %collective-permute-start.27 = (bf16[48,4096]{1,0:T(8,128)(2,1)}, bf16[48,4096]{1,0:T(8,128)(2,1)S(1)}, u32[]{:S(2)}, u32[]{:S(2)}) collective-permute-start(bf16[48,4096]{1,0:T(8,128)(2,1)} %get-tuple-element.72), channel_id=1, source_target_pairs={{0,1},{1,0},{2,6},{3,7},{4,5},{5,4},{6,2},{7,3},{8,9},{9,8},{10,14... | collective-permute-start | bytes 1179656 | tf_op jit(solution)/shard_map/ppermute | solution.py:33
  419.0 7.1 %copy-start.6 = (bf16[8,48,4096]{2,1,0:T(8,128)(2,1)S(1)}, bf16[8,48,4096]{2,1,0:T(8,128)(2,1)}, u32[]{:S(2)}) copy-start(bf16[8,48,4096]{2,1,0:T(8,128)(2,1)} %get-tuple-element.71) | copy-start | bytes 9437188
  419.0 17.6 %copy-start.21 = (f32[256,4096]{1,0:T(8,128)S(1)}, f32[256,4096]{1,0:T(8,128)}, u32[]{:S(2)}) copy-start(f32[256,4096]{1,0:T(8,128)} %broadcast_add_fusion) | copy-start | bytes 12582916
  424.6 12.1 %collective-permute-start.28 = (bf16[2,48,4096]{2,1,0:T(8,128)(2,1)S(1)}, bf16[2,48,4096]{2,1,0:T(8,128)(2,1)S(1)}, u32[]{:S(2)}, u32[]{:S(2)}) collective-permute-start(bf16[2,48,4096]{2,1,0:T(8,128)(2,1)S(1)} %pad_maximum_fusion.7), channel_id=1, source_target_pairs={{0,4},{1,5},{2,3},{3,2},{4,0},{5,1},{6,7},{7,6},{8,12},{9,13},{10,... | collective-permute-start | bytes 2359304 | tf_op jit(solution)/shard_map/ppermute | solution.py:33
  426.1 14.2 %collective-permute-start.29 = (bf16[2,48,4096]{2,1,0:T(8,128)(2,1)S(1)}, bf16[2,48,4096]{2,1,0:T(8,128)(2,1)S(1)}, u32[]{:S(2)}, u32[]{:S(2)}) collective-permute-start(bf16[2,48,4096]{2,1,0:T(8,128)(2,1)S(1)} %pad_maximum_fusion.7), channel_id=1, source_target_pairs={{0,2},{2,0},{4,6},{6,4},{1,3},{3,1},{5,7},{7,5},{8,10},{10,8},{12,... | collective-permute-start | bytes 2359304 | tf_op jit(solution)/shard_map/ppermute | solution.py:22
  436.6 3.7 collective-permute-start.30
  438.7 16.5 %copy-start.3 = (bf16[4,96,2048]{2,1,0:T(8,128)(2,1)S(1)}, bf16[4,96,2048]{2,1,0:T(8,128)(2,1)}, u32[]{:S(2)}) copy-start(bf16[4,96,2048]{2,1,0:T(8,128)(2,1)} %copy-done.2) | copy-start | bytes 4718596
  438.7 16.5 %copy-start.5 = (bf16[4,96,2048]{2,1,0:T(8,128)(2,1)S(1)}, bf16[4,96,2048]{2,1,0:T(8,128)(2,1)}, u32[]{:S(2)}) copy-start(bf16[4,96,2048]{2,1,0:T(8,128)(2,1)} %copy-done.4) | copy-start | bytes 4718596
  438.7 14.9 %collective-permute-start.35 = (f32[2,32,4096]{2,1,0:T(8,128)S(1)}, f32[2,32,4096]{2,1,0:T(8,128)S(1)}, u32[]{:S(2)}, u32[]{:S(2)}) collective-permute-start(f32[2,32,4096]{2,1,0:T(8,128)S(1)} %pad_maximum_fusion.5), channel_id=1, source_target_pairs={{0,4},{1,5},{2,3},{3,2},{4,0},{5,1},{6,7},{7,6},{8,12},{9,13},{10,... | collective-permute-start | bytes 3145736 | tf_op jit(solution)/shard_map/ppermute | solution.py:33
  453.6 16.8 %collective-permute-start.36 = (f32[32,4096]{1,0:T(8,128)S(1)}, f32[32,4096]{1,0:T(8,128)S(1)}, u32[]{:S(2)}, u32[]{:S(2)}) collective-permute-start(f32[32,4096]{1,0:T(8,128)S(1)} %fusion.16), channel_id=1, source_target_pairs={{0,1},{1,0},{2,6},{3,7},{4,5},{5,4},{6,2},{7,3},{8,9},{9,8},{10,14... | collective-permute-start | bytes 1572872 | tf_op jit(solution)/shard_map/ppermute | solution.py:33
  471.5 15.8 %collective-permute-start.37 = (bf16[32,4096]{1,0:T(8,128)(2,1)S(1)}, bf16[32,4096]{1,0:T(8,128)(2,1)S(1)}, u32[]{:S(2)}, u32[]{:S(2)}) collective-permute-start(bf16[32,4096]{1,0:T(8,128)(2,1)S(1)} %get-tuple-element.68), channel_id=1, source_target_pairs={{0,1},{1,0},{2,6},{3,7},{4,5},{5,4},{6,2},{7,3},{8,9},{9,8},{10,14... | collective-permute-start | bytes 786440 | tf_op jit(solution)/shard_map/ppermute | solution.py:33
  487.4 11.3 %copy-start.9 = (bf16[8,48,4096]{2,1,0:T(8,128)(2,1)S(1)}, bf16[8,48,4096]{2,1,0:T(8,128)(2,1)}, u32[]{:S(2)}) copy-start(bf16[8,48,4096]{2,1,0:T(8,128)(2,1)} %copy-done.8) | copy-start | bytes 9437188
  487.4 9.2 %collective-permute-start.38 = (bf16[2,32,4096]{2,1,0:T(8,128)(2,1)S(1)}, bf16[2,32,4096]{2,1,0:T(8,128)(2,1)S(1)}, u32[]{:S(2)}, u32[]{:S(2)}) collective-permute-start(bf16[2,32,4096]{2,1,0:T(8,128)(2,1)S(1)} %pad_maximum_fusion.8), channel_id=1, source_target_pairs={{0,4},{1,5},{2,3},{3,2},{4,0},{5,1},{6,7},{7,6},{8,12},{9,13},{10,... | collective-permute-start | bytes 1572872 | tf_op jit(solution)/shard_map/ppermute | solution.py:33
  488.9 7.8 %collective-permute-start.39 = (bf16[2,32,4096]{2,1,0:T(8,128)(2,1)S(1)}, bf16[2,32,4096]{2,1,0:T(8,128)(2,1)S(1)}, u32[]{:S(2)}, u32[]{:S(2)}) collective-permute-start(bf16[2,32,4096]{2,1,0:T(8,128)(2,1)S(1)} %pad_maximum_fusion.8), channel_id=1, source_target_pairs={{0,2},{2,0},{4,6},{6,4},{1,3},{3,1},{5,7},{7,5},{8,10},{10,8},{12,... | collective-permute-start | bytes 1572872 | tf_op jit(solution)/shard_map/ppermute | solution.py:22
  496.7 1.9 collective-permute-start.40
  498.6 27.2 %copy-start.1 = (f32[1,4096]{1,0:T(1,128)S(1)}, f32[1,4096]{1,0:T(1,128)}, u32[]{:S(2)}) copy-start(f32[1,4096]{1,0:T(1,128)} %param.9) | copy-start | bytes 49156
  (22 other events, 72.6 us)
Sparse Core Ops, SparseCore 0:
  50.4 60.5 reduce-scatter.3
  118.9 82.9 reduce-scatter.5
  220.7 66.0 reduce-scatter.7

commit v4 on v3

--- a/solution.py
+++ b/solution.py
@@ -37,17 +37,8 @@
     return lax.psum_scatter(partial, "lat", scatter_dimension=0, tiled=True)
 
 
-def gather_rows(block, me):
-    n = lax.axis_size("lat")
-    rows, width = block.shape
-    if n > 4:
-        return lax.all_gather(block, "lat", axis=0, tiled=True)
-    out = jnp.zeros((n, rows, width), block.dtype)
-    out = lax.dynamic_update_index_in_dim(out, block, me, 0)
-    for shift in sorted(range(1, n), key=lambda i: min(i, n - i)):
-        got = lax.ppermute(block, "lat", [(i, (i + shift) % n) for i in range(n)])
-        out = lax.dynamic_update_index_in_dim(out, got, lax.rem(me - shift + n, n), 0)
-    return out.reshape(n * rows, width)
+def gather_rows(block):
+    return lax.all_gather(block, "lat", axis=0, tiled=True)
 
 
 def store_rows(out_ref, value):
@@ -190,7 +181,7 @@
     got = swap_split(pair, False)
     twin_got = swap(got, "lyr")
     rows = jnp.concatenate([pair, got, twin_pair, twin_got])
-    return rows.reshape(-1, mine.shape[1]), pair
+    return rows.reshape(-1, mine.shape[1])
 
 
 def plane_rows(core, column):
@@ -271,26 +262,27 @@
         inputs_chunks.append(inputs_of(k))
         inputs = lax.dynamic_slice_in_dim(inputs_chunks[k], me * block, block, 0)
         resid_own.append((recon + bias - inputs).astype(jnp.bfloat16))
-        resid_chunks.append(gather_rows(resid_own[k], me))
+        resid_chunks.append(gather_rows(resid_own[k]))
 
     local_resid(0, squares)
-    for k in range(count):
-        resid = resid_chunks[k]
-        if k >= 1:
-            resid = after(resid, mines[k - 1])
-        total, terms = reduce_pair(resid, weight, offset, core)
-        if k + 1 < count:
-            local_resid(k + 1, terms)
-            total = after(total, resid_own[k + 1])
+    def finish(k, total):
         mine = reduce_plane(total, core, column)
-        if k >= 1:
-            mine = after(mine, grad_chunks[k - 1])
         mines.append(mine)
         sub = (starts[k + 1] - starts[k]) // 4
         lat_mine = lax.dynamic_slice_in_dim(latents, starts[k] + layer * sub, sub, 0)
         grad_pre = jnp.where(lat_mine > 0, mine, 0.0).astype(jnp.bfloat16)
-        grad_rows, pair = gather_plane(grad_pre)
-        grad_chunks.append(grad_rows)
+        grad_chunks.append(gather_plane(grad_pre))
+
+    waiting = None
+    for k in range(count):
+        total, terms = reduce_pair(resid_chunks[k], weight, offset, core)
+        if waiting is not None:
+            finish(k - 1, after(waiting, terms if k < count - 1 else resid_own[k]))
+        waiting = total
+        if k + 1 < count:
+            local_resid(k + 1, terms, *mines[k - 1 : k])
+    finish(count - 1, total)
+    mine = mines[-1]
 
     inputs_bf = jnp.concatenate([x.astype(jnp.bfloat16) for x in inputs_chunks])
     order = after(plane_rows(core, column), resid_own[0])

time: 540 us -> 488 us (0.904)
  waiting for transfers between devices: 227 us -> 185 us
  starting transfers between devices: 41.3 us -> 28.5 us
    ppermute x9 -> x0, waiting for transfers between devices: 124 us -> none  [gather_rows(): got = lax.ppermute(block, 'lat', [(i, (i + shift) % n) for i in range(n)])]
    reduce_scatter x3, waiting for transfers between devices: 0.02 us -> 46.2 us  [reduce_rows(): return lax.psum_scatter(partial, 'lat', scatter_dimension=0, tiled=True)]
    ppermute x20, waiting for transfers between devices: 27.9 us -> 58.3 us  [swap(): return lax.ppermute(value, axis, [(i, i ^ bit) for i in range(size)])]
    all_gather x0 -> x3, waiting for transfers between devices: none -> 15.4 us  [gather_rows(): return lax.all_gather(block, 'lat', axis=0, tiled=True)]
    ppermute x9 -> x0, starting transfers between devices: 12.8 us -> none  [gather_rows(): got = lax.ppermute(block, 'lat', [(i, (i + shift) % n) for i in range(n)])]
    ppermute x12, waiting for transfers between devices: 75.1 us -> 63.8 us  [swap_split(): return lax.ppermute(value, ('lyr', 'dp'), pairs)]
    dot_general x4, matrix products: 15.8 us -> 25.7 us  [transposed(): lax.dot_general(value, selected, (((0,), (0,)), ((), ())), preferred_elem...]
    dot_general x3, matrix products: 40.6 us -> 34.1 us  [reduce_pair(): lax.dot_general(resid, weight, (((1,), (1,)), ((), ())), preferred_elemen...]
  transfers between devices with their start and end apart: 44 -> 38, of which waited for: 23 -> 17; matrix products, arithmetic and copies ran while one was open for 26% -> 33% of each run, Pallas kernels for 6% -> 6%
where the time goes in v4:
time: 488 us; the launch traced here: 480 us
  waiting for transfers between devices  185 us (38%)
  matrix products  104 us (21%)
  Pallas kernels  58.5 us (12%)
  local copies, waits for them, and re-layouts  49.7 us (10%)
  other arithmetic  39 us (8%)
  starting transfers between devices  28.5 us (6%)
  between operations  15 us (3%)
    ppermute x12, waiting for transfers between devices, swap_split(): return lax.ppermute(value, ('lyr', 'dp'), pairs)  63.8 us
    ppermute x20, waiting for transfers between devices, swap(): return lax.ppermute(value, axis, [(i, i ^ bit) for i in range(size)])  58.3 us
    reduce_scatter x3, waiting for transfers between devices, reduce_rows(): return lax.psum_scatter(partial, 'lat', scatter_dimension=0, tiled=True)  46.2 us
    dot_general x3, matrix products, reduce_pair(): lax.dot_general(resid, weight, (((1,), (1,)), ((), ())), preferred_elemen...  34.1 us
    dot_general x3, matrix products, shards(): jnp.dot(lat_chunks[k], weight, preferred_element_type=jnp.float32)  33.3 us
    pallas_call x2, Pallas kernels, decoder_grad(): pl.pallas_call(functools.partial(dec_kernel, len(pieces)), grid=(tiles, w...  30.7 us
    pallas_call x1, Pallas kernels, encoder_grad(): pl.pallas_call(functools.partial(enc_kernel, len(pieces)), grid=(feats //...  27.8 us
    dot_general x4, matrix products, transposed(): lax.dot_general(value, selected, (((0,), (0,)), ((), ())), preferred_elem...  25.7 us
  transfers between devices with their start and end apart: 38, of which 17 were waited for; matrix products, arithmetic and copies ran while one was open for 33% of the time, Pallas kernels for 6%

profile of v4, /device:TPU:0, one launch (start us, length us, event | category | flops | bytes accessed | tf_op | source)
XLA Modules:
  0.0 479.5 jit_solution(10776311815552827141)
XLA Ops:
  8.4 3.0 collective-permute-start
  11.5 3.3 fusion.60
  14.8 2.3 slice.74
  18.1 11.0 %collective-permute-done = bf16[96,4096]{1,0:T(8,128)(2,1)} collective-permute-done((bf16[96,4096]{1,0:T(8,128)(2,1)S(1)}, bf16[96,4096]{1,0:T(8,128)(2,1)}, u32[]{:S(2)}, u32[]{:S(2)}) %collective-permute-start) | collective-permute-done | bytes 786464 | tf_op jit(solution)/shard_map/ppermute | solution.py:22
  29.1 2.1 fusion.61
  31.6 1.7 maximum_select_fusion
  34.5 11.9 %fusion.53 = f32[384,2048]{1,0:T(8,128)} fusion(bf16[4096,1,2048]{2,0,1:T(8,128)(2,1)} %param.8, bf16[192,4096]{1,0:T(8,128)(2,1)S(1)} %bitcast.143, bf16[192,4096]{1,0:T(8,128)(2,1)S(1)} %get-tuple-element.72), kind=kOutput, calls=%fused_computation.136 | convolution fusion | flops 6448742400 | bytes 23068672 | tf_op jit(solution)/shard_map/dot_general | solution.py:233
  46.4 2.1 constant_dynamic-slice_fusion.11
  48.4 1.7 collective-permute-start.4
  50.3 7.3 %multiply_reduce_fusion = f32[4096]{0:T(1024)S(1)} fusion(bf16[4096,2048]{1,0:T(8,128)(2,1)} %bitcast.127), kind=kLoop, calls=%fused_computation | loop fusion | flops 25161728 | bytes 16793600 | tf_op jit(solution)/shard_map/reduce_sum | solution.py:242
  60.3 1.9 collective-permute-start.2
  62.3 6.8 %collective-permute-done.4 = bf16[96,4096]{1,0:T(8,128)(2,1)} collective-permute-done((bf16[96,4096]{1,0:T(8,128)(2,1)}, bf16[96,4096]{1,0:T(8,128)(2,1)}, u32[]{:S(2)}, u32[]{:S(2)}) %collective-permute-start.4) | collective-permute-done | bytes 786464 | tf_op jit(solution)/shard_map/ppermute | solution.py:22
  69.4 1.9 constant_dynamic-slice_fusion.9
  71.3 1.7 collective-permute-start.7
  73.0 1.7 maximum_select_fusion.1
  75.8 11.9 %fusion.51 = f32[384,2048]{1,0:T(8,128)} fusion(bf16[4096,1,2048]{2,0,1:T(8,128)(2,1)} %param.8, bf16[192,4096]{1,0:T(8,128)(2,1)S(1)} %bitcast.145, bf16[192,4096]{1,0:T(8,128)(2,1)S(1)} %get-tuple-element.71), kind=kOutput, calls=%fused_computation.134 | convolution fusion | flops 6448742400 | bytes 23068672 | tf_op jit(solution)/shard_map/dot_general | solution.py:233
  87.8 9.4 %collective-permute-done.7 = bf16[64,4096]{1,0:T(8,128)(2,1)} collective-permute-done((bf16[64,4096]{1,0:T(8,128)(2,1)}, bf16[64,4096]{1,0:T(8,128)(2,1)}, u32[]{:S(2)}, u32[]{:S(2)}) %collective-permute-start.7) | collective-permute-done | bytes 524320 | tf_op jit(solution)/shard_map/ppermute | solution.py:22
  97.3 4.5 fusion.66
  104.2 9.5 %fusion.49 = f32[256,2048]{1,0:T(8,128)} fusion(bf16[4096,1,2048]{2,0,1:T(8,128)(2,1)} %param.8, bf16[128,4096]{1,0:T(8,128)(2,1)S(1)} %bitcast.153, bf16[128,4096]{1,0:T(8,128)(2,1)S(1)} %copy-done.15), kind=kOutput, calls=%fused_computation.132 | convolution fusion | flops 4299161600 | bytes 20971520 | tf_op jit(solution)/shard_map/dot_general | solution.py:233
  113.7 2.2 subtract_convert_fusion.1
  119.4 1.7 collective-permute-start.6
  122.3 17.3 %collective-permute-done.6 = bf16[192,2048]{1,0:T(8,128)(2,1)} collective-permute-done((bf16[192,2048]{1,0:T(8,128)(2,1)}, bf16[192,2048]{1,0:T(8,128)(2,1)}, u32[]{:S(2)}, u32[]{:S(2)}) %collective-permute-start.6) | collective-permute-done | bytes 786464 | tf_op jit(solution)/shard_map/ppermute | solution.py:22
  139.6 4.0 fusion.65
  143.6 11.1 %all-gather.4.cloned.1.call-done.refs_5_ = bf16[384,2048]{1,0:T(8,128)(2,1)} async-done(((bf16[96,2048]{1,0:T(8,128)(2,1)}), bf16[384,2048]{1,0:T(8,128)(2,1)}) %all-gather.4.cloned.1.call-update) | async-done | bytes 1572880 | tf_op jit(solution)/shard_map/all_gather | solution.py:41
  154.7 10.7 %convolution_add_fusion.1 = f32[384,4096]{1,0:T(8,128)S(1)} fusion(bf16[384,2048]{1,0:T(8,128)(2,1)} %all-gather.4.cloned.1.call-done.refs_5_, f32[4096]{0:T(1024)S(1)} %get-tuple-element.67, bf16[4096,1,2048]{2,0,1:T(8,128)(2,1)} %param.8), kind=kOutput, calls=%fused_computation.4 | convolution fusion | flops 6444023808 | bytes 24657920 | tf_op jit(solution)/shard_map/dot_general | solution.py:156
  165.5 2.7 copy-done.11
  168.2 1.8 dynamic-slice_bitcast_fusion.1
  170.0 46.2 %reduce-scatter.6.cloned.1.call-done = f32[96,2048]{1,0:T(8,128)} async-done(((f32[384,2048]{1,0:T(8,128)}), f32[96,2048]{1,0:T(8,128)}) %reduce-scatter.6.cloned.1.call-update) | async-done | bytes 786448 | tf_op jit(solution)/shard_map/reduce_scatter | solution.py:37
  216.2 2.2 subtract_convert_fusion
  218.5 2.3 slice.77
  220.9 1.9 dynamic-slice_bitcast_fusion.5
  222.8 4.4 pad_maximum_fusion
  230.9 11.4 %collective-permute-done.10 = bf16[128,2048]{1,0:T(8,128)(2,1)S(1)} collective-permute-done((bf16[128,2048]{1,0:T(8,128)(2,1)S(1)}, bf16[128,2048]{1,0:T(8,128)(2,1)S(1)}, u32[]{:S(2)}, u32[]{:S(2)}) %collective-permute-start.10) | collective-permute-done | bytes 524320 | tf_op jit(solution)/shard_map/ppermute | solution.py:22
  243.1 5.5 %convolution_convert_fusion.1.refs_2_ = bf16[4096,384]{1,0:T(8,128)(2,1)} fusion(bf16[384,4096]{1,0:T(8,128)(2,1)} %get-tuple-element.47), kind=kOutput, calls=%fused_computation.6 | convolution fusion | flops 1209679872 | bytes 6291456 | tf_op jit(solution)/shard_map/dot_general | solution.py:149
  248.6 2.8 fusion.64
  251.4 4.3 all-gather.6.cloned.1.call-done.refs_6_
  255.7 10.7 %convolution_add_fusion = f32[384,4096]{1,0:T(8,128)S(1)} fusion(bf16[384,2048]{1,0:T(8,128)(2,1)} %all-gather.6.cloned.1.call-done.refs_6_, f32[4096]{0:T(1024)S(1)} %get-tuple-element.67, bf16[4096,1,2048]{2,0,1:T(8,128)(2,1)} %param.8), kind=kOutput, calls=%fused_computation.3 | convolution fusion | flops 6444023808 | bytes 24657920 | tf_op jit(solution)/shard_map/dot_general | solution.py:156
  266.8 3.2 bitcast_add_fusion.1
  273.6 3.6 convolution_convert_fusion.refs_3_
  277.2 14.2 %fusion.6.refs_0_ = bf16[2048,1024]{1,0:T(8,128)(2,1)} fusion(bf16[256,2048]{1,0:T(8,128)(2,1)S(1)} %get-tuple-element.85, bf16[384,2048]{1,0:T(8,128)(2,1)S(1)} %copy-done.19, bf16[384,2048]{1,0:T(8,128)(2,1)S(1)} %copy-done.18, s32[1024]{0:T(1024)S(1)} %pad_add_fusion), kind=kOutput, calls=%fused_computation.16 | convolution fusion | flops 4310695936 | bytes 8392704 | tf_op jit(solution)/shard_map/dot_general | solution.py:149
  291.5 1.5 collective-permute-start.13
  293.1 2.1 bitcast_add_fusion
  295.2 8.4 %collective-permute-done.13 = f32[48,4096]{1,0:T(8,128)S(1)} collective-permute-done((f32[48,4096]{1,0:T(8,128)S(1)}, f32[48,4096]{1,0:T(8,128)S(1)}, u32[]{:S(2)}, u32[]{:S(2)}) %collective-permute-start.13) | collective-permute-done | bytes 786464 | tf_op jit(solution)/shard_map/ppermute | solution.py:33
  303.6 1.9 constant_dynamic-update-slice_fusion.4
  305.5 2.0 subtract_convert_fusion.2
  309.4 1.5 collective-permute-start.14
  312.2 2.0 copy.12.refs_0_
  315.6 2.3 convolution_convert_fusion.2.refs_4_
  319.0 2.4 collective-permute-start.15
  322.2 21.1 %collective-permute-done.15 = bf16[2,48,4096]{2,1,0:T(8,128)(2,1)} collective-permute-done((bf16[2,48,4096]{2,1,0:T(8,128)(2,1)}, bf16[2,48,4096]{2,1,0:T(8,128)(2,1)}, u32[]{:S(2)}, u32[]{:S(2)}) %collective-permute-start.15) | collective-permute-done | bytes 786464 | tf_op jit(solution)/shard_map/ppermute | solution.py:33
  343.3 2.1 constant_dynamic-update-slice_fusion.2
  348.5 12.6 %broadcast_add_fusion = f32[256,4096]{1,0:T(8,128)} fusion(f32[4096]{0:T(1024)S(1)} %get-tuple-element.67, bf16[256,2048]{1,0:T(8,128)(2,1)} %all-gather.8.cloned.1.call-done.refs_7_, bf16[4096,1,2048]{2,0,1:T(8,128)(2,1)} %param.8), kind=kOutput, calls=%fused_computation.29 | convolution fusion | flops 4296015872 | bytes 22036480 | tf_op jit(solution)/shard_map/dot_general | solution.py:156
  361.2 1.9 dynamic-slice_bitcast_fusion.2
  364.2 2.1 constant_dynamic-update-slice_fusion.1
  366.3 1.8 constant_dynamic-update-slice_fusion.9
  368.7 2.1 constant_dynamic-update-slice_fusion
  370.8 5.1 %collective-permute-done.21 = bf16[48,4096]{1,0:T(8,128)(2,1)S(1)} collective-permute-done((bf16[48,4096]{1,0:T(8,128)(2,1)S(1)}, bf16[48,4096]{1,0:T(8,128)(2,1)S(1)}, u32[]{:S(2)}, u32[]{:S(2)}) %collective-permute-start.21) | collective-permute-done | bytes 393248 | tf_op jit(solution)/shard_map/ppermute | solution.py:33
  378.7 9.4 %collective-permute-done.22 = bf16[2,48,4096]{2,1,0:T(8,128)(2,1)S(1)} collective-permute-done((bf16[2,48,4096]{2,1,0:T(8,128)(2,1)S(1)}, bf16[2,48,4096]{2,1,0:T(8,128)(2,1)S(1)}, u32[]{:S(2)}, u32[]{:S(2)}) %collective-permute-start.22) | collective-permute-done | bytes 786464 | tf_op jit(solution)/shard_map/ppermute | solution.py:33
  388.2 11.1 %collective-permute-done.26 = f32[2,32,4096]{2,1,0:T(8,128)S(1)} collective-permute-done((f32[2,32,4096]{2,1,0:T(8,128)S(1)}, f32[2,32,4096]{2,1,0:T(8,128)S(1)}, u32[]{:S(2)}, u32[]{:S(2)}) %collective-permute-start.26) | collective-permute-done | bytes 1048608 | tf_op jit(solution)/shard_map/ppermute | solution.py:33
  400.0 15.3 %shard_map.77.refs_8_ = f32[4096,16,128]{2,1,0:T(8,128)} custom-call(f32[4096,1]{1,0:T(8,128)S(1)} %copy-done.2, bf16[4096,2048]{1,0:T(8,128)(2,1)} %bitcast.128, bf16[4096,384]{1,0:T(8,128)(2,1)} %convolution_convert_fusion.1.refs_2_, bf16[4096,384]{1,0:T(8,128)(2,1)} %convolution_convert_fusion.refs_3_, ...), custom_call_target="tpu_custom_call" | custom-call | flops 8589934592 | bytes 33554432 | tf_op jit(solution)/shard_map/pallas_call | solution.py:99
  417.9 15.4 %shard_map.78 = f32[4096,16,128]{2,1,0:T(8,128)} custom-call(f32[4096,1]{1,0:T(8,128)S(1)} %copy-done.2, bf16[4096,2048]{1,0:T(8,128)(2,1)} %bitcast.129, bf16[4096,384]{1,0:T(8,128)(2,1)} %convolution_convert_fusion.1.refs_2_, bf16[4096,384]{1,0:T(8,128)(2,1)} %convolution_convert_fusion.refs_3_, ...), custom_call_target="tpu_custom_call", output_to_operand_aliasing={{}: (8, {})} | custom-call | flops 8589934592 | bytes 33554432 | tf_op jit(solution)/shard_map/pallas_call | solution.py:99
  434.0 8.6 %collective-permute-done.29 = bf16[2,32,4096]{2,1,0:T(8,128)(2,1)S(1)} collective-permute-done((bf16[2,32,4096]{2,1,0:T(8,128)(2,1)S(1)}, bf16[2,32,4096]{2,1,0:T(8,128)(2,1)S(1)}, u32[]{:S(2)}, u32[]{:S(2)}) %collective-permute-start.29) | collective-permute-done | bytes 524320 | tf_op jit(solution)/shard_map/ppermute | solution.py:33
  442.7 1.8 collective-permute-done.31
  444.6 27.8 %shard_map.76 = (f32[2048,32,128]{2,1,0:T(8,128)}, f32[1,4096]{1,0:T(1,128)}) custom-call(bf16[2048,1024]{1,0:T(8,128)(2,1)} %fusion.6.refs_0_, bf16[384,4096]{1,0:T(8,128)(2,1)} %bitcast.34.refs_1_, bf16[384,4096]{1,0:T(8,128)(2,1)S(1)} %bitcast.125, bf16[256,4096]{1,0:T(8,128)(2,1)S(1)} %bitcast.126), custom_call_target="tpu_custom_call" | custom-call | flops 17179869184 | bytes 46137344 | tf_op jit(solution)/shard_map/pallas_call | solution.py:121
  (165 shorter events, 42.1 us)
Async XLA Ops:
  7.2 10.0 %copy-start = (f32[1,4096]{1,0:T(1,128)S(1)}, f32[1,4096]{1,0:T(1,128)}, u32[]{:S(2)}) copy-start(f32[1,4096]{1,0:T(1,128)} %param.9) | copy-start | bytes 49156
  7.2 106.5 %reduce-scatter.4.cloned.1.call-start = ((), (), s32[]{:S(2)}) async-start(), calls=%async_computation.3 | async-start | bytes 3932160 | tf_op jit(solution)/shard_map/reduce_scatter | solution.py:37
  8.4 20.7 %collective-permute-start = (bf16[96,4096]{1,0:T(8,128)(2,1)S(1)}, bf16[96,4096]{1,0:T(8,128)(2,1)}, u32[]{:S(2)}, u32[]{:S(2)}) collective-permute-start(bf16[96,4096]{1,0:T(8,128)(2,1)S(1)} %constant_dynamic-slice_fusion.14), channel_id=1, source_target_pairs={{0,1},{1,0},{2,3},{3,2},{4,5},{5,4},{6,7},{7,6},{8,9},{9,8},{10,11... | collective-permute-start | bytes 2359304 | tf_op jit(solution)/shard_map/ppermute | solution.py:22
  29.1 2.5 collective-permute-start.1
  33.3 1.2 copy-start.9
  48.4 20.7 %collective-permute-start.4 = (bf16[96,4096]{1,0:T(8,128)(2,1)}, bf16[96,4096]{1,0:T(8,128)(2,1)}, u32[]{:S(2)}, u32[]{:S(2)}) collective-permute-start(bf16[96,4096]{1,0:T(8,128)(2,1)} %constant_dynamic-slice_fusion.11), channel_id=1, source_target_pairs={{0,1},{1,0},{2,3},{3,2},{4,5},{5,4},{6,7},{7,6},{8,9},{9,8},{10,11... | collective-permute-start | bytes 2359304 | tf_op jit(solution)/shard_map/ppermute | solution.py:22
  50.2 104.5 %all-gather.4.cloned.1.call-start = ((), (), s32[]{:S(2)}) async-start(), calls=%async_computation.5 | async-start | bytes 1966080 | tf_op jit(solution)/shard_map/all_gather | solution.py:41
  57.6 4.6 copy-start.23
  57.6 11.8 %collective-permute-start.9 = (f32[4096]{0:T(1024)S(1)}, f32[4096]{0:T(1024)S(1)}, u32[]{:S(2)}, u32[]{:S(2)}) collective-permute-start(f32[4096]{0:T(1024)S(1)} %multiply_reduce_fusion), channel_id=1, source_target_pairs={{0,1},{1,0},{2,3},{3,2},{4,5},{5,4},{6,7},{7,6},{8,9},{9,8},{10,11... | collective-permute-start | bytes 49160 | tf_op jit(solution)/shard_map/ppermute | solution.py:22
  60.3 37.0 %collective-permute-start.2 = (bf16[192,2048]{1,0:T(8,128)(2,1)}, bf16[192,2048]{1,0:T(8,128)(2,1)}, u32[]{:S(2)}, u32[]{:S(2)}) collective-permute-start(bf16[192,2048]{1,0:T(8,128)(2,1)} %constant_dynamic-slice_fusion.13), channel_id=1, source_target_pairs={{0,1},{1,0},{2,3},{3,2},{4,5},{5,4},{6,7},{7,6},{8,9},{9,8},{10,11... | collective-permute-start | bytes 2359304 | tf_op jit(solution)/shard_map/ppermute | solution.py:22
  62.2 35.0 %collective-permute-start.3 = (bf16[512,16]{0,1:T(8,128)(2,1)S(1)}, bf16[512,16]{0,1:T(8,128)(2,1)S(1)}, u32[]{:S(2)}, u32[]{:S(2)}) collective-permute-start(bf16[512,16]{0,1:T(8,128)(2,1)S(1)} %constant_dynamic-slice_fusion.12), channel_id=1, source_target_pairs={{0,1},{1,0},{2,3},{3,2},{4,5},{5,4},{6,7},{7,6},{8,9},{9,8},{10,11... | collective-permute-start | bytes 49160 | tf_op jit(solution)/shard_map/ppermute | solution.py:22
  69.1 3.9 collective-permute-start.5
  71.3 25.8 %collective-permute-start.7 = (bf16[64,4096]{1,0:T(8,128)(2,1)}, bf16[64,4096]{1,0:T(8,128)(2,1)}, u32[]{:S(2)}, u32[]{:S(2)}) collective-permute-start(bf16[64,4096]{1,0:T(8,128)(2,1)} %constant_dynamic-slice_fusion.9), channel_id=1, source_target_pairs={{0,1},{1,0},{2,3},{3,2},{4,5},{5,4},{6,7},{7,6},{8,9},{9,8},{10,11... | collective-permute-start | bytes 1572872 | tf_op jit(solution)/shard_map/ppermute | solution.py:22
  74.7 1.1 copy-start.10
  97.1 4.7 collective-permute-start.8
  97.1 125.7 %copy-start.24 = (bf16[512,16]{0,1:T(8,128)(2,1)}, bf16[512,16]{0,1:T(8,128)(2,1)S(1)}, u32[]{:S(2)}) copy-start(bf16[512,16]{0,1:T(8,128)(2,1)S(1)} %collective-permute-done.3) | copy-start | bytes 49156
  97.3 6.9 %copy-start.15 = (bf16[128,4096]{1,0:T(8,128)(2,1)S(1)}, bf16[128,4096]{1,0:T(8,128)(2,1)}, u32[]{:S(2)}) copy-start(bf16[128,4096]{1,0:T(8,128)(2,1)} %slice.74) | copy-start | bytes 3145732
  103.2 1.0 copy-start.13
  115.9 100.3 %reduce-scatter.6.cloned.1.call-start = ((), (), s32[]{:S(2)}) async-start(), calls=%async_computation.4 | async-start | bytes 3932160 | tf_op jit(solution)/shard_map/reduce_scatter | solution.py:37
  116.7 139.0 %all-gather.6.cloned.1.call-start = ((), (), s32[]{:S(2)}) async-start(), calls=%async_computation.6 | async-start | bytes 1966080 | tf_op jit(solution)/shard_map/all_gather | solution.py:41
  119.4 20.2 %collective-permute-start.6 = (bf16[192,2048]{1,0:T(8,128)(2,1)}, bf16[192,2048]{1,0:T(8,128)(2,1)}, u32[]{:S(2)}, u32[]{:S(2)}) collective-permute-start(bf16[192,2048]{1,0:T(8,128)(2,1)} %constant_dynamic-slice_fusion.10), channel_id=1, source_target_pairs={{0,1},{1,0},{2,3},{3,2},{4,5},{5,4},{6,7},{7,6},{8,9},{9,8},{10,11... | collective-permute-start | bytes 2359304 | tf_op jit(solution)/shard_map/ppermute | solution.py:22
  165.5 2.7 copy-start.11
  218.4 87.1 %reduce-scatter.8.cloned.1.call-start = ((), (), s32[]{:S(2)}) async-start(), calls=%async_computation.7 | async-start | bytes 2621440 | tf_op jit(solution)/shard_map/reduce_scatter | solution.py:37
  227.2 3.0 copy-start.14
  227.2 3.0 copy-start.16
  228.7 13.6 %collective-permute-start.10 = (bf16[128,2048]{1,0:T(8,128)(2,1)S(1)}, bf16[128,2048]{1,0:T(8,128)(2,1)S(1)}, u32[]{:S(2)}, u32[]{:S(2)}) collective-permute-start(bf16[128,2048]{1,0:T(8,128)(2,1)S(1)} %constant_dynamic-slice_fusion.7), channel_id=1, source_target_pairs={{0,1},{1,0},{2,3},{3,2},{4,5},{5,4},{6,7},{7,6},{8,9},{9,8},{10,11... | collective-permute-start | bytes 1572872 | tf_op jit(solution)/shard_map/ppermute | solution.py:22
  230.4 77.1 %copy-start.6 = (bf16[256,4096]{1,0:T(8,128)(2,1)}, bf16[256,4096]{1,0:T(8,128)(2,1)S(1)}, u32[]{:S(2)}) copy-start(bf16[256,4096]{1,0:T(8,128)(2,1)S(1)} %pad_maximum_fusion.2) | copy-start | bytes 6291460
  230.8 117.7 %all-gather.8.cloned.1.call-start = ((), (), s32[]{:S(2)}) async-start(), calls=%async_computation.8 | async-start | bytes 1310720 | tf_op jit(solution)/shard_map/all_gather | solution.py:41
  230.8 36.0 %collective-permute-start.11 = (f32[2,2,48,4096]{3,2,1,0:T(8,128)}, f32[2,2,48,4096]{3,2,1,0:T(8,128)}, u32[]{:S(2)}, u32[]{:S(2)}) collective-permute-start(f32[2,2,48,4096]{3,2,1,0:T(8,128)} %dynamic-slice_bitcast_fusion.1), channel_id=1, source_target_pairs={{0,2},{2,0},{4,6},{6,4},{1,3},{3,1},{5,7},{7,5},{8,10},{10,8},{12,... | collective-permute-start | bytes 9437192 | tf_op jit(solution)/shard_map/ppermute | solution.py:22
  242.3 0.8 copy-start.22
  243.1 5.5 %copy-start.17 = (bf16[128,2048]{1,0:T(8,128)(2,1)S(1)}, bf16[128,2048]{1,0:T(8,128)(2,1)}, u32[]{:S(2)}) copy-start(bf16[128,2048]{1,0:T(8,128)(2,1)} %dynamic-slice_bitcast_fusion.5) | copy-start | bytes 1572868
  243.1 5.5 %slice-start = ((bf16[512,16]{0,1:T(8,128)(2,1)}), bf16[128,16]{0,1:T(8,128)(2,1)S(1)}, s32[]{:S(2)}) async-start(bf16[512,16]{0,1:T(8,128)(2,1)} %copy-done.24), calls=%async_computation.9 | async-start | bytes 8192 | tf_op jit(solution)/shard_map/slice | solution.py:252
  266.7 26.3 %collective-permute-start.18 = (f32[2,2,48,4096]{3,2,1,0:T(8,128)S(1)}, f32[2,2,48,4096]{3,2,1,0:T(8,128)S(1)}, u32[]{:S(2)}, u32[]{:S(2)}) collective-permute-start(f32[2,2,48,4096]{3,2,1,0:T(8,128)S(1)} %dynamic-slice_bitcast_fusion), channel_id=1, source_target_pairs={{0,2},{2,0},{4,6},{6,4},{1,3},{3,1},{5,7},{7,5},{8,10},{10,8},{12,... | collective-permute-start | bytes 9437192 | tf_op jit(solution)/shard_map/ppermute | solution.py:22
  270.1 1.9 copy-start.8
  270.2 2.8 copy-start.7
  270.3 21.1 %collective-permute-start.12 = (f32[2,48,4096]{2,1,0:T(8,128)S(1)}, f32[2,48,4096]{2,1,0:T(8,128)S(1)}, u32[]{:S(2)}, u32[]{:S(2)}) collective-permute-start(f32[2,48,4096]{2,1,0:T(8,128)S(1)} %pad_maximum_fusion.3), channel_id=1, source_target_pairs={{0,4},{1,5},{2,3},{3,2},{4,0},{5,1},{6,7},{7,6},{8,12},{9,13},{10,... | collective-permute-start | bytes 4718600 | tf_op jit(solution)/shard_map/ppermute | solution.py:33
  273.6 3.6 copy-start.18
  273.6 3.6 copy-start.19
  291.5 12.1 %collective-permute-start.13 = (f32[48,4096]{1,0:T(8,128)S(1)}, f32[48,4096]{1,0:T(8,128)S(1)}, u32[]{:S(2)}, u32[]{:S(2)}) collective-permute-start(f32[48,4096]{1,0:T(8,128)S(1)} %fusion.15), channel_id=1, source_target_pairs={{0,1},{1,0},{2,6},{3,7},{4,5},{5,4},{6,2},{7,3},{8,9},{9,8},{10,14... | collective-permute-start | bytes 2359304 | tf_op jit(solution)/shard_map/ppermute | solution.py:33
  309.4 8.6 %collective-permute-start.14 = (bf16[48,4096]{1,0:T(8,128)(2,1)S(1)}, bf16[48,4096]{1,0:T(8,128)(2,1)S(1)}, u32[]{:S(2)}, u32[]{:S(2)}) collective-permute-start(bf16[48,4096]{1,0:T(8,128)(2,1)S(1)} %get-tuple-element.65), channel_id=1, source_target_pairs={{0,1},{1,0},{2,6},{3,7},{4,5},{5,4},{6,2},{7,3},{8,9},{9,8},{10,14... | collective-permute-start | bytes 1179656 | tf_op jit(solution)/shard_map/ppermute | solution.py:33
  314.1 31.3 %collective-permute-start.19 = (f32[2,48,4096]{2,1,0:T(8,128)}, f32[2,48,4096]{2,1,0:T(8,128)S(1)}, u32[]{:S(2)}, u32[]{:S(2)}) collective-permute-start(f32[2,48,4096]{2,1,0:T(8,128)} %pad_maximum_fusion.4), channel_id=1, source_target_pairs={{0,4},{1,5},{2,3},{3,2},{4,0},{5,1},{6,7},{7,6},{8,12},{9,13},{10,... | collective-permute-start | bytes 4718600 | tf_op jit(solution)/shard_map/ppermute | solution.py:33
  319.0 24.3 %collective-permute-start.15 = (bf16[2,48,4096]{2,1,0:T(8,128)(2,1)}, bf16[2,48,4096]{2,1,0:T(8,128)(2,1)}, u32[]{:S(2)}, u32[]{:S(2)}) collective-permute-start(bf16[2,48,4096]{2,1,0:T(8,128)(2,1)} %pad_maximum_fusion.6), channel_id=1, source_target_pairs={{0,4},{1,5},{2,3},{3,2},{4,0},{5,1},{6,7},{7,6},{8,12},{9,13},{10,... | collective-permute-start | bytes 2359304 | tf_op jit(solution)/shard_map/ppermute | solution.py:33
  321.4 42.8 %collective-permute-start.16 = (bf16[2,48,4096]{2,1,0:T(8,128)(2,1)}, bf16[2,48,4096]{2,1,0:T(8,128)(2,1)}, u32[]{:S(2)}, u32[]{:S(2)}) collective-permute-start(bf16[2,48,4096]{2,1,0:T(8,128)(2,1)} %pad_maximum_fusion.6), channel_id=1, source_target_pairs={{0,2},{2,0},{4,6},{6,4},{1,3},{3,1},{5,7},{7,5},{8,10},{10,8},{12,... | collective-permute-start | bytes 2359304 | tf_op jit(solution)/shard_map/ppermute | solution.py:22
  343.3 25.4 %collective-permute-start.17 = (bf16[2,48,4096]{2,1,0:T(8,128)(2,1)}, bf16[2,48,4096]{2,1,0:T(8,128)(2,1)}, u32[]{:S(2)}, u32[]{:S(2)}) collective-permute-start(bf16[2,48,4096]{2,1,0:T(8,128)(2,1)} %collective-permute-done.15), channel_id=1, source_target_pairs={{0,2},{2,0},{4,6},{6,4},{1,3},{3,1},{5,7},{7,5},{8,10},{10,8},{12,... | collective-permute-start | bytes 2359304 | tf_op jit(solution)/shard_map/ppermute | solution.py:22
  345.4 1.2 copy-start.20
  347.8 18.5 %collective-permute-start.20 = (f32[48,4096]{1,0:T(8,128)S(1)}, f32[48,4096]{1,0:T(8,128)}, u32[]{:S(2)}, u32[]{:S(2)}) collective-permute-start(f32[48,4096]{1,0:T(8,128)S(1)} %fusion.10), channel_id=1, source_target_pairs={{0,1},{1,0},{2,6},{3,7},{4,5},{5,4},{6,2},{7,3},{8,9},{9,8},{10,14... | collective-permute-start | bytes 2359304 | tf_op jit(solution)/shard_map/ppermute | solution.py:33
  361.2 5.1 %copy-start.21 = (f32[2,48,4096]{2,1,0:T(8,128)S(1)}, f32[2,48,4096]{2,1,0:T(8,128)}, u32[]{:S(2)}) copy-start(f32[2,48,4096]{2,1,0:T(8,128)} %copy-done.20) | copy-start | bytes 4718596
  363.1 13.5 %collective-permute-start.25 = (f32[2,2,32,4096]{3,2,1,0:T(8,128)S(1)}, f32[2,2,32,4096]{3,2,1,0:T(8,128)S(1)}, u32[]{:S(2)}, u32[]{:S(2)}) collective-permute-start(f32[2,2,32,4096]{3,2,1,0:T(8,128)S(1)} %dynamic-slice_bitcast_fusion.2), channel_id=1, source_target_pairs={{0,2},{2,0},{4,6},{6,4},{1,3},{3,1},{5,7},{7,5},{8,10},{10,8},{12,... | collective-permute-start | bytes 6291464 | tf_op jit(solution)/shard_map/ppermute | solution.py:22
  366.3 10.4 %copy-start.12 = (f32[256,4096]{1,0:T(8,128)S(1)}, f32[256,4096]{1,0:T(8,128)}, u32[]{:S(2)}) copy-start(f32[256,4096]{1,0:T(8,128)} %broadcast_add_fusion) | copy-start | bytes 12582916
  368.1 7.8 %collective-permute-start.21 = (bf16[48,4096]{1,0:T(8,128)(2,1)S(1)}, bf16[48,4096]{1,0:T(8,128)(2,1)S(1)}, u32[]{:S(2)}, u32[]{:S(2)}) collective-permute-start(bf16[48,4096]{1,0:T(8,128)(2,1)S(1)} %get-tuple-element.63), channel_id=1, source_target_pairs={{0,1},{1,0},{2,6},{3,7},{4,5},{5,4},{6,2},{7,3},{8,9},{9,8},{10,14... | collective-permute-start | bytes 1179656 | tf_op jit(solution)/shard_map/ppermute | solution.py:33
  376.0 12.1 %collective-permute-start.22 = (bf16[2,48,4096]{2,1,0:T(8,128)(2,1)S(1)}, bf16[2,48,4096]{2,1,0:T(8,128)(2,1)S(1)}, u32[]{:S(2)}, u32[]{:S(2)}) collective-permute-start(bf16[2,48,4096]{2,1,0:T(8,128)(2,1)S(1)} %pad_maximum_fusion.7), channel_id=1, source_target_pairs={{0,4},{1,5},{2,3},{3,2},{4,0},{5,1},{6,7},{7,6},{8,12},{9,13},{10,... | collective-permute-start | bytes 2359304 | tf_op jit(solution)/shard_map/ppermute | solution.py:33
  376.6 11.5 %collective-permute-start.23 = (bf16[2,48,4096]{2,1,0:T(8,128)(2,1)S(1)}, bf16[2,48,4096]{2,1,0:T(8,128)(2,1)S(1)}, u32[]{:S(2)}, u32[]{:S(2)}) collective-permute-start(bf16[2,48,4096]{2,1,0:T(8,128)(2,1)S(1)} %pad_maximum_fusion.7), channel_id=1, source_target_pairs={{0,2},{2,0},{4,6},{6,4},{1,3},{3,1},{5,7},{7,5},{8,10},{10,8},{12,... | collective-permute-start | bytes 2359304 | tf_op jit(solution)/shard_map/ppermute | solution.py:22
  377.0 23.0 %copy-start.5 = (bf16[256,2048]{1,0:T(8,128)(2,1)S(1)}, bf16[256,2048]{1,0:T(8,128)(2,1)}, u32[]{:S(2)}) copy-start(bf16[256,2048]{1,0:T(8,128)(2,1)} %all-gather.8.cloned.1.call-done.refs_7_) | copy-start | bytes 3145732
  377.1 22.9 %copy-start.2 = (f32[4096,1]{1,0:T(8,128)S(1)}, f32[4096,1]{1,0:T(8,128)}, u32[]{:S(2)}) copy-start(f32[4096,1]{1,0:T(8,128)} %copy.12.refs_0_) | copy-start | bytes 49156
  377.1 22.9 %copy-start.3 = (bf16[384,2048]{1,0:T(8,128)(2,1)S(1)}, bf16[384,2048]{1,0:T(8,128)(2,1)}, u32[]{:S(2)}) copy-start(bf16[384,2048]{1,0:T(8,128)(2,1)} %all-gather.4.cloned.1.call-done.refs_5_) | copy-start | bytes 4718596
  377.1 22.9 %copy-start.4 = (bf16[384,2048]{1,0:T(8,128)(2,1)S(1)}, bf16[384,2048]{1,0:T(8,128)(2,1)}, u32[]{:S(2)}) copy-start(bf16[384,2048]{1,0:T(8,128)(2,1)} %all-gather.6.cloned.1.call-done.refs_6_) | copy-start | bytes 4718596
  377.1 22.2 %collective-permute-start.26 = (f32[2,32,4096]{2,1,0:T(8,128)S(1)}, f32[2,32,4096]{2,1,0:T(8,128)S(1)}, u32[]{:S(2)}, u32[]{:S(2)}) collective-permute-start(f32[2,32,4096]{2,1,0:T(8,128)S(1)} %pad_maximum_fusion.5), channel_id=1, source_target_pairs={{0,4},{1,5},{2,3},{3,2},{4,0},{5,1},{6,7},{7,6},{8,12},{9,13},{10,... | collective-permute-start | bytes 3145736 | tf_op jit(solution)/shard_map/ppermute | solution.py:33
  388.0 27.2 %collective-permute-start.24 = (bf16[2,48,4096]{2,1,0:T(8,128)(2,1)S(1)}, bf16[2,48,4096]{2,1,0:T(8,128)(2,1)S(1)}, u32[]{:S(2)}, u32[]{:S(2)}) collective-permute-start(bf16[2,48,4096]{2,1,0:T(8,128)(2,1)S(1)} %collective-permute-done.22), channel_id=1, source_target_pairs={{0,2},{2,0},{4,6},{6,4},{1,3},{3,1},{5,7},{7,5},{8,10},{10,8},{12,... | collective-permute-start | bytes 2359304 | tf_op jit(solution)/shard_map/ppermute | solution.py:22
  399.3 16.0 %collective-permute-start.27 = (f32[32,4096]{1,0:T(8,128)S(1)}, f32[32,4096]{1,0:T(8,128)S(1)}, u32[]{:S(2)}, u32[]{:S(2)}) collective-permute-start(f32[32,4096]{1,0:T(8,128)S(1)} %fusion.18), channel_id=1, source_target_pairs={{0,1},{1,0},{2,6},{3,7},{4,5},{5,4},{6,2},{7,3},{8,9},{9,8},{10,14... | collective-permute-start | bytes 1572872 | tf_op jit(solution)/shard_map/ppermute | solution.py:33
  416.4 17.0 %collective-permute-start.28 = (bf16[32,4096]{1,0:T(8,128)(2,1)S(1)}, bf16[32,4096]{1,0:T(8,128)(2,1)S(1)}, u32[]{:S(2)}, u32[]{:S(2)}) collective-permute-start(bf16[32,4096]{1,0:T(8,128)(2,1)S(1)} %get-tuple-element.60), channel_id=1, source_target_pairs={{0,1},{1,0},{2,6},{3,7},{4,5},{5,4},{6,2},{7,3},{8,9},{9,8},{10,14... | collective-permute-start | bytes 786440 | tf_op jit(solution)/shard_map/ppermute | solution.py:33
  433.4 9.2 %collective-permute-start.29 = (bf16[2,32,4096]{2,1,0:T(8,128)(2,1)S(1)}, bf16[2,32,4096]{2,1,0:T(8,128)(2,1)S(1)}, u32[]{:S(2)}, u32[]{:S(2)}) collective-permute-start(bf16[2,32,4096]{2,1,0:T(8,128)(2,1)S(1)} %pad_maximum_fusion.8), channel_id=1, source_target_pairs={{0,4},{1,5},{2,3},{3,2},{4,0},{5,1},{6,7},{7,6},{8,12},{9,13},{10,... | collective-permute-start | bytes 1572872 | tf_op jit(solution)/shard_map/ppermute | solution.py:33
  434.0 8.7 %collective-permute-start.30 = (bf16[2,32,4096]{2,1,0:T(8,128)(2,1)S(1)}, bf16[2,32,4096]{2,1,0:T(8,128)(2,1)S(1)}, u32[]{:S(2)}, u32[]{:S(2)}) collective-permute-start(bf16[2,32,4096]{2,1,0:T(8,128)(2,1)S(1)} %pad_maximum_fusion.8), channel_id=1, source_target_pairs={{0,2},{2,0},{4,6},{6,4},{1,3},{3,1},{5,7},{7,5},{8,10},{10,8},{12,... | collective-permute-start | bytes 1572872 | tf_op jit(solution)/shard_map/ppermute | solution.py:22
  442.6 1.9 collective-permute-start.31
  444.6 27.9 %copy-start.1 = (f32[1,4096]{1,0:T(1,128)S(1)}, f32[1,4096]{1,0:T(1,128)}, u32[]{:S(2)}) copy-start(f32[1,4096]{1,0:T(1,128)} %param.9) | copy-start | bytes 49156
Sparse Core Ops, SparseCore 0:
  50.3 60.5 reduce-scatter.3
  116.1 38.6 all-gather.3
  157.0 59.1 reduce-scatter.5
  218.6 37.0 all-gather.5
  257.8 42.7 reduce-scatter.7
  307.6 26.7 all-gather.7
